TPU v7x, 32 devices: a whole 2x2x4 slice. The times are simulated.
32 devices in a mesh: groups: 2 (over x), expert: 16 (over z, y, core).
Axes of the slice: x: 2, y: 2, z: 4, core: 2. Of those that a mesh axis runs over, the one named last changes fastest.
Arguments:
- tokens: bfloat16 [8192, 1024], P(('groups', 'expert')), parts along dimension 0, may hold values from -6 to 6
- expert_ids: int32 [8192, 2], P(('groups', 'expert')), parts along dimension 0, may hold values from 0 to 15, as said below
- gate_weights: float32 [8192, 2], P(('groups', 'expert')), parts along dimension 0, may hold values from 0.2 to 1
- out_grad: bfloat16 [8192, 1024], P(('groups', 'expert')), parts along dimension 0, may hold values from -6 to 6
- w_in: bfloat16 [16, 1024, 2048], P('expert'), may hold values from -0.1875 to 0.1875
- w_out: bfloat16 [16, 2048, 1024], P('expert'), may hold values from -0.125 to 0.125
Outputs:
- moe_out: bfloat16 [8192, 1024], P(('groups', 'expert')), parts along dimension 0
- token_grad: bfloat16 [8192, 1024], P(('groups', 'expert')), parts along dimension 0
- w_in_grad: bfloat16 [32, 1024, 2048], P(('groups', 'expert')), parts along dimension 0
- w_out_grad: bfloat16 [32, 2048, 1024], P(('groups', 'expert')), parts along dimension 0
There are 2 independent parts, one for each index of `groups`. A program takes and returns all parts, laid end to end along the dimension named above; an argument that names none is the same for every part. Nothing has to cross between parts.
Inputs may be any that keep to these rules, and one draw needn't show every extreme that they name: `expert_ids`: each token names two different experts. Among the 256 tokens of one device, one expert, the same for all devices of a part, is named by exactly 96 tokens, and no expert by more than 96.
All inputs are finite; a program needn't handle non-finite values.
Results may differ from a plain program's by a relative error of at most 0.0065.
Values may be sent and summed in bfloat16 or wider, within the bound.
No kernel may reach another device: no remote copies, remote signals or barrier semaphores. Data moves between devices by JAX's collectives and lax.ppermute only.
A program may use at most 128 MiB of HBM per device.

v0:
```python
import math

import jax
import jax.numpy as jnp
from jax import lax
from jax.sharding import PartitionSpec as P

INV_ROOT_TWO = 0.7071067811865476
INV_ROOT_TAU = 0.3989422804014327


def gelu_parts(pre_act):
    normal_cdf = 0.5 * (1.0 + lax.erf(pre_act * INV_ROOT_TWO))
    normal_pdf = jnp.exp(-0.5 * pre_act * pre_act) * INV_ROOT_TAU
    return (pre_act * normal_cdf, normal_cdf + pre_act * normal_pdf)


def expert_pass(x_block, grad_block, weight_in, weight_out):
    pre_act = jnp.dot(x_block, weight_in, preferred_element_type=jnp.float32)
    activation, gelu_slope = gelu_parts(pre_act)
    activation = activation.astype(jnp.bfloat16)
    expert_out = jnp.dot(activation, weight_out, preferred_element_type=jnp.float32).astype(
        jnp.bfloat16
    )
    act_grad = lax.dot_general(
        grad_block, weight_out, (((1,), (1,)), ((), ())), preferred_element_type=jnp.float32
    )
    pre_grad = (act_grad * gelu_slope).astype(jnp.bfloat16)
    row_grad = lax.dot_general(
        pre_grad, weight_in, (((1,), (1,)), ((), ())), preferred_element_type=jnp.float32
    ).astype(jnp.bfloat16)
    grad_out = lax.dot_general(
        activation, grad_block, (((0,), (0,)), ((), ())), preferred_element_type=jnp.float32
    )
    grad_in = lax.dot_general(
        x_block, pre_grad, (((0,), (0,)), ((), ())), preferred_element_type=jnp.float32
    )
    return (expert_out, row_grad, grad_in, grad_out)


def slot_ranks(expert_flat, expert_count):
    one_hot = (expert_flat[:, None] == jnp.arange(expert_count, dtype=jnp.int32)[None, :]).astype(
        jnp.int32
    )
    before = jnp.cumsum(one_hot, axis=0) - one_hot
    return jnp.sum(before * one_hot, axis=1)


def serve_rows(slot_rows, slot_grads, counts, weight_in, weight_out):
    sources, slot_cap, feature_dim = slot_rows.shape
    slot_total = sources * slot_cap
    hidden_dim = weight_in.shape[1]
    starts = jnp.cumsum(counts) - counts
    row_total = jnp.sum(counts)
    slot_pos = jnp.arange(slot_cap, dtype=jnp.int32)
    packed_pos = jnp.where(
        slot_pos[None, :] < counts[:, None], starts[:, None] + slot_pos[None, :], slot_total
    ).reshape(-1)
    pack_source = (
        jnp.full((slot_total + 1,), slot_total, jnp.int32)
        .at[packed_pos]
        .set(jnp.arange(slot_total, dtype=jnp.int32))[:slot_total]
    )
    zero_row = jnp.zeros((1, feature_dim), jnp.bfloat16)
    packed_x = jnp.concatenate([slot_rows.reshape(slot_total, feature_dim), zero_row], axis=0)[
        pack_source
    ]
    packed_grad = jnp.concatenate([slot_grads.reshape(slot_total, feature_dim), zero_row], axis=0)[
        pack_source
    ]
    block_width = 128
    block_rows = math.gcd(slot_total, block_width)
    block_count = (row_total + block_rows - 1) // block_rows

    def block_step(block_index, state_tuple):
        outs_acc, rows_acc, in_acc, out_acc = state_tuple
        first_row = block_index * block_rows
        x_block = lax.dynamic_slice_in_dim(packed_x, first_row, block_rows, 0)
        grad_block = lax.dynamic_slice_in_dim(packed_grad, first_row, block_rows, 0)
        expert_out, row_grad, grad_in, grad_out = expert_pass(
            x_block, grad_block, weight_in, weight_out
        )
        outs_acc = lax.dynamic_update_slice_in_dim(outs_acc, expert_out, first_row, 0)
        rows_acc = lax.dynamic_update_slice_in_dim(rows_acc, row_grad, first_row, 0)
        return (outs_acc, rows_acc, in_acc + grad_in, out_acc + grad_out)

    initial = (
        jnp.zeros((slot_total, feature_dim), jnp.bfloat16),
        jnp.zeros((slot_total, feature_dim), jnp.bfloat16),
        jnp.zeros((feature_dim, hidden_dim), jnp.float32),
        jnp.zeros((hidden_dim, feature_dim), jnp.float32),
    )
    packed_out, packed_rows, grad_in, grad_out = lax.fori_loop(0, block_count, block_step, initial)
    slot_out = jnp.concatenate([packed_out, zero_row], axis=0)[packed_pos].reshape(
        sources, slot_cap, feature_dim
    )
    slot_back = jnp.concatenate([packed_rows, zero_row], axis=0)[packed_pos].reshape(
        sources, slot_cap, feature_dim
    )
    return (slot_out, slot_back, grad_in, grad_out)


def local(tokens, expert_ids, gate_weights, out_grad, w_in, w_out):
    axis_devices = lax.axis_size("expert")
    my_index = lax.axis_index("expert")
    tok_count, feature_dim = tokens.shape
    slot_cap = 6 * tok_count // axis_devices
    assign_count = 2 * tok_count
    all_ids = lax.all_gather(expert_ids, "expert", axis=0, tiled=True)
    source_ids = all_ids.reshape(axis_devices, assign_count)
    flat_ids = expert_ids.reshape(-1)
    slot_rank = slot_ranks(flat_ids, axis_devices)
    stays_here = jnp.zeros(flat_ids.shape, bool)
    spare_slot = axis_devices * slot_cap
    slot_index = jnp.where(stays_here, spare_slot, flat_ids * slot_cap + slot_rank)
    slot_source = (
        jnp.full((spare_slot + 1,), assign_count, jnp.int32)
        .at[slot_index]
        .set(jnp.arange(assign_count, dtype=jnp.int32))[:spare_slot]
    )
    zero_row = jnp.zeros((1, feature_dim), jnp.bfloat16)
    x_rows = jnp.concatenate([jnp.repeat(tokens, 2, axis=0), zero_row], axis=0)
    scaled = (
        gate_weights.reshape(-1, 1) * jnp.repeat(out_grad, 2, axis=0).astype(jnp.float32)
    ).astype(jnp.bfloat16)
    grad_rows = jnp.concatenate([scaled, zero_row], axis=0)
    send_x = x_rows[slot_source].reshape(axis_devices, slot_cap, feature_dim)
    send_grad = grad_rows[slot_source].reshape(axis_devices, slot_cap, feature_dim)
    got_x, got_grad = (
        lax.all_to_all(send_x, "expert", split_axis=0, concat_axis=0, tiled=True),
        lax.all_to_all(send_grad, "expert", split_axis=0, concat_axis=0, tiled=True),
    )
    local_out = jnp.zeros((slot_cap + 1, feature_dim), jnp.bfloat16)
    local_back = jnp.zeros((slot_cap + 1, feature_dim), jnp.bfloat16)
    counts = jnp.sum(source_ids == my_index, axis=1)
    expert_out, row_grad, grad_in, grad_out = serve_rows(got_x, got_grad, counts, w_in[0], w_out[0])
    ret_out, ret_grad = (
        lax.all_to_all(expert_out, "expert", split_axis=0, concat_axis=0, tiled=True),
        lax.all_to_all(row_grad, "expert", split_axis=0, concat_axis=0, tiled=True),
    )
    padded_out = jnp.concatenate([ret_out.reshape(-1, feature_dim), zero_row], axis=0)[slot_index]
    padded_back = jnp.concatenate([ret_grad.reshape(-1, feature_dim), zero_row], axis=0)[slot_index]
    local_slot = jnp.where(stays_here, slot_rank, slot_cap)
    keep_mask = stays_here[:, None]
    picked_out = jnp.where(keep_mask, local_out[local_slot], padded_out)
    picked_back = jnp.where(keep_mask, local_back[local_slot], padded_back)
    out_rows = picked_out.reshape(tok_count, 2, feature_dim).astype(jnp.float32)
    moe_out = jnp.sum(gate_weights[:, :, None] * out_rows, axis=1).astype(jnp.bfloat16)
    back_rows = picked_back.reshape(tok_count, 2, feature_dim).astype(jnp.float32)
    token_grad = jnp.sum(back_rows, axis=1).astype(jnp.bfloat16)
    return (
        moe_out,
        token_grad,
        grad_in[None].astype(jnp.bfloat16),
        grad_out[None].astype(jnp.bfloat16),
    )


def solution(mesh):
    placed = (
        P(("groups", "expert"), None),
        P(("groups", "expert"), None),
        P(("groups", "expert"), None),
        P(("groups", "expert"), None),
        P("expert", None, None),
        P("expert", None, None),
    )
    return jax.shard_map(
        local,
        mesh=mesh,
        in_specs=placed,
        out_specs=(
            P(("groups", "expert"), None),
            P(("groups", "expert"), None),
            P(("groups", "expert"), None, None),
            P(("groups", "expert"), None, None),
        ),
        check_vma=False,
    )
```

profile of v0, /device:TPU:15, one launch (start us, length us, event | category | flops | bytes accessed | tf_op | source)
XLA Modules:
  0.0 654.1 jit_solution(4019939654064476231)
XLA Ops:
  14.8 5.8 gather_fusion.2
  20.6 6.7 %all-to-all-start.1 = ((bf16[16,96,1024]{2,1,0:T(8,128)(2,1)}), bf16[16,96,1024]{2,1,0:T(8,128)(2,1)}, u32[]{:S(2)}, u32[]{:S(2)}) async-start(bf16[16,96,1024]{2,1,0:T(8,128)(2,1)} %bitcast.60), calls=%async_computation.1 | async-start | bytes 6291456 | tf_op jit(solution)/shard_map/all_to_all | solution.py:131
  28.4 5.8 gather_fusion
  34.2 63.1 %all-to-all-done.1 = bf16[16,96,1024]{2,1,0:T(8,128)(2,1)} async-done(((bf16[16,96,1024]{2,1,0:T(8,128)(2,1)}), bf16[16,96,1024]{2,1,0:T(8,128)(2,1)}, u32[]{:S(2)}, u32[]{:S(2)}) %all-to-all-start.1) | async-done | bytes 3145760 | tf_op jit(solution)/shard_map/all_to_all | solution.py:131
  97.3 5.0 all-to-all-start
  102.3 79.4 %all_gather.3 = s32[4096,2]{0,1:T(2,128)S(1)} all-gather(s32[256,2]{0,1:T(2,128)S(1)} %copy-done.9), channel_id=1, replica_groups=mesh['groups'=2,'expert'=16] {'expert'}, dimensions={0}, use_global_device_ids=true | all-gather | bytes 34816 | tf_op jit(solution)/shard_map/all_gather | solution.py:109
  183.7 6.2 scatter_custom_fusion.1
  192.1 5.9 gather_fusion.3
  200.2 5.8 gather_fusion.1
  205.9 4.3 broadcast_in_dim.35
  210.2 4.3 broadcast_in_dim.36
  217.0 268.4 %while.16 = (s32[]{:T(128)}, bf16[1536,1024]{1,0:T(8,128)(2,1)S(1)}, bf16[1536,1024]{1,0:T(8,128)(2,1)}, f32[1024,2048]{1,0:T(8,128)}, f32[2048,1024]{1,0:T(8,12...) while((s32[]{:T(128)}, ...), condition=%wide.region_10.11_spmd, body=%wide.region_9.10_spmd.sunk | while | flops 3230924800 | bytes 217055648 | solution.py:93
  220.1 4.4 fusion.59
  242.5 4.4 fusion.59
  264.9 4.4 fusion.59
  287.2 4.4 fusion.59
  309.6 4.4 fusion.59
  332.0 4.4 fusion.59
  354.3 4.4 fusion.59
  376.7 4.4 fusion.59
  399.1 4.4 fusion.59
  421.4 4.4 fusion.59
  443.8 4.4 fusion.59
  466.2 4.4 fusion.59
  489.2 5.8 gather_fusion.4
  495.0 4.4 all-to-all-start.2
  501.6 5.9 gather_fusion.6
  507.4 61.5 %all-to-all-done.2 = bf16[16,96,1024]{2,1,0:T(8,128)(2,1)} async-done(((bf16[16,96,1024]{2,1,0:T(8,128)(2,1)}), bf16[16,96,1024]{2,1,0:T(8,128)(2,1)}, u32[]{:S(2)}, u32[]{:S(2)}) %all-to-all-start.2) | async-done | bytes 3145760 | tf_op jit(solution)/shard_map/all_to_all | solution.py:138
  569.0 5.0 all-to-all-start.3
  574.0 6.1 convert_bitcast_fusion
  580.1 6.0 convert_bitcast_fusion.1
  597.0 47.0 %all-to-all-done.3 = bf16[16,96,1024]{2,1,0:T(8,128)(2,1)} async-done(((bf16[16,96,1024]{2,1,0:T(8,128)(2,1)}), bf16[16,96,1024]{2,1,0:T(8,128)(2,1)}, u32[]{:S(2)}, u32[]{:S(2)}) %all-to-all-start.3) | async-done | bytes 3145760 | tf_op jit(solution)/shard_map/all_to_all | solution.py:139
  (310 shorter events, 263.8 us)
Async XLA Ops:
  20.6 6.7 %copy-start.8 = (bf16[256,1024]{1,0:T(8,128)(2,1)S(1)}, bf16[256,1024]{1,0:T(8,128)(2,1)}, u32[]{:S(2)}) copy-start(bf16[256,1024]{1,0:T(8,128)(2,1)} %param.8) | copy-start | bytes 1572868
  20.6 76.7 %all-to-all-start.1 = ((bf16[16,96,1024]{2,1,0:T(8,128)(2,1)}), bf16[16,96,1024]{2,1,0:T(8,128)(2,1)}, u32[]{:S(2)}, u32[]{:S(2)}) async-start(bf16[16,96,1024]{2,1,0:T(8,128)(2,1)} %bitcast.60), calls=%async_computation.1 | async-start | bytes 6291456 | tf_op jit(solution)/shard_map/all_to_all | solution.py:131
  97.3 100.7 %all-to-all-start = ((bf16[16,96,1024]{2,1,0:T(8,128)(2,1)}), bf16[16,96,1024]{2,1,0:T(8,128)(2,1)}, u32[]{:S(2)}, u32[]{:S(2)}) async-start(bf16[16,96,1024]{2,1,0:T(8,128)(2,1)} %bitcast.58), calls=%async_computation | async-start | bytes 6291456 | tf_op jit(solution)/shard_map/all_to_all | solution.py:130
  217.0 7.6 %copy-start.1 = (f32[1024,2048]{1,0:T(8,128)S(1)}, f32[1024,2048]{1,0:T(8,128)}, u32[]{:S(2)}) copy-start(f32[1024,2048]{1,0:T(8,128)} %get-tuple-element.165) | copy-start | bytes 25165828 | tf_op jit(solution)/shard_map/while
  220.1 10.4 %slice-start = ((s8[8388608]{0:T(1024)(128)(4,1)}), s8[4194304]{0:T(1024)(128)(4,1)S(1)}, s32[]{:S(2)}) async-start(s8[8388608]{0:T(1024)(128)(4,1)} %bitcast.55), calls=%async_computation.4 | async-start | bytes 8388608 | tf_op jit(solution)/shard_map/while
  239.3 7.6 %copy-start.1 = (f32[1024,2048]{1,0:T(8,128)S(1)}, f32[1024,2048]{1,0:T(8,128)}, u32[]{:S(2)}) copy-start(f32[1024,2048]{1,0:T(8,128)} %get-tuple-element.165) | copy-start | bytes 25165828 | tf_op jit(solution)/shard_map/while
  242.5 10.4 %slice-start = ((s8[8388608]{0:T(1024)(128)(4,1)}), s8[4194304]{0:T(1024)(128)(4,1)S(1)}, s32[]{:S(2)}) async-start(s8[8388608]{0:T(1024)(128)(4,1)} %bitcast.55), calls=%async_computation.4 | async-start | bytes 8388608 | tf_op jit(solution)/shard_map/while
  246.9 5.9 slice-start.1
  261.7 7.6 %copy-start.1 = (f32[1024,2048]{1,0:T(8,128)S(1)}, f32[1024,2048]{1,0:T(8,128)}, u32[]{:S(2)}) copy-start(f32[1024,2048]{1,0:T(8,128)} %get-tuple-element.165) | copy-start | bytes 25165828 | tf_op jit(solution)/shard_map/while
  264.8 10.4 %slice-start = ((s8[8388608]{0:T(1024)(128)(4,1)}), s8[4194304]{0:T(1024)(128)(4,1)S(1)}, s32[]{:S(2)}) async-start(s8[8388608]{0:T(1024)(128)(4,1)} %bitcast.55), calls=%async_computation.4 | async-start | bytes 8388608 | tf_op jit(solution)/shard_map/while
  269.3 5.9 slice-start.1
  284.1 7.6 %copy-start.1 = (f32[1024,2048]{1,0:T(8,128)S(1)}, f32[1024,2048]{1,0:T(8,128)}, u32[]{:S(2)}) copy-start(f32[1024,2048]{1,0:T(8,128)} %get-tuple-element.165) | copy-start | bytes 25165828 | tf_op jit(solution)/shard_map/while
  287.2 10.4 %slice-start = ((s8[8388608]{0:T(1024)(128)(4,1)}), s8[4194304]{0:T(1024)(128)(4,1)S(1)}, s32[]{:S(2)}) async-start(s8[8388608]{0:T(1024)(128)(4,1)} %bitcast.55), calls=%async_computation.4 | async-start | bytes 8388608 | tf_op jit(solution)/shard_map/while
  306.4 7.6 %copy-start.1 = (f32[1024,2048]{1,0:T(8,128)S(1)}, f32[1024,2048]{1,0:T(8,128)}, u32[]{:S(2)}) copy-start(f32[1024,2048]{1,0:T(8,128)} %get-tuple-element.165) | copy-start | bytes 25165828 | tf_op jit(solution)/shard_map/while
  309.6 10.4 %slice-start = ((s8[8388608]{0:T(1024)(128)(4,1)}), s8[4194304]{0:T(1024)(128)(4,1)S(1)}, s32[]{:S(2)}) async-start(s8[8388608]{0:T(1024)(128)(4,1)} %bitcast.55), calls=%async_computation.4 | async-start | bytes 8388608 | tf_op jit(solution)/shard_map/while
  328.8 7.6 %copy-start.1 = (f32[1024,2048]{1,0:T(8,128)S(1)}, f32[1024,2048]{1,0:T(8,128)}, u32[]{:S(2)}) copy-start(f32[1024,2048]{1,0:T(8,128)} %get-tuple-element.165) | copy-start | bytes 25165828 | tf_op jit(solution)/shard_map/while
  331.9 10.4 %slice-start = ((s8[8388608]{0:T(1024)(128)(4,1)}), s8[4194304]{0:T(1024)(128)(4,1)S(1)}, s32[]{:S(2)}) async-start(s8[8388608]{0:T(1024)(128)(4,1)} %bitcast.55), calls=%async_computation.4 | async-start | bytes 8388608 | tf_op jit(solution)/shard_map/while
  351.2 7.6 %copy-start.1 = (f32[1024,2048]{1,0:T(8,128)S(1)}, f32[1024,2048]{1,0:T(8,128)}, u32[]{:S(2)}) copy-start(f32[1024,2048]{1,0:T(8,128)} %get-tuple-element.165) | copy-start | bytes 25165828 | tf_op jit(solution)/shard_map/while
  354.3 10.4 %slice-start = ((s8[8388608]{0:T(1024)(128)(4,1)}), s8[4194304]{0:T(1024)(128)(4,1)S(1)}, s32[]{:S(2)}) async-start(s8[8388608]{0:T(1024)(128)(4,1)} %bitcast.55), calls=%async_computation.4 | async-start | bytes 8388608 | tf_op jit(solution)/shard_map/while
  358.8 5.9 slice-start.1
  373.5 7.6 %copy-start.1 = (f32[1024,2048]{1,0:T(8,128)S(1)}, f32[1024,2048]{1,0:T(8,128)}, u32[]{:S(2)}) copy-start(f32[1024,2048]{1,0:T(8,128)} %get-tuple-element.165) | copy-start | bytes 25165828 | tf_op jit(solution)/shard_map/while
  376.7 10.4 %slice-start = ((s8[8388608]{0:T(1024)(128)(4,1)}), s8[4194304]{0:T(1024)(128)(4,1)S(1)}, s32[]{:S(2)}) async-start(s8[8388608]{0:T(1024)(128)(4,1)} %bitcast.55), calls=%async_computation.4 | async-start | bytes 8388608 | tf_op jit(solution)/shard_map/while
  395.9 7.6 %copy-start.1 = (f32[1024,2048]{1,0:T(8,128)S(1)}, f32[1024,2048]{1,0:T(8,128)}, u32[]{:S(2)}) copy-start(f32[1024,2048]{1,0:T(8,128)} %get-tuple-element.165) | copy-start | bytes 25165828 | tf_op jit(solution)/shard_map/while
  399.0 10.4 %slice-start = ((s8[8388608]{0:T(1024)(128)(4,1)}), s8[4194304]{0:T(1024)(128)(4,1)S(1)}, s32[]{:S(2)}) async-start(s8[8388608]{0:T(1024)(128)(4,1)} %bitcast.55), calls=%async_computation.4 | async-start | bytes 8388608 | tf_op jit(solution)/shard_map/while
  418.3 7.6 %copy-start.1 = (f32[1024,2048]{1,0:T(8,128)S(1)}, f32[1024,2048]{1,0:T(8,128)}, u32[]{:S(2)}) copy-start(f32[1024,2048]{1,0:T(8,128)} %get-tuple-element.165) | copy-start | bytes 25165828 | tf_op jit(solution)/shard_map/while
  421.4 10.4 %slice-start = ((s8[8388608]{0:T(1024)(128)(4,1)}), s8[4194304]{0:T(1024)(128)(4,1)S(1)}, s32[]{:S(2)}) async-start(s8[8388608]{0:T(1024)(128)(4,1)} %bitcast.55), calls=%async_computation.4 | async-start | bytes 8388608 | tf_op jit(solution)/shard_map/while
  440.6 7.6 %copy-start.1 = (f32[1024,2048]{1,0:T(8,128)S(1)}, f32[1024,2048]{1,0:T(8,128)}, u32[]{:S(2)}) copy-start(f32[1024,2048]{1,0:T(8,128)} %get-tuple-element.165) | copy-start | bytes 25165828 | tf_op jit(solution)/shard_map/while
  443.8 10.4 %slice-start = ((s8[8388608]{0:T(1024)(128)(4,1)}), s8[4194304]{0:T(1024)(128)(4,1)S(1)}, s32[]{:S(2)}) async-start(s8[8388608]{0:T(1024)(128)(4,1)} %bitcast.55), calls=%async_computation.4 | async-start | bytes 8388608 | tf_op jit(solution)/shard_map/while
  463.0 7.6 %copy-start.1 = (f32[1024,2048]{1,0:T(8,128)S(1)}, f32[1024,2048]{1,0:T(8,128)}, u32[]{:S(2)}) copy-start(f32[1024,2048]{1,0:T(8,128)} %get-tuple-element.165) | copy-start | bytes 25165828 | tf_op jit(solution)/shard_map/while
  466.1 10.4 %slice-start = ((s8[8388608]{0:T(1024)(128)(4,1)}), s8[4194304]{0:T(1024)(128)(4,1)S(1)}, s32[]{:S(2)}) async-start(s8[8388608]{0:T(1024)(128)(4,1)} %bitcast.55), calls=%async_computation.4 | async-start | bytes 8388608 | tf_op jit(solution)/shard_map/while
  495.0 74.0 %all-to-all-start.2 = ((bf16[16,96,1024]{2,1,0:T(8,128)(2,1)}), bf16[16,96,1024]{2,1,0:T(8,128)(2,1)}, u32[]{:S(2)}, u32[]{:S(2)}) async-start(bf16[16,96,1024]{2,1,0:T(8,128)(2,1)} %bitcast.61), calls=%async_computation.2 | async-start | bytes 6291456 | tf_op jit(solution)/shard_map/all_to_all | solution.py:138
  569.0 75.0 %all-to-all-start.3 = ((bf16[16,96,1024]{2,1,0:T(8,128)(2,1)}), bf16[16,96,1024]{2,1,0:T(8,128)(2,1)}, u32[]{:S(2)}, u32[]{:S(2)}) async-start(bf16[16,96,1024]{2,1,0:T(8,128)(2,1)} %bitcast.59), calls=%async_computation.3 | async-start | bytes 6291456 | tf_op jit(solution)/shard_map/all_to_all | solution.py:139
  (63 other events, 256.1 us)
where the time goes:
time: 656 us; the launch traced here: 654 us
  matrix products  191 us (29%)
  waiting for transfers between devices  172 us (26%)
  local copies, waits for them, and re-layouts  163 us (25%)
  blocking collectives  79.4 us (12%)
  other arithmetic  24 us (4%)
  starting transfers between devices  21.1 us (3%)
    all_gather x1, blocking collectives, local(): all_ids = lax.all_gather(expert_ids, 'expert', axis=0, tiled=True)  79.4 us
    while x168, local copies, waits for them, and re-layouts  75.6 us
    all_to_all x1, waiting for transfers between devices, local(): lax.all_to_all(send_grad, 'expert', split_axis=0, concat_axis=0, tiled=True)  63.1 us
    all_to_all x1, waiting for transfers between devices, local(): lax.all_to_all(expert_out, 'expert', split_axis=0, concat_axis=0, tiled=T...  61.5 us
    dot_general x12, matrix products, expert_pass(): lax.dot_general(grad_block, weight_out, (((1,), (1,)), ((), ())), preferr...  53.2 us
    all_to_all x1, waiting for transfers between devices, local(): lax.all_to_all(row_grad, 'expert', split_axis=0, concat_axis=0, tiled=True)  47 us
    dot_general x12, matrix products, expert_pass(): pre_act = jnp.dot(x_block, weight_in, preferred_element_type=jnp.float32)  37.6 us
    dot_general x12, matrix products, expert_pass(): lax.dot_general(x_block, pre_grad, (((0,), (0,)), ((), ())), preferred_el...  32.4 us
  transfers between devices with their start and end apart: 4, of which 3 were waited for; matrix products, arithmetic and copies ran while one was open for 8% of the time, Pallas kernels for 0%

commit v1 on v0

v1 whole, which is shorter than its diff:
```python
import functools

import jax
import jax.numpy as jnp
from jax import lax
from jax.experimental import pallas as pl
from jax.experimental.pallas import tpu as pltpu
from jax.sharding import PartitionSpec as P

AXIS = "expert"
PLANE = 4
INV_ROOT_TWO = 0.7071067811865476
INV_ROOT_TAU = 0.3989422804014327
BF16 = jnp.bfloat16
F32 = jnp.float32
SMEM = pl.BlockSpec(memory_space=pltpu.SMEM)
VMEM = pl.BlockSpec(memory_space=pltpu.VMEM)


def params(mib):
    return pltpu.CompilerParams(vmem_limit_bytes=mib * 1024 * 1024)


def dot(a, b, dims):
    return lax.dot_general(a, b, (dims, ((), ())), preferred_element_type=F32)


def slot_source(z, slot, length):
    near = min(z, length - 1 - z)
    far_up = z < length - 1 - z
    if slot <= 2 * near:
        return (slot + 1) // 2, far_up == (slot % 2 == 1)
    return slot - near, far_up


def slot_of(z, t, up, length):
    for slot in range(1, length):
        if slot_source(z, slot, length) == (t, up):
            return slot
    return None


def choose(z, values, pick):
    used = sorted({p for p in pick if p is not None})
    result = values[used[0]]
    for p in used[1:]:
        here = functools.reduce(jnp.logical_or, [z == k for k, q in enumerate(pick) if q == p])
        result = jnp.where(here, values[p], result)
    return result


def route_kernel(slots, cap, where_ref, meta_ref, pick_ref, put_ref, row_gate_ref, token_gate_ref):
    z, lo = where_ref[0], where_ref[1]
    length, _, tokens = meta_ref.shape
    upper = (
        lax.broadcasted_iota(jnp.int32, (tokens, tokens), 0)
        < lax.broadcasted_iota(jnp.int32, (tokens, tokens), 1)
    ).astype(BF16)
    eye = lax.broadcasted_iota(jnp.int32, (tokens, tokens), 0) == lax.broadcasted_iota(
        jnp.int32, (tokens, tokens), 1
    )
    down = lax.broadcasted_iota(jnp.int32, (cap, tokens), 0).astype(F32)
    along = lax.broadcasted_iota(jnp.int32, (tokens, cap), 1).astype(F32)
    lane = lax.broadcasted_iota(jnp.int32, (tokens, 128), 1)
    for at, slot in enumerate(slots):
        block = meta_ref[where_ref[2 + slot]]
        first, second = block[0:1], block[1:2]
        gate_one, gate_two = block[2:3], block[3:4]
        marks, gates = [], []
        for peer in range(PLANE):
            expert = (z * PLANE + (lo ^ peer)).astype(F32)
            is_one = (first == expert).astype(F32)
            is_two = (second == expert).astype(F32)
            marks.append(is_one + is_two)
            gates.append(is_one * gate_one + is_two * gate_two)
        marks = jnp.concatenate(marks + marks, axis=0)
        rank = dot(marks.astype(BF16), upper, ((1,), (0,)))
        rank = jnp.where(marks > 0.0, rank, -1.0)
        token_gate = jnp.zeros((tokens, 128), F32)
        for peer in range(PLANE):
            row = rank[peer : peer + 1]
            hit = down == row
            pick_ref[at, peer] = hit.astype(F32).astype(BF16)
            gate = jnp.sum(jnp.where(hit, gates[peer], 0.0), axis=1, keepdims=True)
            row_gate_ref[at, peer] = jnp.broadcast_to(gate, (cap, 128))
            column = jnp.sum(jnp.where(eye, row, 0.0), axis=1, keepdims=True)
            put_ref[at, peer] = (along == column).astype(F32).astype(BF16)
            gate = jnp.sum(jnp.where(eye, gates[peer], 0.0), axis=1, keepdims=True)
            token_gate = jnp.where(lane == peer, gate, token_gate)
        token_gate_ref[at] = token_gate


def route(where, meta, slots, cap):
    _, _, tokens = meta.shape
    count = len(slots)
    return pl.pallas_call(
        functools.partial(route_kernel, slots, cap),
        out_shape=(
            jax.ShapeDtypeStruct((count, PLANE, cap, tokens), BF16),
            jax.ShapeDtypeStruct((count, PLANE, tokens, cap), BF16),
            jax.ShapeDtypeStruct((count, PLANE, cap, 128), F32),
            jax.ShapeDtypeStruct((count, tokens, 128), F32),
        ),
        in_specs=[SMEM, VMEM],
        out_specs=(VMEM,) * 4,
        compiler_params=params(32),
        cost_estimate=pl.CostEstimate(flops=10**7, bytes_accessed=10**6, transcendentals=0),
        name="route",
    )(where, meta)


def select_kernel(pick, scaled, where_ref, *refs):
    blocks = refs[: len(refs) - 2 - PLANE]
    pick_ref, row_gate_ref = refs[len(blocks) : len(blocks) + 2]
    outs = refs[len(blocks) + 2 :]
    block = choose(where_ref[0], [r[...] for r in blocks], pick)
    for peer in range(PLANE):
        rows = dot(pick_ref[0, peer], block, ((1,), (0,)))
        if scaled:
            rows = rows * row_gate_ref[0, peer][:, :1]
        outs[peer][...] = rows.astype(BF16)


def select(where, blocks, pick, routes, at, scaled):
    picks, _, row_gates, _ = routes
    _, _, cap, tokens = picks.shape
    width = blocks[0].shape[1]
    return pl.pallas_call(
        functools.partial(select_kernel, pick, scaled),
        grid=(1,),
        out_shape=(jax.ShapeDtypeStruct((cap, width), BF16),) * PLANE,
        in_specs=[SMEM]
        + [pl.BlockSpec(b.shape, lambda i: (0, 0)) for b in blocks]
        + [
            pl.BlockSpec((1, PLANE, cap, tokens), lambda i: (at, 0, 0, 0)),
            pl.BlockSpec((1, PLANE, cap, 128), lambda i: (at, 0, 0, 0)),
        ],
        out_specs=(pl.BlockSpec((cap, width), lambda i: (0, 0)),) * PLANE,
        compiler_params=params(40),
        cost_estimate=pl.CostEstimate(
            flops=2 * PLANE * cap * tokens * width,
            bytes_accessed=4 * 10**6,
            transcendentals=0,
        ),
        name="select_rows",
    )(where, *blocks, picks, row_gates)


def combine_kernel(pick, slots, gated, extras, where_ref, *refs):
    rows = [refs[PLANE * k : PLANE * (k + 1)] for k in range(len(slots))]
    rest = refs[PLANE * len(slots) :]
    puts, rest = rest[: len(slots)], rest[len(slots) :]
    gates, rest = rest[: len(slots)], rest[len(slots) :]
    more, out_ref = rest[:extras], rest[extras]
    z = where_ref[0]
    total = None
    for ref in more:
        value = ref[...].astype(F32)
        total = value if total is None else total + value
    gate = choose(z, [g[0] for g in gates], pick)
    for peer in range(PLANE):
        put = choose(z, [p[0, peer] for p in puts], pick)
        row = choose(z, [r[peer][...] for r in rows], pick)
        part = dot(put, row, ((1,), (0,)))
        if gated:
            part = part * gate[:, peer : peer + 1]
        total = part if total is None else total + part
    out_ref[...] = total.astype(BF16)


def combine(where, rows, routes, pick, gated, extras):
    slots = sorted({p for p in pick if p is not None})
    pick = [None if p is None else slots.index(p) for p in pick]
    cap, width = rows[slots[0]][0].shape
    tokens = routes[slots[0]][0][1].shape[2]
    operands, specs = [], []
    for s in slots:
        operands += list(rows[s])
        specs += [pl.BlockSpec((cap, width), lambda i: (0, 0))] * PLANE
    for s in slots:
        found, at = routes[s]
        operands.append(found[1])
        specs.append(
            pl.BlockSpec((1, PLANE, tokens, cap), functools.partial(lambda a, i: (a, 0, 0, 0), at))
        )
    for s in slots:
        found, at = routes[s]
        operands.append(found[3])
        specs.append(pl.BlockSpec((1, tokens, 128), functools.partial(lambda a, i: (a, 0, 0), at)))
    operands += list(extras)
    specs += [pl.BlockSpec((tokens, width), lambda i: (0, 0))] * len(extras)
    return pl.pallas_call(
        functools.partial(combine_kernel, pick, slots, gated, len(extras)),
        grid=(1,),
        out_shape=jax.ShapeDtypeStruct((tokens, width), BF16),
        in_specs=[SMEM] + specs,
        out_specs=pl.BlockSpec((tokens, width), lambda i: (0, 0)),
        compiler_params=params(40),
        cost_estimate=pl.CostEstimate(
            flops=2 * PLANE * cap * tokens * width,
            bytes_accessed=4 * 10**6,
            transcendentals=0,
        ),
        name="combine_rows",
    )(where, *operands)


def gelu_parts(pre_act):
    normal_cdf = 0.5 * (1.0 + lax.erf(pre_act * INV_ROOT_TWO))
    normal_pdf = jnp.exp(-0.5 * pre_act * pre_act) * INV_ROOT_TAU
    return (pre_act * normal_cdf, normal_cdf + pre_act * normal_pdf)


def gather_pieces(cap, pieces, whole_ref):
    for k, ref in enumerate(pieces):
        whole_ref[k * cap : (k + 1) * cap, :] = ref[...]


def forward_kernel(cap, steps, *refs):
    pieces, (win_ref, wout_ref) = refs[:PLANE], refs[PLANE : PLANE + 2]
    outs = refs[PLANE + 2 : 2 * PLANE + 2]
    x_ref, act_ref, slope_ref, total = refs[2 * PLANE + 2 :]
    step = pl.program_id(0)

    @pl.when(step == 0)
    def _():
        gather_pieces(cap, pieces, x_ref)

    pre_act = dot(x_ref[...], win_ref[0], ((1,), (0,)))
    act, slope = gelu_parts(pre_act)
    act = act.astype(BF16)
    act_ref[...] = act
    slope_ref[...] = slope
    part = dot(act, wout_ref[0], ((1,), (0,)))

    @pl.when(step == 0)
    def _():
        total[...] = part

    @pl.when(step > 0)
    def _():
        total[...] += part

    @pl.when(step == steps - 1)
    def _():
        for k, ref in enumerate(outs):
            ref[...] = total[k * cap : (k + 1) * cap, :].astype(BF16)


def forward(pieces, w_in, w_out, tile=512):
    cap, width = pieces[0].shape
    hidden = w_in.shape[2]
    rows, steps = PLANE * cap, hidden // tile
    piece = pl.BlockSpec((cap, width), lambda f: (0, 0))
    result = pl.pallas_call(
        functools.partial(forward_kernel, cap, steps),
        grid=(steps,),
        out_shape=(jax.ShapeDtypeStruct((cap, width), BF16),) * PLANE
        + (
            jax.ShapeDtypeStruct((rows, width), BF16),
            jax.ShapeDtypeStruct((rows, hidden), BF16),
            jax.ShapeDtypeStruct((rows, hidden), F32),
        ),
        in_specs=[piece] * PLANE
        + [
            pl.BlockSpec((1, width, tile), lambda f: (0, 0, f)),
            pl.BlockSpec((1, tile, width), lambda f: (0, f, 0)),
        ],
        out_specs=(piece,) * PLANE
        + (
            pl.BlockSpec((rows, width), lambda f: (0, 0)),
            pl.BlockSpec((rows, tile), lambda f: (0, f)),
            pl.BlockSpec((rows, tile), lambda f: (0, f)),
        ),
        scratch_shapes=[pltpu.VMEM((rows, width), F32)],
        compiler_params=params(48),
        cost_estimate=pl.CostEstimate(
            flops=4 * rows * width * hidden,
            bytes_accessed=4 * width * hidden + 8 * rows * hidden,
            transcendentals=2 * rows * hidden,
        ),
        name="expert_forward",
    )(*pieces, w_in, w_out)
    return result[:PLANE], result[PLANE], result[PLANE + 1], result[PLANE + 2]


def backward_kernel(cap, steps, *refs):
    pieces, (win_ref, wout_ref, slope_ref) = refs[:PLANE], refs[PLANE : PLANE + 3]
    outs = refs[PLANE + 3 : 2 * PLANE + 3]
    grad_ref, pre_ref, total = refs[2 * PLANE + 3 :]
    step = pl.program_id(0)

    @pl.when(step == 0)
    def _():
        gather_pieces(cap, pieces, grad_ref)

    act_grad = dot(grad_ref[...], wout_ref[0], ((1,), (1,)))
    pre_grad = (act_grad * slope_ref[...]).astype(BF16)
    pre_ref[...] = pre_grad
    part = dot(pre_grad, win_ref[0], ((1,), (1,)))

    @pl.when(step == 0)
    def _():
        total[...] = part

    @pl.when(step > 0)
    def _():
        total[...] += part

    @pl.when(step == steps - 1)
    def _():
        for k, ref in enumerate(outs):
            ref[...] = total[k * cap : (k + 1) * cap, :].astype(BF16)


def backward(pieces, w_in, w_out, slope, tile=512):
    cap, width = pieces[0].shape
    hidden = w_in.shape[2]
    rows, steps = PLANE * cap, hidden // tile
    piece = pl.BlockSpec((cap, width), lambda f: (0, 0))
    result = pl.pallas_call(
        functools.partial(backward_kernel, cap, steps),
        grid=(steps,),
        out_shape=(jax.ShapeDtypeStruct((cap, width), BF16),) * PLANE
        + (
            jax.ShapeDtypeStruct((rows, width), BF16),
            jax.ShapeDtypeStruct((rows, hidden), BF16),
        ),
        in_specs=[piece] * PLANE
        + [
            pl.BlockSpec((1, width, tile), lambda f: (0, 0, f)),
            pl.BlockSpec((1, tile, width), lambda f: (0, f, 0)),
            pl.BlockSpec((rows, tile), lambda f: (0, f)),
        ],
        out_specs=(piece,) * PLANE
        + (
            pl.BlockSpec((rows, width), lambda f: (0, 0)),
            pl.BlockSpec((rows, tile), lambda f: (0, f)),
        ),
        scratch_shapes=[pltpu.VMEM((rows, width), F32)],
        compiler_params=params(48),
        cost_estimate=pl.CostEstimate(
            flops=4 * rows * width * hidden,
            bytes_accessed=4 * width * hidden + 6 * rows * hidden,
            transcendentals=0,
        ),
        name="expert_backward",
    )(*pieces, w_in, w_out, slope)
    return result[:PLANE], result[PLANE], result[PLANE + 1]


def weights_kernel(count, *refs):
    xs, pres = refs[:count], refs[count : 2 * count]
    acts, grads = refs[2 * count : 3 * count], refs[3 * count : 4 * count]
    gin_ref, gout_ref = refs[4 * count :]
    gin = gout = None
    for x, pre, act, grad in zip(xs, pres, acts, grads):
        part = dot(x[...], pre[...], ((0,), (0,)))
        gin = part if gin is None else gin + part
        part = dot(act[...], grad[...], ((0,), (0,)))
        gout = part if gout is None else gout + part
    gin_ref[0] = gin.astype(BF16)
    gout_ref[0] = gout.astype(BF16)


def weight_grads(xs, pres, acts, grads, tile=512):
    rows, width = xs[0].shape
    hidden = acts[0].shape[1]
    count = len(xs)
    whole = pl.BlockSpec((rows, width), lambda f: (0, 0))
    part = pl.BlockSpec((rows, tile), lambda f: (0, f))
    return pl.pallas_call(
        functools.partial(weights_kernel, count),
        grid=(hidden // tile,),
        out_shape=(
            jax.ShapeDtypeStruct((1, width, hidden), BF16),
            jax.ShapeDtypeStruct((1, hidden, width), BF16),
        ),
        in_specs=[whole] * count + [part] * (2 * count) + [whole] * count,
        out_specs=(
            pl.BlockSpec((1, width, tile), lambda f: (0, 0, f)),
            pl.BlockSpec((1, tile, width), lambda f: (0, f, 0)),
        ),
        compiler_params=params(56),
        cost_estimate=pl.CostEstimate(
            flops=4 * count * rows * width * hidden,
            bytes_accessed=4 * width * hidden + 4 * count * rows * (width + hidden),
            transcendentals=0,
        ),
        name="weight_grads",
    )(*xs, *pres, *acts, *grads)


def permute(value, pairs):
    return lax.ppermute(value, AXIS, pairs)


def shift_pairs(length, step, first, last):
    return [
        (z * PLANE + lo, (z + step) * PLANE + lo)
        for z in range(max(first, 0), min(last, length))
        if 0 <= z + step < length
        for lo in range(PLANE)
    ]


def to_peer(value, peer, count):
    return permute(value, [(i, i ^ peer) for i in range(count)])


def gather_line(block, length):
    got = {(0, True): block, (0, False): block}
    for t in range(1, length):
        got[t, False] = permute(got[t - 1, False], shift_pairs(length, 1, t - 1, length))
        got[t, True] = permute(got[t - 1, True], shift_pairs(length, -1, 0, length - t + 1))
    return got


def local(tokens, expert_ids, gate_weights, out_grad, w_in, w_out):
    count = lax.axis_size(AXIS)
    me = lax.axis_index(AXIS)
    length = count // PLANE
    tok_count, _ = tokens.shape
    cap = 6 * tok_count // count
    z, lo = me // PLANE, me % PLANE

    sources = []
    for slot in range(length):
        per_z = []
        for k in range(length):
            t, up = slot_source(k, slot, length) if slot else (0, True)
            per_z.append((-t if up else t) % length)
        sources.append(jnp.asarray(per_z, jnp.int32)[z])
    where = jnp.stack([z, lo] + sources).astype(jnp.int32)

    meta = jnp.concatenate([expert_ids.T.astype(F32), gate_weights.T], axis=0)
    ring = [meta]
    for t in range(1, length):
        pairs = [
            (k * PLANE + j, (k + t) % length * PLANE + j)
            for k in range(length)
            for j in range(PLANE)
        ]
        ring.append(permute(meta, pairs))
    own_routes = route(where, meta[None], (0,), cap)
    far_routes = route(where, jnp.stack(ring), tuple(range(1, length)), cap)
    routes = [(own_routes, 0)] + [(far_routes, s) for s in range(length - 1)]

    def dispatch(got, slot, scaled):
        found, at = routes[slot]
        if slot == 0:
            blocks, pick = [got[0, True]], [0] * length
        else:
            per_z = [slot_source(k, slot, length) for k in range(length)]
            keys = sorted(set(per_z))
            blocks, pick = [got[k] for k in keys], [keys.index(k) for k in per_z]
        parts = select(where, blocks, pick, found, at, scaled)
        return [parts[0]] + [to_peer(parts[p], p, count) for p in range(1, PLANE)]

    def give_back(parts):
        return [parts[0]] + [to_peer(parts[p], p, count) for p in range(1, PLANE)]

    def reduce_line(rows, gated):
        up_in = down_in = None
        for t in range(length - 1, 0, -1):
            sends = []
            for up, moving in ((True, up_in), (False, down_in)):
                pick = [slot_of(k, t, up, length) for k in range(length)]
                extras = [] if moving is None else [moving]
                sends.append(combine(where, rows, routes, pick, gated, extras))
            up_in = permute(sends[0], shift_pairs(length, 1, 0, length - t))
            down_in = permute(sends[1], shift_pairs(length, -1, t, length))
        return combine(where, rows, routes, [0] * length, gated, [up_in, down_in])

    slots = range(length)
    got_x = gather_line(tokens, length)
    x_parts = [dispatch(got_x, s, False) for s in slots]
    held, _ = lax.optimization_barrier((out_grad, got_x[max(length - 2, 1), True]))
    got_grad = gather_line(held, length)
    grad_parts = [dispatch(got_grad, s, True) for s in slots]

    outs, xs, acts, slopes = zip(*[forward(x_parts[s], w_in, w_out) for s in slots])
    out_rows = [None] * length
    for s in reversed(slots):
        out_rows[s] = give_back(outs[s])
    moe_out = reduce_line(out_rows, True)

    backs, grads, pres = zip(*[backward(grad_parts[s], w_in, w_out, slopes[s]) for s in slots])
    back_rows = [None] * length
    for s in reversed(slots):
        back_rows[s] = give_back(backs[s])
    token_grad = reduce_line(back_rows, False)

    w_in_grad, w_out_grad = weight_grads(xs, pres, acts, grads)
    return moe_out, token_grad, w_in_grad, w_out_grad


def solution(mesh):
    rows, wide = P(("groups", AXIS), None), P(("groups", AXIS), None, None)
    weights = P(AXIS, None, None)
    return jax.shard_map(
        local,
        mesh=mesh,
        in_specs=(rows, rows, rows, rows, weights, weights),
        out_specs=(rows, rows, wide, wide),
        check_vma=False,
    )
```

time: 656 us -> 295 us (0.45)
  the two profiles are of different devices: /device:TPU:15 before, /device:TPU:0 now
where the time goes in v1:
time: 295 us; the launch traced here: 294 us
  Pallas kernels  117 us (40%)
  starting transfers between devices  95.2 us (32%)
  waiting for transfers between devices  67.7 us (23%)
  local copies, waits for them, and re-layouts  11.8 us (4%)
    ppermute x75, starting transfers between devices, permute(): return lax.ppermute(value, AXIS, pairs)  95.2 us
    ppermute x75, waiting for transfers between devices, permute(): return lax.ppermute(value, AXIS, pairs)  67.7 us
    pallas_call x4, Pallas kernels, forward(): pl.pallas_call(functools.partial(forward_kernel, cap, steps), grid=(steps...  35.1 us
    pallas_call x4, Pallas kernels, backward(): pl.pallas_call(functools.partial(backward_kernel, cap, steps), grid=(step...  30.2 us
    pallas_call x1, Pallas kernels, weight_grads(): pl.pallas_call(functools.partial(weights_kernel, count), grid=(hidden //...  23.5 us
    pallas_call x12, Pallas kernels, combine(): pl.pallas_call(functools.partial(combine_kernel, pick, slots, gated, len(...  16.8 us
    pallas_call x8, Pallas kernels, select(): pl.pallas_call(functools.partial(select_kernel, pick, scaled), grid=(1,),...  8.39 us
    unnamed x56, local copies, waits for them, and re-layouts  6.04 us
  transfers between devices with their start and end apart: 75, of which 19 were waited for; matrix products, arithmetic and copies ran while one was open for 2% of the time, Pallas kernels for 39%

profile of v1, /device:TPU:0, one launch (start us, length us, event | category | flops | bytes accessed | tf_op | source)
XLA Modules:
  0.0 294.1 jit_solution(7516685083013143925)
XLA Ops:
  1.9 15.8 %collective-permute-done.7.refs_1_ = bf16[256,1024]{1,0:T(8,128)(2,1)S(1)} collective-permute-done((bf16[256,1024]{1,0:T(8,128)(2,1)}, bf16[256,1024]{1,0:T(8,128)(2,1)S(1)}, u32[]{:S(2)}, u32[]{:S(2)}) %collective-permute-start.7) | collective-permute-done | bytes 524320 | tf_op jit(solution)/shard_map/ppermute | solution.py:395
  19.0 4.6 %collective-permute-start.6 = (bf16[256,1024]{1,0:T(8,128)(2,1)}, bf16[256,1024]{1,0:T(8,128)(2,1)S(1)}, u32[]{:S(2)}, u32[]{:S(2)}) collective-permute-start(bf16[256,1024]{1,0:T(8,128)(2,1)} %refs_0_.1), channel_id=1, source_target_pairs={{0,4},{1,5},{2,6},{3,7},{4,8},{5,9},{6,10},{7,11},{8,12},{9,13},{1... | collective-permute-start | bytes 1572872 | tf_op jit(solution)/shard_map/ppermute | solution.py:395
  23.6 9.1 %collective-permute-done.18.refs_3_.refs_1_ = bf16[256,1024]{1,0:T(8,128)(2,1)S(1)} collective-permute-done((bf16[256,1024]{1,0:T(8,128)(2,1)S(1)}, bf16[256,1024]{1,0:T(8,128)(2,1)S(1)}, u32[]{:S(2)}, u32[]{:S(2)}) %collective-permute-start.18) | collective-permute-done | bytes 524320 | tf_op jit(solution)/shard_map/ppermute | solution.py:395
  34.0 4.6 %collective-permute-start.45 = (bf16[256,1024]{1,0:T(8,128)(2,1)}, bf16[256,1024]{1,0:T(8,128)(2,1)S(1)}, u32[]{:S(2)}, u32[]{:S(2)}) collective-permute-start(bf16[256,1024]{1,0:T(8,128)(2,1)} %refs_0_.2), channel_id=1, source_target_pairs={{0,4},{1,5},{2,6},{3,7},{4,8},{5,9},{6,10},{7,11},{8,12},{9,13},{1... | collective-permute-start | bytes 1572872 | tf_op jit(solution)/shard_map/ppermute | solution.py:395
  40.6 2.1 collective-permute-start.9
  43.3 5.0 %collective-permute-done.9 = f32[4,256]{1,0:T(4,128)S(1)} collective-permute-done((f32[4,256]{1,0:T(4,128)S(1)}, f32[4,256]{1,0:T(4,128)S(1)}, u32[]{:S(2)}, u32[]{:S(2)}) %collective-permute-start.9) | collective-permute-done | bytes 4128 | tf_op jit(solution)/shard_map/ppermute | solution.py:395
  48.3 15.2 %collective-permute-start.10 = (f32[4,256]{1,0:T(4,128)S(1)}, f32[4,256]{1,0:T(4,128)S(1)}, u32[]{:S(2)}, u32[]{:S(2)}) collective-permute-start(f32[4,256]{1,0:T(4,128)S(1)} %get-tuple-element.194), channel_id=1, source_target_pairs={{0,12},{1,13},{2,14},{3,15},{4,0},{5,1},{6,2},{7,3},{8,4},{9,5},{1... | collective-permute-start | bytes 12296 | tf_op jit(solution)/shard_map/ppermute | solution.py:395
  77.8 5.8 %collective-permute-done.12.refs_2_ = bf16[96,1024]{1,0:T(8,128)(2,1)S(1)} collective-permute-done((bf16[96,1024]{1,0:T(8,128)(2,1)S(1)}, bf16[96,1024]{1,0:T(8,128)(2,1)S(1)}, u32[]{:S(2)}, u32[]{:S(2)}) %collective-permute-start.12) | collective-permute-done | bytes 196640 | tf_op jit(solution)/shard_map/ppermute | solution.py:395
  95.2 8.8 %expert_forward.5 = (bf16[96,1024]{1,0:T(8,128)(2,1)S(1)}, bf16[96,1024]{1,0:T(8,128)(2,1)S(1)}, bf16[96,1024]{1,0:T(8,128)(2,1)S(1)}, bf16[96,1024]{1,0:T(8,128...) custom-call(bf16[96,1024]{1,0:T(8,128)(2,1)S(1)} %get-tuple-element.113.refs_0_, ...), custom_call_target="tpu_custom_call" | custom-call | flops 3221225472 | bytes 14680064 | tf_op jit(solution)/shard_map/expert_forward/pallas_call | solution.py:255
  110.2 8.7 %expert_forward.6 = (bf16[96,1024]{1,0:T(8,128)(2,1)S(1)}, bf16[96,1024]{1,0:T(8,128)(2,1)S(1)}, bf16[96,1024]{1,0:T(8,128)(2,1)S(1)}, bf16[96,1024]{1,0:T(8,128...) custom-call(bf16[96,1024]{1,0:T(8,128)(2,1)S(1)} %get-tuple-element.121.refs_0_, ...), custom_call_target="tpu_custom_call" | custom-call | flops 3221225472 | bytes 14680064 | tf_op jit(solution)/shard_map/expert_forward/pallas_call | solution.py:255
  123.0 8.8 %expert_forward.7 = (bf16[96,1024]{1,0:T(8,128)(2,1)S(1)}, bf16[96,1024]{1,0:T(8,128)(2,1)S(1)}, bf16[96,1024]{1,0:T(8,128)(2,1)S(1)}, bf16[96,1024]{1,0:T(8,128...) custom-call(bf16[96,1024]{1,0:T(8,128)(2,1)S(1)} %get-tuple-element.131.refs_0_, ...), custom_call_target="tpu_custom_call" | custom-call | flops 3221225472 | bytes 14680064 | tf_op jit(solution)/shard_map/expert_forward/pallas_call | solution.py:255
  137.3 7.5 %expert_backward.7 = (bf16[96,1024]{1,0:T(8,128)(2,1)S(1)}, bf16[96,1024]{1,0:T(8,128)(2,1)S(1)}, bf16[96,1024]{1,0:T(8,128)(2,1)S(1)}, bf16[96,1024]{1,0:T(8,12...) custom-call(bf16[96,1024]{1,0:T(8,128)(2,1)S(1)} %get-tuple-element.167.refs_0_, ...), custom_call_target="tpu_custom_call" | custom-call | flops 3221225472 | bytes 13107200 | tf_op jit(solution)/shard_map/expert_backward/pallas_call | solution.py:321
  150.4 3.1 %collective-permute-done.31.refs_2_.refs_6_ = bf16[96,1024]{1,0:T(8,128)(2,1)S(1)} collective-permute-done((bf16[96,1024]{1,0:T(8,128)(2,1)S(1)}, bf16[96,1024]{1,0:T(8,128)(2,1)S(1)}, u32[]{:S(2)}, u32[]{:S(2)}) %collective-permute-start.31) | collective-permute-done | bytes 196640 | tf_op jit(solution)/shard_map/ppermute | solution.py:395
  158.6 3.4 %collective-permute-done.67.refs_2_.refs_6_ = bf16[96,1024]{1,0:T(8,128)(2,1)S(1)} collective-permute-done((bf16[96,1024]{1,0:T(8,128)(2,1)S(1)}, bf16[96,1024]{1,0:T(8,128)(2,1)S(1)}, u32[]{:S(2)}, u32[]{:S(2)}) %collective-permute-start.67) | collective-permute-done | bytes 196640 | tf_op jit(solution)/shard_map/ppermute | solution.py:395
  166.7 3.7 %collective-permute-done.23.refs_2_.refs_6_ = bf16[96,1024]{1,0:T(8,128)(2,1)S(1)} collective-permute-done((bf16[96,1024]{1,0:T(8,128)(2,1)S(1)}, bf16[96,1024]{1,0:T(8,128)(2,1)S(1)}, u32[]{:S(2)}, u32[]{:S(2)}) %collective-permute-start.23) | collective-permute-done | bytes 196640 | tf_op jit(solution)/shard_map/ppermute | solution.py:395
  170.4 2.7 collective-permute-start.33
  175.3 2.1 collective-permute-done.57.refs_3_
  177.4 3.3 %collective-permute-start.69 = (bf16[256,1024]{1,0:T(8,128)(2,1)S(1)}, bf16[256,1024]{1,0:T(8,128)(2,1)S(1)}, u32[]{:S(2)}, u32[]{:S(2)}) collective-permute-start(bf16[256,1024]{1,0:T(8,128)(2,1)S(1)} %combine_rows.18), channel_id=1, source_target_pairs={{0,4},{1,5},{2,6},{3,7},{16,20},{17,21},{18,22},{19,23}} | collective-permute-start | bytes 1572872 | tf_op jit(solution)/shard_map/ppermute | solution.py:395
  180.7 7.6 %expert_backward.6 = (bf16[96,1024]{1,0:T(8,128)(2,1)S(1)}, bf16[96,1024]{1,0:T(8,128)(2,1)S(1)}, bf16[96,1024]{1,0:T(8,128)(2,1)S(1)}, bf16[96,1024]{1,0:T(8,12...) custom-call(bf16[96,1024]{1,0:T(8,128)(2,1)S(1)} %get-tuple-element.158.refs_0_, ...), custom_call_target="tpu_custom_call" | custom-call | flops 3221225472 | bytes 13107200 | tf_op jit(solution)/shard_map/expert_backward/pallas_call | solution.py:321
  195.5 2.6 collective-permute-done.59.refs_2_.refs_6_
  206.6 2.7 collective-permute-done.48.refs_2_
  210.0 2.0 collective-permute-done.49.refs_3_
  212.1 2.2 collective-permute-start.70
  214.3 7.6 %expert_backward.5 = (bf16[96,1024]{1,0:T(8,128)(2,1)S(1)}, bf16[96,1024]{1,0:T(8,128)(2,1)S(1)}, bf16[96,1024]{1,0:T(8,128)(2,1)S(1)}, bf16[96,1024]{1,0:T(8,12...) custom-call(bf16[96,1024]{1,0:T(8,128)(2,1)S(1)} %get-tuple-element.149.refs_0_, ...), custom_call_target="tpu_custom_call" | custom-call | flops 3221225472 | bytes 13107200 | tf_op jit(solution)/shard_map/expert_backward/pallas_call | solution.py:321
  231.7 2.5 collective-permute-done.51.refs_2_
  234.2 2.5 collective-permute-start.35
  236.8 8.7 %expert_forward.4 = (bf16[96,1024]{1,0:T(8,128)(2,1)S(1)}, bf16[96,1024]{1,0:T(8,128)(2,1)S(1)}, bf16[96,1024]{1,0:T(8,128)(2,1)S(1)}, bf16[96,1024]{1,0:T(8,128...) custom-call(bf16[96,1024]{1,0:T(8,128)(2,1)S(1)} %get-tuple-element.101.refs_0_, ...), custom_call_target="tpu_custom_call" | custom-call | flops 3221225472 | bytes 14680064 | tf_op jit(solution)/shard_map/expert_forward/pallas_call | solution.py:255
  248.6 7.5 %expert_backward.4 = (bf16[96,1024]{1,0:T(8,128)(2,1)S(1)}, bf16[96,1024]{1,0:T(8,128)(2,1)S(1)}, bf16[96,1024]{1,0:T(8,128)(2,1)S(1)}, bf16[96,1024]{1,0:T(8,12...) custom-call(bf16[96,1024]{1,0:T(8,128)(2,1)S(1)} %get-tuple-element.140.refs_0_, ...), custom_call_target="tpu_custom_call" | custom-call | flops 3221225472 | bytes 13107200 | tf_op jit(solution)/shard_map/expert_backward/pallas_call | solution.py:321
  261.9 4.6 %collective-permute-start.71 = (bf16[256,1024]{1,0:T(8,128)(2,1)S(1)}, bf16[256,1024]{1,0:T(8,128)(2,1)S(1)}, u32[]{:S(2)}, u32[]{:S(2)}) collective-permute-start(bf16[256,1024]{1,0:T(8,128)(2,1)S(1)} %combine_rows.20), channel_id=1, source_target_pairs={{0,4},{1,5},{2,6},{3,7},{4,8},{5,9},{6,10},{7,11},{8,12},{9,13},{1... | collective-permute-start | bytes 1572872 | tf_op jit(solution)/shard_map/ppermute | solution.py:395
  266.5 23.5 %weight_grads.1 = (bf16[1,1024,2048]{2,1,0:T(8,128)(2,1)}, bf16[1,2048,1024]{2,1,0:T(8,128)(2,1)}) custom-call(bf16[384,1024]{1,0:T(8,128)(2,1)} %copy-done.27, bf16[384,1024]{1,0:T(8,128)(2,1)} %copy-done.24, bf16[384,1024]{1,0:T(8,128)(2,1)} %copy-done.25, bf16[384,1024]{1,0:T(8,128)(2,1)} %copy-done.26, bf16[384,2048]{1,0:T(8,128)(2,1)} %copy-done.5, ...), custom_call_target="tpu_custom_call" | custom-call | flops 12884901888 | bytes 27262976 | tf_op jit(solution)/shard_map/weight_grads/pallas_call | solution.py:372
  289.9 2.1 combine_rows.17
  292.1 2.0 combine_rows.23
  (212 shorter events, 100.3 us)
Async XLA Ops:
  0.6 17.1 %collective-permute-start.7 = (bf16[256,1024]{1,0:T(8,128)(2,1)}, bf16[256,1024]{1,0:T(8,128)(2,1)S(1)}, u32[]{:S(2)}, u32[]{:S(2)}) collective-permute-start(bf16[256,1024]{1,0:T(8,128)(2,1)} %refs_0_.1), channel_id=1, source_target_pairs={{4,0},{5,1},{6,2},{7,3},{8,4},{9,5},{10,6},{11,7},{12,8},{13,9},{1... | collective-permute-start | bytes 1572872 | tf_op jit(solution)/shard_map/ppermute | solution.py:395
  19.0 19.6 %collective-permute-start.6 = (bf16[256,1024]{1,0:T(8,128)(2,1)}, bf16[256,1024]{1,0:T(8,128)(2,1)S(1)}, u32[]{:S(2)}, u32[]{:S(2)}) collective-permute-start(bf16[256,1024]{1,0:T(8,128)(2,1)} %refs_0_.1), channel_id=1, source_target_pairs={{0,4},{1,5},{2,6},{3,7},{4,8},{5,9},{6,10},{7,11},{8,12},{9,13},{1... | collective-permute-start | bytes 1572872 | tf_op jit(solution)/shard_map/ppermute | solution.py:395
  32.7 36.6 %collective-permute-start.46 = (bf16[256,1024]{1,0:T(8,128)(2,1)}, bf16[256,1024]{1,0:T(8,128)(2,1)S(1)}, u32[]{:S(2)}, u32[]{:S(2)}) collective-permute-start(bf16[256,1024]{1,0:T(8,128)(2,1)} %refs_0_.2), channel_id=1, source_target_pairs={{4,0},{5,1},{6,2},{7,3},{8,4},{9,5},{10,6},{11,7},{12,8},{13,9},{1... | collective-permute-start | bytes 1572872 | tf_op jit(solution)/shard_map/ppermute | solution.py:395
  34.0 36.6 %collective-permute-start.45 = (bf16[256,1024]{1,0:T(8,128)(2,1)}, bf16[256,1024]{1,0:T(8,128)(2,1)S(1)}, u32[]{:S(2)}, u32[]{:S(2)}) collective-permute-start(bf16[256,1024]{1,0:T(8,128)(2,1)} %refs_0_.2), channel_id=1, source_target_pairs={{0,4},{1,5},{2,6},{3,7},{4,8},{5,9},{6,10},{7,11},{8,12},{9,13},{1... | collective-permute-start | bytes 1572872 | tf_op jit(solution)/shard_map/ppermute | solution.py:395
  38.6 36.9 %collective-permute-start.17 = (bf16[256,1024]{1,0:T(8,128)(2,1)S(1)}, bf16[256,1024]{1,0:T(8,128)(2,1)S(1)}, u32[]{:S(2)}, u32[]{:S(2)}) collective-permute-start(bf16[256,1024]{1,0:T(8,128)(2,1)S(1)} %collective-permute-done.6.refs_0_), channel_id=1, source_target_pairs={{4,8},{5,9},{6,10},{7,11},{8,12},{9,13},{10,14},{11,15},{20,24},{2... | collective-permute-start | bytes 1572872 | tf_op jit(solution)/shard_map/ppermute | solution.py:395
  42.7 28.6 %collective-permute-start.8 = (f32[4,256]{1,0:T(4,128)S(1)}, f32[4,256]{1,0:T(4,128)S(1)}, u32[]{:S(2)}, u32[]{:S(2)}) collective-permute-start(f32[4,256]{1,0:T(4,128)S(1)} %get-tuple-element.194), channel_id=1, source_target_pairs={{0,4},{1,5},{2,6},{3,7},{4,8},{5,9},{6,10},{7,11},{8,12},{9,13},{1... | collective-permute-start | bytes 12296 | tf_op jit(solution)/shard_map/ppermute | solution.py:395
  48.3 23.0 %collective-permute-start.10 = (f32[4,256]{1,0:T(4,128)S(1)}, f32[4,256]{1,0:T(4,128)S(1)}, u32[]{:S(2)}, u32[]{:S(2)}) collective-permute-start(f32[4,256]{1,0:T(4,128)S(1)} %get-tuple-element.194), channel_id=1, source_target_pairs={{0,12},{1,13},{2,14},{3,15},{4,0},{5,1},{6,2},{7,3},{8,4},{9,5},{1... | collective-permute-start | bytes 12296 | tf_op jit(solution)/shard_map/ppermute | solution.py:395
  74.2 19.5 %collective-permute-start.26 = (bf16[256,1024]{1,0:T(8,128)(2,1)S(1)}, bf16[256,1024]{1,0:T(8,128)(2,1)S(1)}, u32[]{:S(2)}, u32[]{:S(2)}) collective-permute-start(bf16[256,1024]{1,0:T(8,128)(2,1)S(1)} %collective-permute-done.18.refs_3_.refs_1_), channel_id=1, source_target_pairs={{4,0},{5,1},{6,2},{7,3},{20,16},{21,17},{22,18},{23,19}} | collective-permute-start | bytes 1572872 | tf_op jit(solution)/shard_map/ppermute | solution.py:395
  75.5 19.7 %collective-permute-start.25 = (bf16[256,1024]{1,0:T(8,128)(2,1)S(1)}, bf16[256,1024]{1,0:T(8,128)(2,1)S(1)}, u32[]{:S(2)}, u32[]{:S(2)}) collective-permute-start(bf16[256,1024]{1,0:T(8,128)(2,1)S(1)} %collective-permute-done.17.refs_2_.refs_0_), channel_id=1, source_target_pairs={{8,12},{9,13},{10,14},{11,15},{24,28},{25,29},{26,30},{27,31}} | collective-permute-start | bytes 1572872 | tf_op jit(solution)/shard_map/ppermute | solution.py:395
  84.4 23.9 %collective-permute-start.62 = (bf16[256,1024]{1,0:T(8,128)(2,1)S(1)}, bf16[256,1024]{1,0:T(8,128)(2,1)S(1)}, u32[]{:S(2)}, u32[]{:S(2)}) collective-permute-start(bf16[256,1024]{1,0:T(8,128)(2,1)S(1)} %collective-permute-done.54.refs_3_.refs_1_), channel_id=1, source_target_pairs={{4,0},{5,1},{6,2},{7,3},{20,16},{21,17},{22,18},{23,19}} | collective-permute-start | bytes 1572872 | tf_op jit(solution)/shard_map/ppermute | solution.py:395
  85.7 23.2 %collective-permute-start.61 = (bf16[256,1024]{1,0:T(8,128)(2,1)S(1)}, bf16[256,1024]{1,0:T(8,128)(2,1)S(1)}, u32[]{:S(2)}, u32[]{:S(2)}) collective-permute-start(bf16[256,1024]{1,0:T(8,128)(2,1)S(1)} %collective-permute-done.53.refs_2_.refs_0_), channel_id=1, source_target_pairs={{8,12},{9,13},{10,14},{11,15},{24,28},{25,29},{26,30},{27,31}} | collective-permute-start | bytes 1572872 | tf_op jit(solution)/shard_map/ppermute | solution.py:395
  121.1 15.7 %collective-permute-start.64 = (bf16[96,1024]{1,0:T(8,128)(2,1)S(1)}, bf16[96,1024]{1,0:T(8,128)(2,1)S(1)}, u32[]{:S(2)}, u32[]{:S(2)}) collective-permute-start(bf16[96,1024]{1,0:T(8,128)(2,1)S(1)} %get-tuple-element.169), channel_id=1, source_target_pairs={{0,2},{1,3},{2,0},{3,1},{4,6},{5,7},{6,4},{7,5},{8,10},{9,11},{10,... | collective-permute-start | bytes 589832 | tf_op jit(solution)/shard_map/ppermute | solution.py:395
  153.5 16.9 %collective-permute-start.23 = (bf16[96,1024]{1,0:T(8,128)(2,1)S(1)}, bf16[96,1024]{1,0:T(8,128)(2,1)S(1)}, u32[]{:S(2)}, u32[]{:S(2)}) collective-permute-start(bf16[96,1024]{1,0:T(8,128)(2,1)S(1)} %get-tuple-element.127), channel_id=1, source_target_pairs={{0,2},{1,3},{2,0},{3,1},{4,6},{5,7},{6,4},{7,5},{8,10},{9,11},{10,... | collective-permute-start | bytes 589832 | tf_op jit(solution)/shard_map/ppermute | solution.py:395
  157.6 17.0 %collective-permute-start.56 = (bf16[96,1024]{1,0:T(8,128)(2,1)S(1)}, bf16[96,1024]{1,0:T(8,128)(2,1)S(1)}, u32[]{:S(2)}, u32[]{:S(2)}) collective-permute-start(bf16[96,1024]{1,0:T(8,128)(2,1)S(1)} %get-tuple-element.160), channel_id=1, source_target_pairs={{0,2},{1,3},{2,0},{3,1},{4,6},{5,7},{6,4},{7,5},{8,10},{9,11},{10,... | collective-permute-start | bytes 589832 | tf_op jit(solution)/shard_map/ppermute | solution.py:395
  164.7 26.7 %collective-permute-start.36 = (bf16[256,1024]{1,0:T(8,128)(2,1)S(1)}, bf16[256,1024]{1,0:T(8,128)(2,1)S(1)}, u32[]{:S(2)}, u32[]{:S(2)}) collective-permute-start(bf16[256,1024]{1,0:T(8,128)(2,1)S(1)} %combine_rows.12), channel_id=1, source_target_pairs={{12,8},{13,9},{14,10},{15,11},{28,24},{29,25},{30,26},{31,27}} | collective-permute-start | bytes 1572872 | tf_op jit(solution)/shard_map/ppermute | solution.py:395
  170.4 17.9 %collective-permute-start.24 = (bf16[96,1024]{1,0:T(8,128)(2,1)S(1)}, bf16[96,1024]{1,0:T(8,128)(2,1)S(1)}, u32[]{:S(2)}, u32[]{:S(2)}) collective-permute-start(bf16[96,1024]{1,0:T(8,128)(2,1)S(1)} %get-tuple-element.128), channel_id=1, source_target_pairs={{0,3},{1,2},{2,1},{3,0},{4,7},{5,6},{6,5},{7,4},{8,11},{9,10},{10,... | collective-permute-start | bytes 589832 | tf_op jit(solution)/shard_map/ppermute | solution.py:395
  170.4 23.0 %collective-permute-start.33 = (bf16[256,1024]{1,0:T(8,128)(2,1)S(1)}, bf16[256,1024]{1,0:T(8,128)(2,1)S(1)}, u32[]{:S(2)}, u32[]{:S(2)}) collective-permute-start(bf16[256,1024]{1,0:T(8,128)(2,1)S(1)} %combine_rows.12), channel_id=1, source_target_pairs={{0,4},{1,5},{2,6},{3,7},{16,20},{17,21},{18,22},{19,23}} | collective-permute-start | bytes 1572872 | tf_op jit(solution)/shard_map/ppermute | solution.py:395
  174.6 27.0 %collective-permute-start.72 = (bf16[256,1024]{1,0:T(8,128)(2,1)S(1)}, bf16[256,1024]{1,0:T(8,128)(2,1)S(1)}, u32[]{:S(2)}, u32[]{:S(2)}) collective-permute-start(bf16[256,1024]{1,0:T(8,128)(2,1)S(1)} %combine_rows.18), channel_id=1, source_target_pairs={{12,8},{13,9},{14,10},{15,11},{28,24},{29,25},{30,26},{31,27}} | collective-permute-start | bytes 1572872 | tf_op jit(solution)/shard_map/ppermute | solution.py:395
  177.4 25.2 %collective-permute-start.69 = (bf16[256,1024]{1,0:T(8,128)(2,1)S(1)}, bf16[256,1024]{1,0:T(8,128)(2,1)S(1)}, u32[]{:S(2)}, u32[]{:S(2)}) collective-permute-start(bf16[256,1024]{1,0:T(8,128)(2,1)S(1)} %combine_rows.18), channel_id=1, source_target_pairs={{0,4},{1,5},{2,6},{3,7},{16,20},{17,21},{18,22},{19,23}} | collective-permute-start | bytes 1572872 | tf_op jit(solution)/shard_map/ppermute | solution.py:395
  193.4 29.8 %collective-permute-start.37 = (bf16[256,1024]{1,0:T(8,128)(2,1)S(1)}, bf16[256,1024]{1,0:T(8,128)(2,1)S(1)}, u32[]{:S(2)}, u32[]{:S(2)}) collective-permute-start(bf16[256,1024]{1,0:T(8,128)(2,1)S(1)} %combine_rows.15), channel_id=1, source_target_pairs={{8,4},{9,5},{10,6},{11,7},{12,8},{13,9},{14,10},{15,11},{24,20},{2... | collective-permute-start | bytes 1572872 | tf_op jit(solution)/shard_map/ppermute | solution.py:395
  198.1 25.2 %collective-permute-start.34 = (bf16[256,1024]{1,0:T(8,128)(2,1)S(1)}, bf16[256,1024]{1,0:T(8,128)(2,1)S(1)}, u32[]{:S(2)}, u32[]{:S(2)}) collective-permute-start(bf16[256,1024]{1,0:T(8,128)(2,1)S(1)} %combine_rows.13), channel_id=1, source_target_pairs={{0,4},{1,5},{2,6},{3,7},{4,8},{5,9},{6,10},{7,11},{16,20},{17,21},... | collective-permute-start | bytes 1572872 | tf_op jit(solution)/shard_map/ppermute | solution.py:395
  205.6 16.4 %collective-permute-start.40 = (bf16[96,1024]{1,0:T(8,128)(2,1)S(1)}, bf16[96,1024]{1,0:T(8,128)(2,1)S(1)}, u32[]{:S(2)}, u32[]{:S(2)}) collective-permute-start(bf16[96,1024]{1,0:T(8,128)(2,1)S(1)} %copy-done.17), channel_id=1, source_target_pairs={{0,2},{1,3},{2,0},{3,1},{4,6},{5,7},{6,4},{7,5},{8,10},{9,11},{10,... | collective-permute-start | bytes 589832 | tf_op jit(solution)/shard_map/ppermute | solution.py:395
  209.3 37.4 %collective-permute-start.73 = (bf16[256,1024]{1,0:T(8,128)(2,1)S(1)}, bf16[256,1024]{1,0:T(8,128)(2,1)S(1)}, u32[]{:S(2)}, u32[]{:S(2)}) collective-permute-start(bf16[256,1024]{1,0:T(8,128)(2,1)S(1)} %combine_rows.21), channel_id=1, source_target_pairs={{8,4},{9,5},{10,6},{11,7},{12,8},{13,9},{14,10},{15,11},{24,20},{2... | collective-permute-start | bytes 1572872 | tf_op jit(solution)/shard_map/ppermute | solution.py:395
  212.1 35.7 %collective-permute-start.70 = (bf16[256,1024]{1,0:T(8,128)(2,1)S(1)}, bf16[256,1024]{1,0:T(8,128)(2,1)S(1)}, u32[]{:S(2)}, u32[]{:S(2)}) collective-permute-start(bf16[256,1024]{1,0:T(8,128)(2,1)S(1)} %combine_rows.19), channel_id=1, source_target_pairs={{0,4},{1,5},{2,6},{3,7},{4,8},{5,9},{6,10},{7,11},{16,20},{17,21},... | collective-permute-start | bytes 1572872 | tf_op jit(solution)/shard_map/ppermute | solution.py:395
  228.5 18.1 %collective-permute-start.52 = (bf16[96,1024]{1,0:T(8,128)(2,1)S(1)}, bf16[96,1024]{1,0:T(8,128)(2,1)S(1)}, u32[]{:S(2)}, u32[]{:S(2)}) collective-permute-start(bf16[96,1024]{1,0:T(8,128)(2,1)S(1)} %get-tuple-element.157), channel_id=1, source_target_pairs={{0,3},{1,2},{2,1},{3,0},{4,7},{5,6},{6,5},{7,4},{8,11},{9,10},{10,... | collective-permute-start | bytes 589832 | tf_op jit(solution)/shard_map/ppermute | solution.py:395
  230.5 30.1 %collective-permute-start.38 = (bf16[256,1024]{1,0:T(8,128)(2,1)S(1)}, bf16[256,1024]{1,0:T(8,128)(2,1)S(1)}, u32[]{:S(2)}, u32[]{:S(2)}) collective-permute-start(bf16[256,1024]{1,0:T(8,128)(2,1)S(1)} %combine_rows.16), channel_id=1, source_target_pairs={{4,0},{5,1},{6,2},{7,3},{8,4},{9,5},{10,6},{11,7},{12,8},{13,9},{1... | collective-permute-start | bytes 1572872 | tf_op jit(solution)/shard_map/ppermute | solution.py:395
  234.2 27.6 %collective-permute-start.35 = (bf16[256,1024]{1,0:T(8,128)(2,1)S(1)}, bf16[256,1024]{1,0:T(8,128)(2,1)S(1)}, u32[]{:S(2)}, u32[]{:S(2)}) collective-permute-start(bf16[256,1024]{1,0:T(8,128)(2,1)S(1)} %combine_rows.14), channel_id=1, source_target_pairs={{0,4},{1,5},{2,6},{3,7},{4,8},{5,9},{6,10},{7,11},{8,12},{9,13},{1... | collective-permute-start | bytes 1572872 | tf_op jit(solution)/shard_map/ppermute | solution.py:395
  258.6 33.4 %collective-permute-start.42 = (bf16[96,1024]{1,0:T(8,128)(2,1)S(1)}, bf16[96,1024]{1,0:T(8,128)(2,1)S(1)}, u32[]{:S(2)}, u32[]{:S(2)}) collective-permute-start(bf16[96,1024]{1,0:T(8,128)(2,1)S(1)} %get-tuple-element.146), channel_id=1, source_target_pairs={{0,1},{1,0},{2,3},{3,2},{4,5},{5,4},{6,7},{7,6},{8,9},{9,8},{10,11... | collective-permute-start | bytes 589832 | tf_op jit(solution)/shard_map/ppermute | solution.py:395
  259.1 33.0 %collective-permute-start.43 = (bf16[96,1024]{1,0:T(8,128)(2,1)S(1)}, bf16[96,1024]{1,0:T(8,128)(2,1)S(1)}, u32[]{:S(2)}, u32[]{:S(2)}) collective-permute-start(bf16[96,1024]{1,0:T(8,128)(2,1)S(1)} %get-tuple-element.147), channel_id=1, source_target_pairs={{0,2},{1,3},{2,0},{3,1},{4,6},{5,7},{6,4},{7,5},{8,10},{9,11},{10,... | collective-permute-start | bytes 589832 | tf_op jit(solution)/shard_map/ppermute | solution.py:395
  260.1 32.0 %collective-permute-start.44 = (bf16[96,1024]{1,0:T(8,128)(2,1)S(1)}, bf16[96,1024]{1,0:T(8,128)(2,1)S(1)}, u32[]{:S(2)}, u32[]{:S(2)}) collective-permute-start(bf16[96,1024]{1,0:T(8,128)(2,1)S(1)} %get-tuple-element.148), channel_id=1, source_target_pairs={{0,3},{1,2},{2,1},{3,0},{4,7},{5,6},{6,5},{7,4},{8,11},{9,10},{10,... | collective-permute-start | bytes 589832 | tf_op jit(solution)/shard_map/ppermute | solution.py:395
  260.6 31.5 %collective-permute-start.74 = (bf16[256,1024]{1,0:T(8,128)(2,1)S(1)}, bf16[256,1024]{1,0:T(8,128)(2,1)S(1)}, u32[]{:S(2)}, u32[]{:S(2)}) collective-permute-start(bf16[256,1024]{1,0:T(8,128)(2,1)S(1)} %combine_rows.22), channel_id=1, source_target_pairs={{4,0},{5,1},{6,2},{7,3},{8,4},{9,5},{10,6},{11,7},{12,8},{13,9},{1... | collective-permute-start | bytes 1572872 | tf_op jit(solution)/shard_map/ppermute | solution.py:395
  261.9 30.2 %collective-permute-start.71 = (bf16[256,1024]{1,0:T(8,128)(2,1)S(1)}, bf16[256,1024]{1,0:T(8,128)(2,1)S(1)}, u32[]{:S(2)}, u32[]{:S(2)}) collective-permute-start(bf16[256,1024]{1,0:T(8,128)(2,1)S(1)} %combine_rows.20), channel_id=1, source_target_pairs={{0,4},{1,5},{2,6},{3,7},{4,8},{5,9},{6,10},{7,11},{8,12},{9,13},{1... | collective-permute-start | bytes 1572872 | tf_op jit(solution)/shard_map/ppermute | solution.py:395
  (71 other events, 650.0 us)

commit v2 on v0

v2 whole, which is shorter than its diff:
```python
import functools

import jax
import jax.numpy as jnp
from jax import lax
from jax.experimental import pallas as pl
from jax.experimental.pallas import tpu as pltpu
from jax.sharding import PartitionSpec as P

AXIS = "expert"
PLANE = 4
PAIR = 2
INV_ROOT_TWO = 0.7071067811865476
INV_ROOT_TAU = 0.3989422804014327
PEAK = 5.75e9
BF16 = jnp.bfloat16
F32 = jnp.float32
SMEM = pl.BlockSpec(memory_space=pltpu.SMEM)
VMEM = pl.BlockSpec(memory_space=pltpu.VMEM)


def params(mib):
    return pltpu.CompilerParams(vmem_limit_bytes=mib * 1024 * 1024)


def dot(a, b, dims):
    return lax.dot_general(a, b, (dims, ((), ())), preferred_element_type=F32)


META = 16


def call(
    kernel, order, operands, specs, out_shape, out_specs, name, mib=24, grid=(1,), scratch=(), cost=1.5
):
    result = pl.pallas_call(
        kernel,
        grid=grid,
        out_shape=out_shape,
        in_specs=specs,
        out_specs=out_specs,
        scratch_shapes=list(scratch),
        compiler_params=params(mib),
        cost_estimate=pl.CostEstimate(
            flops=int(cost * PEAK), bytes_accessed=1000, transcendentals=0
        ),
        name=name,
    )(*order.behind(operands))
    order.last = result[0] if isinstance(result, (tuple, list)) else result
    return result


class Order:
    def __init__(self):
        self.last = None

    def behind(self, operands):
        if self.last is None:
            return list(operands)
        return list(lax.optimization_barrier((tuple(operands), self.last))[0])


def whole(shape):
    zeros = (0,) * len(shape)
    return pl.BlockSpec(shape, lambda *i: zeros)


def stack_kernel(tokens_ref, ids_ref, gates_ref, out_ref):
    tokens, _ = tokens_ref.shape
    out_ref[:tokens, :] = tokens_ref[...]
    eye = lax.broadcasted_iota(jnp.int32, (tokens, tokens), 0) == lax.broadcasted_iota(
        jnp.int32, (tokens, tokens), 1
    )

    def as_row(column):
        return jnp.sum(jnp.where(eye, column, 0.0), axis=0, keepdims=True)

    ids, gates = ids_ref[...].astype(F32), gates_ref[...]
    rows = [as_row(ids[:, k : k + 1]) for k in range(2)]
    for k in range(2):
        rest = as_row(gates[:, k : k + 1])
        for _ in range(3):
            part = rest.astype(BF16).astype(F32)
            rows.append(part)
            rest = rest - part
    rows += rows
    out_ref[tokens:, :] = jnp.zeros((META, out_ref.shape[1]), BF16)
    out_ref[tokens:, :tokens] = jnp.concatenate(rows, axis=0).astype(BF16)


def stack_block(order, tokens, expert_ids, gate_weights):
    count, width = tokens.shape
    return call(
        stack_kernel,
        order,
        (tokens, expert_ids, gate_weights),
        [whole(tokens.shape), whole(expert_ids.shape), whole(gate_weights.shape)],
        jax.ShapeDtypeStruct((count + META, width), BF16),
        whole((count + META, width)),
        "stack_block",
    )


def route_rows(experts, meta, cap, at, pick_ref, put_ref, row_gate_ref, token_gate_ref):
    tokens = meta.shape[1]
    upper = (
        lax.broadcasted_iota(jnp.int32, (tokens, tokens), 0)
        < lax.broadcasted_iota(jnp.int32, (tokens, tokens), 1)
    ).astype(BF16)
    eye = lax.broadcasted_iota(jnp.int32, (tokens, tokens), 0) == lax.broadcasted_iota(
        jnp.int32, (tokens, tokens), 1
    )
    down = lax.broadcasted_iota(jnp.int32, (cap, tokens), 0).astype(F32)
    along = lax.broadcasted_iota(jnp.int32, (tokens, cap), 1).astype(F32)
    lane = lax.broadcasted_iota(jnp.int32, (tokens, 128), 1)
    first, second = meta[0:1], meta[1:2]
    gate_one = meta[2:3] + meta[3:4] + meta[4:5]
    gate_two = meta[5:6] + meta[6:7] + meta[7:8]
    marks, gates = [], []
    for expert in experts:
        is_one = (first == expert).astype(F32)
        is_two = (second == expert).astype(F32)
        marks.append(is_one + is_two)
        gates.append(is_one * gate_one + is_two * gate_two)
    marks = jnp.concatenate(marks * 4, axis=0)
    rank = dot(marks.astype(BF16), upper, ((1,), (0,)))
    rank = jnp.where(marks > 0.0, rank, -1.0)
    token_gate = jnp.zeros((tokens, 128), F32)
    picks = []
    for k in range(PAIR):
        row = rank[k : k + 1]
        hit = down == row
        picks.append(hit.astype(F32).astype(BF16))
        pick_ref[k, at] = picks[-1]
        gate = jnp.sum(jnp.where(hit, gates[k], 0.0), axis=1, keepdims=True)
        row_gate_ref[k, at] = jnp.broadcast_to(gate, (cap, 128))
        column = jnp.sum(jnp.where(eye, row, 0.0), axis=1, keepdims=True)
        put_ref[k, at] = (along == column).astype(F32).astype(BF16)
        gate = jnp.sum(jnp.where(eye, gates[k], 0.0), axis=1, keepdims=True)
        token_gate = jnp.where(lane == k, gate, token_gate)
    token_gate_ref[at] = token_gate
    return picks


def select_kernel(scaled, cap, me_ref, *refs):
    blocks, refs = refs[:PAIR], refs[PAIR:]
    if scaled:
        (pick_ref, row_gate_ref), refs = refs[:2], refs[2:]
    outs, routes = refs[:PAIR], refs[PAIR:]
    me = me_ref[0]
    experts = [me.astype(F32), (me ^ 2).astype(F32)]
    for at, ref in enumerate(blocks):
        if scaled:
            block = ref[...]
            picks = [pick_ref[k, at] for k in range(PAIR)]
        else:
            tokens = ref.shape[0] - META
            block = ref[:tokens, :]
            meta = ref[tokens:, :tokens].astype(F32)
            picks = route_rows(experts, meta, cap, at, *routes)
        for k in range(PAIR):
            rows = dot(picks[k], block, ((1,), (0,)))
            if scaled:
                rows = rows * row_gate_ref[k, at][:, :1]
            outs[k][at * cap : (at + 1) * cap, :] = rows.astype(BF16)


def select(order, me, blocks, cap, routes=None):
    width = blocks[0].shape[1]
    tokens = blocks[0].shape[0] - (META if routes is None else 0)
    shapes = [jax.ShapeDtypeStruct((PAIR * cap, width), BF16)] * PAIR
    operands = [me, *blocks]
    specs = [SMEM] + [whole(b.shape) for b in blocks]
    if routes is None:
        shapes += [
            jax.ShapeDtypeStruct((PAIR, PAIR, cap, tokens), BF16),
            jax.ShapeDtypeStruct((PAIR, PAIR, tokens, cap), BF16),
            jax.ShapeDtypeStruct((PAIR, PAIR, cap, 128), F32),
            jax.ShapeDtypeStruct((PAIR, tokens, 128), F32),
        ]
    else:
        operands += [routes[0], routes[2]]
        specs += [whole(routes[0].shape), whole(routes[2].shape)]
    result = call(
        functools.partial(select_kernel, routes is not None, cap),
        order,
        operands,
        specs,
        tuple(shapes),
        tuple(whole(s.shape) for s in shapes),
        "select_rows",
    )
    return result[:PAIR], result[PAIR:]


def combine_kernel(at, gated, *refs):
    rows, (put_ref, gate_ref), more, out_ref = refs[:PAIR], refs[PAIR : PAIR + 2], refs[PAIR + 2 : -1], refs[-1]
    cap = rows[0].shape[0] // PAIR
    total = None
    for k in range(PAIR):
        part = dot(put_ref[k, at], rows[k][at * cap : (at + 1) * cap, :], ((1,), (0,)))
        if gated:
            part = part * gate_ref[at][:, k : k + 1]
        total = part if total is None else total + part
    for ref in more:
        total = total + ref[...].astype(F32)
    out_ref[...] = total.astype(BF16)


def combine(order, rows, routes, at, gated, extras=()):
    operands = [*rows, routes[1], routes[3], *extras]
    shape = (routes[3].shape[1], rows[0].shape[1])
    return call(
        functools.partial(combine_kernel, at, gated),
        order,
        operands,
        [whole(o.shape) for o in operands],
        jax.ShapeDtypeStruct(shape, BF16),
        whole(shape),
        "combine_rows",
    )


def gelu_parts(pre_act):
    normal_cdf = 0.5 * (1.0 + lax.erf(pre_act * INV_ROOT_TWO))
    normal_pdf = jnp.exp(-0.5 * pre_act * pre_act) * INV_ROOT_TAU
    return (pre_act * normal_cdf, normal_cdf + pre_act * normal_pdf)


def expert_kernel(first, steps, mine_ref, side_ref, win_ref, wout_ref, *refs):
    step = pl.program_id(0)
    if first:
        my_out, side_out, rows_ref, act_ref, slope_ref, total = refs
    else:
        slope_ref, my_out, side_out, rows_ref, pre_ref, total = refs
    size = mine_ref.shape[0]

    @pl.when(step == 0)
    def _():
        rows_ref[:size, :] = mine_ref[...]
        rows_ref[size:, :] = side_ref[...]
        total[...] = jnp.zeros_like(total)

    if first:
        act, slope = gelu_parts(dot(rows_ref[...], win_ref[0], ((1,), (0,))))
        act = act.astype(BF16)
        act_ref[...] = act
        slope_ref[...] = slope
        total[...] += dot(act, wout_ref[0], ((1,), (0,)))
    else:
        act_grad = dot(rows_ref[...], wout_ref[0], ((1,), (1,)))
        pre_grad = (act_grad * slope_ref[...]).astype(BF16)
        pre_ref[...] = pre_grad
        total[...] += dot(pre_grad, win_ref[0], ((1,), (1,)))

    @pl.when(step == steps - 1)
    def _():
        my_out[...] = total[:size, :].astype(BF16)
        side_out[...] = total[size:, :].astype(BF16)


def expert_pass(order, mine, side, w_in, w_out, slope=None, tile=512):
    first = slope is None
    width, hidden = w_in.shape[1:]
    size = mine.shape[0]
    steps = hidden // tile
    part = pl.BlockSpec((2 * size, tile), lambda f: (0, f))
    shapes = [jax.ShapeDtypeStruct((size, width), BF16)] * 2
    shapes += [jax.ShapeDtypeStruct((2 * size, width), BF16)]
    shapes += [jax.ShapeDtypeStruct((2 * size, hidden), BF16)]
    shapes += [jax.ShapeDtypeStruct((2 * size, hidden), F32)] if first else []
    result = call(
        functools.partial(expert_kernel, first, steps),
        order,
        [mine, side, w_in, w_out] + ([] if first else [slope]),
        [whole(mine.shape), whole(side.shape)]
        + [
            pl.BlockSpec((1, width, tile), lambda f: (0, 0, f)),
            pl.BlockSpec((1, tile, width), lambda f: (0, f, 0)),
        ]
        + ([] if first else [part]),
        tuple(shapes),
        tuple(whole(k.shape) for k in shapes[:3]) + (part,) * (len(shapes) - 3),
        "expert_forward" if first else "expert_backward",
        mib=32,
        grid=(steps,),
        scratch=[pltpu.VMEM((2 * size, width), F32)],
        cost=5.0,
    )
    return result[:2], result[2:]


def weight_kernel(count, *refs):
    total = None
    for a, b in zip(refs[:count], refs[count : 2 * count]):
        part = dot(a[...], b[...], ((0,), (0,)))
        total = part if total is None else total + part
    refs[-1][0] = total.astype(BF16)


def weight_grad(order, lefts, rights, tile, by_left, name):
    m, n = lefts[0].shape[1], rights[0].shape[1]

    def spec(array, tiled):
        rows, columns = array.shape
        if tiled:
            return pl.BlockSpec((rows, tile), lambda f: (0, f))
        return pl.BlockSpec((rows, columns), lambda f: (0, 0))

    return call(
        functools.partial(weight_kernel, len(lefts)),
        order,
        [*lefts, *rights],
        [spec(a, by_left) for a in lefts] + [spec(b, not by_left) for b in rights],
        jax.ShapeDtypeStruct((1, m, n), BF16),
        pl.BlockSpec((1, tile, n), lambda f: (0, f, 0))
        if by_left
        else pl.BlockSpec((1, m, tile), lambda f: (0, 0, f)),
        name,
        mib=44,
        cost=10.0,
        grid=((m if by_left else n) // tile,),
    )


def permute(value, pairs):
    return lax.ppermute(value, AXIS, pairs)


def ring_pairs(length, step):
    ring = [0] + list(range(1, length, 2)) + list(range(2, length, 2))[::-1]
    return [
        (ring[k] * PLANE + lo, ring[(k + step) % length] * PLANE + lo)
        for k in range(length)
        for lo in range(PLANE)
    ]


def local(tokens, expert_ids, gate_weights, out_grad, w_in, w_out):
    count = lax.axis_size(AXIS)
    length = count // PLANE
    tok_count, _ = tokens.shape
    cap = 6 * tok_count // count
    me = jnp.stack([lax.axis_index(AXIS)]).astype(jnp.int32)
    order = Order()
    onward = ring_pairs(length, 1)
    core, side = ([(i, i ^ p) for i in range(count)] for p in (1, 2))
    routes, slopes = {}, {}

    def send(value, pairs, *after):
        return permute(lax.optimization_barrier((value, order.last, after))[0], pairs)

    class Tensor:
        def __init__(self, block, first):
            self.first, self.block = first, {0: block}
            self.other, self.mine, self.away = {}, {}, {}
            self.outs, self.rows, self.kept, self.crossed = {}, {}, {}, {}
            self.moving = None

        def step(self, t):
            if t < length:
                self.block[t] = send(self.block[t - 1], onward)

        def swap(self, t):
            self.other[t] = send(self.block[t], core)

        def pick(self, t):
            found = None if self.first else routes[t]
            rows, new = select(order, me, [self.block[t], self.other[t]], cap, found)
            if self.first:
                routes[t] = new
            self.mine[t], self.away[t] = rows[0], send(rows[1], side)

        def serve(self, t):
            slope = None if self.first else slopes[t]
            self.outs[t], kept = expert_pass(order, self.mine[t], self.away[t], w_in, w_out, slope)
            self.kept[t] = kept[:2]
            if self.first:
                slopes[t] = kept[2]

        def back(self, t):
            self.rows[t] = [self.outs[t][0], send(self.outs[t][1], side)]

        def cross(self, t):
            self.crossed[t] = send(combine(order, self.rows[t], routes[t], 1, self.first), core)

        def fold(self, t):
            extras = [self.crossed[t]] + ([] if self.moving is None else [self.moving])
            sums = combine(order, self.rows[t], routes[t], 0, self.first, extras)
            self.moving = send(sums, onward) if t else sums

    x = Tensor(stack_block(order, tokens, expert_ids, gate_weights), True)
    grad = Tensor(out_grad, False)
    both = (x, grad)
    for tensor in both:
        tensor.step(1)
        tensor.swap(0)
    for tensor in both:
        tensor.pick(0)
    for t in range(1, length):
        for tensor in both:
            tensor.step(t + 1)
            tensor.swap(t)
            tensor.serve(t - 1)
            if t > 1:
                tensor.back(t - 1)
            if t > 2:
                tensor.cross(t - 2)
            tensor.pick(t)
            if t > 2:
                tensor.fold(t - 2)
    top = length - 1
    x.cross(top - 1)
    x.serve(top)
    x.back(top)
    x.fold(top - 1)
    grad.cross(top - 1)
    grad.serve(top)
    grad.back(top)
    grad.fold(top - 1)
    x.back(0)
    grad.back(0)
    every = range(length)
    w_out_grad = weight_grad(
        order, [x.kept[t][1] for t in every], [grad.kept[t][0] for t in every], 512, True, "weights_out"
    )
    x.cross(top)
    grad.cross(top)
    x.fold(top)
    grad.fold(top)
    w_in_grad = weight_grad(
        order, [x.kept[t][0] for t in every], [grad.kept[t][1] for t in every], 512, False, "weights_in"
    )
    for tensor in both:
        tensor.cross(0)
    for tensor in both:
        tensor.fold(0)
    return x.moving, grad.moving, w_in_grad, w_out_grad


def solution(mesh):
    rows, wide = P(("groups", AXIS), None), P(("groups", AXIS), None, None)
    weights = P(AXIS, None, None)
    return jax.shard_map(
        local,
        mesh=mesh,
        in_specs=(rows, rows, rows, rows, weights, weights),
        out_specs=(rows, rows, wide, wide),
        check_vma=False,
    )
```

time: 656 us -> 220 us (0.34)
  the two profiles are of different devices: /device:TPU:15 before, /device:TPU:0 now
where the time goes in v2:
time: 220 us
  waiting for transfers between devices  87.5 us (40%)
  Pallas kernels  80.2 us (36%)
  starting transfers between devices  41.7 us (19%)
  local copies, waits for them, and re-layouts  8.83 us (4%)
    ppermute x44, waiting for transfers between devices, permute(): return lax.ppermute(value, AXIS, pairs)  87.5 us
    pallas_call x35, Pallas kernels, call(): pl.pallas_call(kernel, grid=grid, out_shape=out_shape, in_specs=specs, ou...  80.2 us
    ppermute x44, starting transfers between devices, permute(): return lax.ppermute(value, AXIS, pairs)  41.7 us
    unnamed x74, local copies, waits for them, and re-layouts  8.83 us
  transfers between devices with their start and end apart: 44, of which 12 were waited for; matrix products, arithmetic and copies ran while one was open for 0% of the time, Pallas kernels for 36%

profile of v2, /device:TPU:0, one launch (start us, length us, event | category | flops | bytes accessed | tf_op | source)
XLA Modules:
  0.0 219.7 jit_solution(12498142218117633567)
XLA Ops:
  4.4 3.0 %collective-permute-start.3 = (bf16[256,1024]{1,0:T(8,128)(2,1)S(1)}, bf16[256,1024]{1,0:T(8,128)(2,1)S(1)}, u32[]{:S(2)}, u32[]{:S(2)}) collective-permute-start(bf16[256,1024]{1,0:T(8,128)(2,1)S(1)} %copy-done.3), channel_id=1, source_target_pairs={{0,4},{1,5},{2,6},{3,7},{4,12},{5,13},{6,14},{7,15},{12,8},{13,9},... | collective-permute-start | bytes 1572872 | tf_op jit(solution)/shard_map/ppermute | solution.py:327
  7.4 2.6 %collective-permute-start.4 = (bf16[272,1024]{1,0:T(8,128)(2,1)S(1)}, bf16[272,1024]{1,0:T(8,128)(2,1)S(1)}, u32[]{:S(2)}, u32[]{:S(2)}) collective-permute-start(bf16[272,1024]{1,0:T(8,128)(2,1)S(1)} %stack_block.1.refs_0_), channel_id=1, source_target_pairs={{0,4},{1,5},{2,6},{3,7},{4,12},{5,13},{6,14},{7,15},{12,8},{13,9},... | collective-permute-start | bytes 1671176 | tf_op jit(solution)/shard_map/ppermute | solution.py:327
  10.8 1.6 collective-permute-start.1
  12.9 19.4 %collective-permute-done.4.refs_0_ = bf16[272,1024]{1,0:T(8,128)(2,1)S(1)} collective-permute-done((bf16[272,1024]{1,0:T(8,128)(2,1)S(1)}, bf16[272,1024]{1,0:T(8,128)(2,1)S(1)}, u32[]{:S(2)}, u32[]{:S(2)}) %collective-permute-start.4) | collective-permute-done | bytes 557088 | tf_op jit(solution)/shard_map/ppermute | solution.py:327
  33.1 1.5 collective-permute-start.9
  34.6 5.9 %expert_forward.4 = (bf16[192,1024]{1,0:T(8,128)(2,1)S(1)}, bf16[192,1024]{1,0:T(8,128)(2,1)S(1)}, bf16[384,1024]{1,0:T(8,128)(2,1)S(1)}, bf16[384,2048]{1,0:T(8,128)(2,1)S(1)}, f32[384,2048]{1,0:T(8,128)S(1)}) custom-call(bf16[192,1024]{1,0:T(8,128)(2,1)S(1)} %get-tuple-element.288.mine_ref, bf16[192,1024]{1,0:T(8,128)(2,1)S(1)} %collective-permute-done.1.side_ref, ...), custom_call_target="tpu_custom_call" | custom-call | flops 28750000128 | bytes 1000 | tf_op jit(solution)/shard_map/expert_forward/pallas_call | solution.py:36
  42.2 3.4 %collective-permute-start.6 = (bf16[256,1024]{1,0:T(8,128)(2,1)S(1)}, bf16[256,1024]{1,0:T(8,128)(2,1)S(1)}, u32[]{:S(2)}, u32[]{:S(2)}) collective-permute-start(bf16[256,1024]{1,0:T(8,128)(2,1)S(1)} %collective-permute-done.3.refs_0_), channel_id=1, source_target_pairs={{0,4},{1,5},{2,6},{3,7},{4,12},{5,13},{6,14},{7,15},{12,8},{13,9},... | collective-permute-start | bytes 1572872 | tf_op jit(solution)/shard_map/ppermute | solution.py:327
  46.1 5.2 %expert_backward.4 = (bf16[192,1024]{1,0:T(8,128)(2,1)S(1)}, bf16[192,1024]{1,0:T(8,128)(2,1)S(1)}, bf16[384,1024]{1,0:T(8,128)(2,1)S(1)}, bf16[384,2048]{1,0:T(8,128)(2,1)S(1)}) custom-call(bf16[192,1024]{1,0:T(8,128)(2,1)S(1)} %get-tuple-element.305.mine_ref, bf16[192,1024]{1,0:T(8,128)(2,1)S(1)} %collective-permute-done.9.side_ref, ...), custom_call_target="tpu_custom_call" | custom-call | flops 28750000128 | bytes 1000 | tf_op jit(solution)/shard_map/expert_backward/pallas_call | solution.py:36
  52.7 3.4 %collective-permute-start.18 = (bf16[272,1024]{1,0:T(8,128)(2,1)S(1)}, bf16[272,1024]{1,0:T(8,128)(2,1)S(1)}, u32[]{:S(2)}, u32[]{:S(2)}) collective-permute-start(bf16[272,1024]{1,0:T(8,128)(2,1)S(1)} %collective-permute-done.7.refs_0_), channel_id=1, source_target_pairs={{0,4},{1,5},{2,6},{3,7},{4,12},{5,13},{6,14},{7,15},{12,8},{13,9},... | collective-permute-start | bytes 1671176 | tf_op jit(solution)/shard_map/ppermute | solution.py:327
  57.1 5.9 %expert_forward.5 = (bf16[192,1024]{1,0:T(8,128)(2,1)S(1)}, bf16[192,1024]{1,0:T(8,128)(2,1)S(1)}, bf16[384,1024]{1,0:T(8,128)(2,1)S(1)}, bf16[384,2048]{1,0:T(8,128)(2,1)S(1)}, f32[384,2048]{1,0:T(8,128)S(1)}) custom-call(bf16[192,1024]{1,0:T(8,128)(2,1)S(1)} %get-tuple-element.320.mine_ref, bf16[192,1024]{1,0:T(8,128)(2,1)S(1)} %collective-permute-done.11.side_ref, ...), custom_call_target="tpu_custom_call" | custom-call | flops 28750000128 | bytes 1000 | tf_op jit(solution)/shard_map/expert_forward/pallas_call | solution.py:36
  64.1 1.5 collective-permute-start.16
  66.5 2.4 %collective-permute-start.24 = (bf16[256,1024]{1,0:T(8,128)(2,1)S(1)}, bf16[256,1024]{1,0:T(8,128)(2,1)S(1)}, u32[]{:S(2)}, u32[]{:S(2)}) collective-permute-start(bf16[256,1024]{1,0:T(8,128)(2,1)S(1)} %collective-permute-done.6.refs_0_), channel_id=1, source_target_pairs={{0,4},{1,5},{2,6},{3,7},{4,12},{5,13},{6,14},{7,15},{12,8},{13,9},... | collective-permute-start | bytes 1572872 | tf_op jit(solution)/shard_map/ppermute | solution.py:327
  68.9 5.2 %expert_backward.5 = (bf16[192,1024]{1,0:T(8,128)(2,1)S(1)}, bf16[192,1024]{1,0:T(8,128)(2,1)S(1)}, bf16[384,1024]{1,0:T(8,128)(2,1)S(1)}, bf16[384,2048]{1,0:T(8,128)(2,1)S(1)}) custom-call(bf16[192,1024]{1,0:T(8,128)(2,1)S(1)} %get-tuple-element.335.mine_ref, bf16[192,1024]{1,0:T(8,128)(2,1)S(1)} %collective-permute-done.13.side_ref, ...), custom_call_target="tpu_custom_call" | custom-call | flops 28750000128 | bytes 1000 | tf_op jit(solution)/shard_map/expert_backward/pallas_call | solution.py:36
  74.1 1.6 collective-permute-start.22
  76.7 17.4 %collective-permute-done.15.side_ref = bf16[192,1024]{1,0:T(8,128)(2,1)S(1)} collective-permute-done((bf16[192,1024]{1,0:T(8,128)(2,1)S(1)}, bf16[192,1024]{1,0:T(8,128)(2,1)S(1)}, u32[]{:S(2)}, u32[]{:S(2)}) %collective-permute-start.15) | collective-permute-done | bytes 393248 | tf_op jit(solution)/shard_map/ppermute | solution.py:327
  94.1 1.5 collective-permute-start.14
  95.7 5.9 %expert_forward.6 = (bf16[192,1024]{1,0:T(8,128)(2,1)S(1)}, bf16[192,1024]{1,0:T(8,128)(2,1)S(1)}, bf16[384,1024]{1,0:T(8,128)(2,1)S(1)}, bf16[384,2048]{1,0:T(8,128)(2,1)S(1)}, f32[384,2048]{1,0:T(8,128)S(1)}) custom-call(bf16[192,1024]{1,0:T(8,128)(2,1)S(1)} %get-tuple-element.351.mine_ref, bf16[192,1024]{1,0:T(8,128)(2,1)S(1)} %collective-permute-done.15.side_ref, ...), custom_call_target="tpu_custom_call" | custom-call | flops 28750000128 | bytes 1000 | tf_op jit(solution)/shard_map/expert_forward/pallas_call | solution.py:36
  105.5 5.2 %expert_backward.6 = (bf16[192,1024]{1,0:T(8,128)(2,1)S(1)}, bf16[192,1024]{1,0:T(8,128)(2,1)S(1)}, bf16[384,1024]{1,0:T(8,128)(2,1)S(1)}, bf16[384,2048]{1,0:T(8,128)(2,1)S(1)}) custom-call(bf16[192,1024]{1,0:T(8,128)(2,1)S(1)} %get-tuple-element.376.mine_ref, bf16[192,1024]{1,0:T(8,128)(2,1)S(1)} %collective-permute-done.14.side_ref, ...), custom_call_target="tpu_custom_call" | custom-call | flops 28750000128 | bytes 1000 | tf_op jit(solution)/shard_map/expert_backward/pallas_call | solution.py:36
  110.8 2.0 collective-permute-start.20
  116.0 2.0 collective-permute-start.31
  118.4 12.8 %collective-permute-done.28.side_ref = bf16[192,1024]{1,0:T(8,128)(2,1)S(1)} collective-permute-done((bf16[192,1024]{1,0:T(8,128)(2,1)S(1)}, bf16[192,1024]{1,0:T(8,128)(2,1)S(1)}, u32[]{:S(2)}, u32[]{:S(2)}) %collective-permute-start.28) | collective-permute-done | bytes 393248 | tf_op jit(solution)/shard_map/ppermute | solution.py:327
  131.3 5.9 %expert_forward.7 = (bf16[192,1024]{1,0:T(8,128)(2,1)S(1)}, bf16[192,1024]{1,0:T(8,128)(2,1)S(1)}, bf16[384,1024]{1,0:T(8,128)(2,1)S(1)}, bf16[384,2048]{1,0:T(8,128)(2,1)S(1)}, f32[384,2048]{1,0:T(8,128)S(1)}) custom-call(bf16[192,1024]{1,0:T(8,128)(2,1)S(1)} %get-tuple-element.417.mine_ref, bf16[192,1024]{1,0:T(8,128)(2,1)S(1)} %collective-permute-done.28.side_ref, ...), custom_call_target="tpu_custom_call" | custom-call | flops 28750000128 | bytes 1000 | tf_op jit(solution)/shard_map/expert_forward/pallas_call | solution.py:36
  137.2 2.0 collective-permute-start.34
  140.6 5.2 %expert_backward.7 = (bf16[192,1024]{1,0:T(8,128)(2,1)S(1)}, bf16[192,1024]{1,0:T(8,128)(2,1)S(1)}, bf16[384,1024]{1,0:T(8,128)(2,1)S(1)}, bf16[384,2048]{1,0:T(8,128)(2,1)S(1)}) custom-call(bf16[192,1024]{1,0:T(8,128)(2,1)S(1)} %get-tuple-element.437.mine_ref, bf16[192,1024]{1,0:T(8,128)(2,1)S(1)} %collective-permute-done.31.side_ref, ...), custom_call_target="tpu_custom_call" | custom-call | flops 28750000128 | bytes 1000 | tf_op jit(solution)/shard_map/expert_backward/pallas_call | solution.py:36
  150.6 10.9 %weights_out.1 = bf16[1,2048,1024]{2,1,0:T(8,128)(2,1)} custom-call(bf16[384,2048]{1,0:T(8,128)(2,1)S(1)} %copy-done.13, bf16[384,2048]{1,0:T(8,128)(2,1)S(1)} %copy-done.15, bf16[384,2048]{1,0:T(8,128)(2,1)S(1)} %copy-done.17, bf16[384,2048]{1,0:T(8,128)(2,1)S(1)} %copy-done.19, bf16[384,1024]{1,0:T(8,128)(2,1)S(1)} %copy-done.21, ...), custom_call_target="tpu_custom_call" | custom-call | flops 57500000256 | bytes 1000 | tf_op jit(solution)/shard_map/weights_out/pallas_call | solution.py:36
  166.8 13.2 %collective-permute-done.36.refs_5_ = bf16[256,1024]{1,0:T(8,128)(2,1)S(1)} collective-permute-done((bf16[256,1024]{1,0:T(8,128)(2,1)S(1)}, bf16[256,1024]{1,0:T(8,128)(2,1)S(1)}, u32[]{:S(2)}, u32[]{:S(2)}) %collective-permute-start.36) | collective-permute-done | bytes 524320 | tf_op jit(solution)/shard_map/ppermute | solution.py:327
  180.5 11.0 %weights_in.1 = bf16[1,1024,2048]{2,1,0:T(8,128)(2,1)} custom-call(bf16[384,1024]{1,0:T(8,128)(2,1)S(1)} %copy-done.29, bf16[384,1024]{1,0:T(8,128)(2,1)S(1)} %copy-done.31, bf16[384,1024]{1,0:T(8,128)(2,1)S(1)} %copy-done.33, bf16[384,1024]{1,0:T(8,128)(2,1)S(1)} %copy-done.35, bf16[384,2048]{1,0:T(8,128)(2,1)S(1)} %copy-done.7, ...), custom_call_target="tpu_custom_call" | custom-call | flops 57500000256 | bytes 1000 | tf_op jit(solution)/shard_map/weights_in/pallas_call | solution.py:36
  193.0 2.3 %collective-permute-start.43 = (bf16[256,1024]{1,0:T(8,128)(2,1)S(1)}, bf16[256,1024]{1,0:T(8,128)(2,1)S(1)}, u32[]{:S(2)}, u32[]{:S(2)}) collective-permute-start(bf16[256,1024]{1,0:T(8,128)(2,1)S(1)} %combine_rows.27), channel_id=1, source_target_pairs={{0,4},{1,5},{2,6},{3,7},{4,12},{5,13},{6,14},{7,15},{12,8},{13,9},... | collective-permute-start | bytes 1572872 | tf_op jit(solution)/shard_map/ppermute | solution.py:327
  195.2 12.4 %collective-permute-done.40.refs_5_ = bf16[256,1024]{1,0:T(8,128)(2,1)S(1)} collective-permute-done((bf16[256,1024]{1,0:T(8,128)(2,1)S(1)}, bf16[256,1024]{1,0:T(8,128)(2,1)S(1)}, u32[]{:S(2)}, u32[]{:S(2)}) %collective-permute-start.40) | collective-permute-done | bytes 524320 | tf_op jit(solution)/shard_map/ppermute | solution.py:327
  207.7 1.3 combine_rows.30
  209.0 9.4 %collective-permute-done.43.refs_5_ = bf16[256,1024]{1,0:T(8,128)(2,1)S(1)} collective-permute-done((bf16[256,1024]{1,0:T(8,128)(2,1)S(1)}, bf16[256,1024]{1,0:T(8,128)(2,1)S(1)}, u32[]{:S(2)}, u32[]{:S(2)}) %collective-permute-start.43) | collective-permute-done | bytes 524320 | tf_op jit(solution)/shard_map/ppermute | solution.py:327
  218.5 1.2 combine_rows.31
  (165 shorter events, 34.0 us)
Async XLA Ops:
  4.4 37.6 %collective-permute-start.3 = (bf16[256,1024]{1,0:T(8,128)(2,1)S(1)}, bf16[256,1024]{1,0:T(8,128)(2,1)S(1)}, u32[]{:S(2)}, u32[]{:S(2)}) collective-permute-start(bf16[256,1024]{1,0:T(8,128)(2,1)S(1)} %copy-done.3), channel_id=1, source_target_pairs={{0,4},{1,5},{2,6},{3,7},{4,12},{5,13},{6,14},{7,15},{12,8},{13,9},... | collective-permute-start | bytes 1572872 | tf_op jit(solution)/shard_map/ppermute | solution.py:327
  7.4 24.9 %collective-permute-start.4 = (bf16[272,1024]{1,0:T(8,128)(2,1)S(1)}, bf16[272,1024]{1,0:T(8,128)(2,1)S(1)}, u32[]{:S(2)}, u32[]{:S(2)}) collective-permute-start(bf16[272,1024]{1,0:T(8,128)(2,1)S(1)} %stack_block.1.refs_0_), channel_id=1, source_target_pairs={{0,4},{1,5},{2,6},{3,7},{4,12},{5,13},{6,14},{7,15},{12,8},{13,9},... | collective-permute-start | bytes 1671176 | tf_op jit(solution)/shard_map/ppermute | solution.py:327
  10.8 23.8 %collective-permute-start.1 = (bf16[192,1024]{1,0:T(8,128)(2,1)S(1)}, bf16[192,1024]{1,0:T(8,128)(2,1)S(1)}, u32[]{:S(2)}, u32[]{:S(2)}) collective-permute-start(bf16[192,1024]{1,0:T(8,128)(2,1)S(1)} %get-tuple-element.278), channel_id=1, source_target_pairs={{0,2},{1,3},{2,0},{3,1},{4,6},{5,7},{6,4},{7,5},{8,10},{9,11},{10,... | collective-permute-start | bytes 1179656 | tf_op jit(solution)/shard_map/ppermute | solution.py:327
  32.3 20.5 %collective-permute-start.7 = (bf16[272,1024]{1,0:T(8,128)(2,1)S(1)}, bf16[272,1024]{1,0:T(8,128)(2,1)S(1)}, u32[]{:S(2)}, u32[]{:S(2)}) collective-permute-start(bf16[272,1024]{1,0:T(8,128)(2,1)S(1)} %collective-permute-done.4.refs_0_), channel_id=1, source_target_pairs={{0,4},{1,5},{2,6},{3,7},{4,12},{5,13},{6,14},{7,15},{12,8},{13,9},... | collective-permute-start | bytes 1671176 | tf_op jit(solution)/shard_map/ppermute | solution.py:327
  33.1 12.5 %collective-permute-start.9 = (bf16[192,1024]{1,0:T(8,128)(2,1)S(1)}, bf16[192,1024]{1,0:T(8,128)(2,1)S(1)}, u32[]{:S(2)}, u32[]{:S(2)}) collective-permute-start(bf16[192,1024]{1,0:T(8,128)(2,1)S(1)} %get-tuple-element.303), channel_id=1, source_target_pairs={{0,2},{1,3},{2,0},{3,1},{4,6},{5,7},{6,4},{7,5},{8,10},{9,11},{10,... | collective-permute-start | bytes 1179656 | tf_op jit(solution)/shard_map/ppermute | solution.py:327
  41.9 9.4 %collective-permute-start.8 = (bf16[256,1024]{1,0:T(8,128)(2,1)S(1)}, bf16[256,1024]{1,0:T(8,128)(2,1)S(1)}, u32[]{:S(2)}, u32[]{:S(2)}) collective-permute-start(bf16[256,1024]{1,0:T(8,128)(2,1)S(1)} %collective-permute-done.3.refs_0_), channel_id=1, source_target_pairs={{0,1},{1,0},{2,3},{3,2},{4,5},{5,4},{6,7},{7,6},{8,9},{9,8},{10,11... | collective-permute-start | bytes 1572872 | tf_op jit(solution)/shard_map/ppermute | solution.py:327
  42.2 24.3 %collective-permute-start.6 = (bf16[256,1024]{1,0:T(8,128)(2,1)S(1)}, bf16[256,1024]{1,0:T(8,128)(2,1)S(1)}, u32[]{:S(2)}, u32[]{:S(2)}) collective-permute-start(bf16[256,1024]{1,0:T(8,128)(2,1)S(1)} %collective-permute-done.3.refs_0_), channel_id=1, source_target_pairs={{0,4},{1,5},{2,6},{3,7},{4,12},{5,13},{6,14},{7,15},{12,8},{13,9},... | collective-permute-start | bytes 1572872 | tf_op jit(solution)/shard_map/ppermute | solution.py:327
  45.5 11.0 %collective-permute-start.11 = (bf16[192,1024]{1,0:T(8,128)(2,1)S(1)}, bf16[192,1024]{1,0:T(8,128)(2,1)S(1)}, u32[]{:S(2)}, u32[]{:S(2)}) collective-permute-start(bf16[192,1024]{1,0:T(8,128)(2,1)S(1)} %get-tuple-element.319), channel_id=1, source_target_pairs={{0,2},{1,3},{2,0},{3,1},{4,6},{5,7},{6,4},{7,5},{8,10},{9,11},{10,... | collective-permute-start | bytes 1179656 | tf_op jit(solution)/shard_map/ppermute | solution.py:327
  52.7 24.0 %collective-permute-start.18 = (bf16[272,1024]{1,0:T(8,128)(2,1)S(1)}, bf16[272,1024]{1,0:T(8,128)(2,1)S(1)}, u32[]{:S(2)}, u32[]{:S(2)}) collective-permute-start(bf16[272,1024]{1,0:T(8,128)(2,1)S(1)} %collective-permute-done.7.refs_0_), channel_id=1, source_target_pairs={{0,4},{1,5},{2,6},{3,7},{4,12},{5,13},{6,14},{7,15},{12,8},{13,9},... | collective-permute-start | bytes 1671176 | tf_op jit(solution)/shard_map/ppermute | solution.py:327
  56.1 9.5 %collective-permute-start.10 = (bf16[272,1024]{1,0:T(8,128)(2,1)S(1)}, bf16[272,1024]{1,0:T(8,128)(2,1)S(1)}, u32[]{:S(2)}, u32[]{:S(2)}) collective-permute-start(bf16[272,1024]{1,0:T(8,128)(2,1)S(1)} %collective-permute-done.7.refs_0_), channel_id=1, source_target_pairs={{0,1},{1,0},{2,3},{3,2},{4,5},{5,4},{6,7},{7,6},{8,9},{9,8},{10,11... | collective-permute-start | bytes 1671176 | tf_op jit(solution)/shard_map/ppermute | solution.py:327
  56.6 12.3 %collective-permute-start.13 = (bf16[192,1024]{1,0:T(8,128)(2,1)S(1)}, bf16[192,1024]{1,0:T(8,128)(2,1)S(1)}, u32[]{:S(2)}, u32[]{:S(2)}) collective-permute-start(bf16[192,1024]{1,0:T(8,128)(2,1)S(1)} %get-tuple-element.333), channel_id=1, source_target_pairs={{0,2},{1,3},{2,0},{3,1},{4,6},{5,7},{6,4},{7,5},{8,10},{9,11},{10,... | collective-permute-start | bytes 1179656 | tf_op jit(solution)/shard_map/ppermute | solution.py:327
  64.1 37.4 %collective-permute-start.16 = (bf16[192,1024]{1,0:T(8,128)(2,1)S(1)}, bf16[192,1024]{1,0:T(8,128)(2,1)S(1)}, u32[]{:S(2)}, u32[]{:S(2)}) collective-permute-start(bf16[192,1024]{1,0:T(8,128)(2,1)S(1)} %get-tuple-element.357), channel_id=1, source_target_pairs={{0,2},{1,3},{2,0},{3,1},{4,6},{5,7},{6,4},{7,5},{8,10},{9,11},{10,... | collective-permute-start | bytes 1179656 | tf_op jit(solution)/shard_map/ppermute | solution.py:327
  66.5 44.3 %collective-permute-start.24 = (bf16[256,1024]{1,0:T(8,128)(2,1)S(1)}, bf16[256,1024]{1,0:T(8,128)(2,1)S(1)}, u32[]{:S(2)}, u32[]{:S(2)}) collective-permute-start(bf16[256,1024]{1,0:T(8,128)(2,1)S(1)} %collective-permute-done.6.refs_0_), channel_id=1, source_target_pairs={{0,4},{1,5},{2,6},{3,7},{4,12},{5,13},{6,14},{7,15},{12,8},{13,9},... | collective-permute-start | bytes 1572872 | tf_op jit(solution)/shard_map/ppermute | solution.py:327
  74.1 36.7 %collective-permute-start.22 = (bf16[192,1024]{1,0:T(8,128)(2,1)S(1)}, bf16[192,1024]{1,0:T(8,128)(2,1)S(1)}, u32[]{:S(2)}, u32[]{:S(2)}) collective-permute-start(bf16[192,1024]{1,0:T(8,128)(2,1)S(1)} %get-tuple-element.389), channel_id=1, source_target_pairs={{0,2},{1,3},{2,0},{3,1},{4,6},{5,7},{6,4},{7,5},{8,10},{9,11},{10,... | collective-permute-start | bytes 1179656 | tf_op jit(solution)/shard_map/ppermute | solution.py:327
  75.7 18.4 %collective-permute-start.15 = (bf16[192,1024]{1,0:T(8,128)(2,1)S(1)}, bf16[192,1024]{1,0:T(8,128)(2,1)S(1)}, u32[]{:S(2)}, u32[]{:S(2)}) collective-permute-start(bf16[192,1024]{1,0:T(8,128)(2,1)S(1)} %get-tuple-element.350), channel_id=1, source_target_pairs={{0,2},{1,3},{2,0},{3,1},{4,6},{5,7},{6,4},{7,5},{8,10},{9,11},{10,... | collective-permute-start | bytes 1179656 | tf_op jit(solution)/shard_map/ppermute | solution.py:327
  94.1 11.4 %collective-permute-start.14 = (bf16[192,1024]{1,0:T(8,128)(2,1)S(1)}, bf16[192,1024]{1,0:T(8,128)(2,1)S(1)}, u32[]{:S(2)}, u32[]{:S(2)}) collective-permute-start(bf16[192,1024]{1,0:T(8,128)(2,1)S(1)} %get-tuple-element.348), channel_id=1, source_target_pairs={{0,2},{1,3},{2,0},{3,1},{4,6},{5,7},{6,4},{7,5},{8,10},{9,11},{10,... | collective-permute-start | bytes 1179656 | tf_op jit(solution)/shard_map/ppermute | solution.py:327
  101.6 14.4 %collective-permute-start.21 = (bf16[192,1024]{1,0:T(8,128)(2,1)S(1)}, bf16[192,1024]{1,0:T(8,128)(2,1)S(1)}, u32[]{:S(2)}, u32[]{:S(2)}) collective-permute-start(bf16[192,1024]{1,0:T(8,128)(2,1)S(1)} %get-tuple-element.387), channel_id=1, source_target_pairs={{0,2},{1,3},{2,0},{3,1},{4,6},{5,7},{6,4},{7,5},{8,10},{9,11},{10,... | collective-permute-start | bytes 1179656 | tf_op jit(solution)/shard_map/ppermute | solution.py:327
  110.8 29.1 %collective-permute-start.20 = (bf16[192,1024]{1,0:T(8,128)(2,1)S(1)}, bf16[192,1024]{1,0:T(8,128)(2,1)S(1)}, u32[]{:S(2)}, u32[]{:S(2)}) collective-permute-start(bf16[192,1024]{1,0:T(8,128)(2,1)S(1)} %get-tuple-element.383), channel_id=1, source_target_pairs={{0,2},{1,3},{2,0},{3,1},{4,6},{5,7},{6,4},{7,5},{8,10},{9,11},{10,... | collective-permute-start | bytes 1179656 | tf_op jit(solution)/shard_map/ppermute | solution.py:327
  112.8 18.4 %collective-permute-start.28 = (bf16[192,1024]{1,0:T(8,128)(2,1)S(1)}, bf16[192,1024]{1,0:T(8,128)(2,1)S(1)}, u32[]{:S(2)}, u32[]{:S(2)}) collective-permute-start(bf16[192,1024]{1,0:T(8,128)(2,1)S(1)} %get-tuple-element.416), channel_id=1, source_target_pairs={{0,2},{1,3},{2,0},{3,1},{4,6},{5,7},{6,4},{7,5},{8,10},{9,11},{10,... | collective-permute-start | bytes 1179656 | tf_op jit(solution)/shard_map/ppermute | solution.py:327
  114.8 22.4 %collective-permute-start.27 = (bf16[256,1024]{1,0:T(8,128)(2,1)S(1)}, bf16[256,1024]{1,0:T(8,128)(2,1)S(1)}, u32[]{:S(2)}, u32[]{:S(2)}) collective-permute-start(bf16[256,1024]{1,0:T(8,128)(2,1)S(1)} %combine_rows.17), channel_id=1, source_target_pairs={{0,4},{1,5},{2,6},{3,7},{4,12},{5,13},{6,14},{7,15},{12,8},{13,9},... | collective-permute-start | bytes 1572872 | tf_op jit(solution)/shard_map/ppermute | solution.py:327
  116.0 24.3 %collective-permute-start.31 = (bf16[192,1024]{1,0:T(8,128)(2,1)S(1)}, bf16[192,1024]{1,0:T(8,128)(2,1)S(1)}, u32[]{:S(2)}, u32[]{:S(2)}) collective-permute-start(bf16[192,1024]{1,0:T(8,128)(2,1)S(1)} %get-tuple-element.435), channel_id=1, source_target_pairs={{0,2},{1,3},{2,0},{3,1},{4,6},{5,7},{6,4},{7,5},{8,10},{9,11},{10,... | collective-permute-start | bytes 1179656 | tf_op jit(solution)/shard_map/ppermute | solution.py:327
  131.2 8.0 %collective-permute-start.26 = (bf16[256,1024]{1,0:T(8,128)(2,1)S(1)}, bf16[256,1024]{1,0:T(8,128)(2,1)S(1)}, u32[]{:S(2)}, u32[]{:S(2)}) collective-permute-start(bf16[256,1024]{1,0:T(8,128)(2,1)S(1)} %combine_rows.20), channel_id=1, source_target_pairs={{0,1},{1,0},{2,3},{3,2},{4,5},{5,4},{6,7},{7,6},{8,9},{9,8},{10,11... | collective-permute-start | bytes 1572872 | tf_op jit(solution)/shard_map/ppermute | solution.py:327
  131.2 16.2 %collective-permute-start.30 = (bf16[256,1024]{1,0:T(8,128)(2,1)S(1)}, bf16[256,1024]{1,0:T(8,128)(2,1)S(1)}, u32[]{:S(2)}, u32[]{:S(2)}) collective-permute-start(bf16[256,1024]{1,0:T(8,128)(2,1)S(1)} %combine_rows.19), channel_id=1, source_target_pairs={{0,4},{1,5},{2,6},{3,7},{4,12},{5,13},{6,14},{7,15},{12,8},{13,9},... | collective-permute-start | bytes 1572872 | tf_op jit(solution)/shard_map/ppermute | solution.py:327
  137.2 24.4 %collective-permute-start.34 = (bf16[192,1024]{1,0:T(8,128)(2,1)S(1)}, bf16[192,1024]{1,0:T(8,128)(2,1)S(1)}, u32[]{:S(2)}, u32[]{:S(2)}) collective-permute-start(bf16[192,1024]{1,0:T(8,128)(2,1)S(1)} %get-tuple-element.465), channel_id=1, source_target_pairs={{0,2},{1,3},{2,0},{3,1},{4,6},{5,7},{6,4},{7,5},{8,10},{9,11},{10,... | collective-permute-start | bytes 1179656 | tf_op jit(solution)/shard_map/ppermute | solution.py:327
  145.8 18.2 %collective-permute-start.33 = (bf16[192,1024]{1,0:T(8,128)(2,1)S(1)}, bf16[192,1024]{1,0:T(8,128)(2,1)S(1)}, u32[]{:S(2)}, u32[]{:S(2)}) collective-permute-start(bf16[192,1024]{1,0:T(8,128)(2,1)S(1)} %get-tuple-element.461), channel_id=1, source_target_pairs={{0,2},{1,3},{2,0},{3,1},{4,6},{5,7},{6,4},{7,5},{8,10},{9,11},{10,... | collective-permute-start | bytes 1179656 | tf_op jit(solution)/shard_map/ppermute | solution.py:327
  146.9 18.2 %collective-permute-start.38 = (bf16[256,1024]{1,0:T(8,128)(2,1)S(1)}, bf16[256,1024]{1,0:T(8,128)(2,1)S(1)}, u32[]{:S(2)}, u32[]{:S(2)}) collective-permute-start(bf16[256,1024]{1,0:T(8,128)(2,1)S(1)} %combine_rows.21), channel_id=1, source_target_pairs={{0,4},{1,5},{2,6},{3,7},{4,12},{5,13},{6,14},{7,15},{12,8},{13,9},... | collective-permute-start | bytes 1572872 | tf_op jit(solution)/shard_map/ppermute | solution.py:327
  161.6 29.9 %collective-permute-start.32 = (bf16[192,1024]{1,0:T(8,128)(2,1)S(1)}, bf16[192,1024]{1,0:T(8,128)(2,1)S(1)}, u32[]{:S(2)}, u32[]{:S(2)}) collective-permute-start(bf16[192,1024]{1,0:T(8,128)(2,1)S(1)} %get-tuple-element.449), channel_id=1, source_target_pairs={{0,2},{1,3},{2,0},{3,1},{4,6},{5,7},{6,4},{7,5},{8,10},{9,11},{10,... | collective-permute-start | bytes 1179656 | tf_op jit(solution)/shard_map/ppermute | solution.py:327
  162.6 29.3 %collective-permute-start.41 = (bf16[192,1024]{1,0:T(8,128)(2,1)S(1)}, bf16[192,1024]{1,0:T(8,128)(2,1)S(1)}, u32[]{:S(2)}, u32[]{:S(2)}) collective-permute-start(bf16[192,1024]{1,0:T(8,128)(2,1)S(1)} %get-tuple-element.521), channel_id=1, source_target_pairs={{0,2},{1,3},{2,0},{3,1},{4,6},{5,7},{6,4},{7,5},{8,10},{9,11},{10,... | collective-permute-start | bytes 1179656 | tf_op jit(solution)/shard_map/ppermute | solution.py:327
  165.1 14.9 %collective-permute-start.36 = (bf16[256,1024]{1,0:T(8,128)(2,1)S(1)}, bf16[256,1024]{1,0:T(8,128)(2,1)S(1)}, u32[]{:S(2)}, u32[]{:S(2)}) collective-permute-start(bf16[256,1024]{1,0:T(8,128)(2,1)S(1)} %combine_rows.23), channel_id=1, source_target_pairs={{0,4},{1,5},{2,6},{3,7},{4,12},{5,13},{6,14},{7,15},{12,8},{13,9},... | collective-permute-start | bytes 1572872 | tf_op jit(solution)/shard_map/ppermute | solution.py:327
  192.0 15.7 %collective-permute-start.40 = (bf16[256,1024]{1,0:T(8,128)(2,1)S(1)}, bf16[256,1024]{1,0:T(8,128)(2,1)S(1)}, u32[]{:S(2)}, u32[]{:S(2)}) collective-permute-start(bf16[256,1024]{1,0:T(8,128)(2,1)S(1)} %combine_rows.26), channel_id=1, source_target_pairs={{0,4},{1,5},{2,6},{3,7},{4,12},{5,13},{6,14},{7,15},{12,8},{13,9},... | collective-permute-start | bytes 1572872 | tf_op jit(solution)/shard_map/ppermute | solution.py:327
  192.5 16.5 %collective-permute-start.42 = (bf16[256,1024]{1,0:T(8,128)(2,1)S(1)}, bf16[256,1024]{1,0:T(8,128)(2,1)S(1)}, u32[]{:S(2)}, u32[]{:S(2)}) collective-permute-start(bf16[256,1024]{1,0:T(8,128)(2,1)S(1)} %combine_rows.29), channel_id=1, source_target_pairs={{0,1},{1,0},{2,3},{3,2},{4,5},{5,4},{6,7},{7,6},{8,9},{9,8},{10,11... | collective-permute-start | bytes 1572872 | tf_op jit(solution)/shard_map/ppermute | solution.py:327
  193.0 25.5 %collective-permute-start.43 = (bf16[256,1024]{1,0:T(8,128)(2,1)S(1)}, bf16[256,1024]{1,0:T(8,128)(2,1)S(1)}, u32[]{:S(2)}, u32[]{:S(2)}) collective-permute-start(bf16[256,1024]{1,0:T(8,128)(2,1)S(1)} %combine_rows.27), channel_id=1, source_target_pairs={{0,4},{1,5},{2,6},{3,7},{4,12},{5,13},{6,14},{7,15},{12,8},{13,9},... | collective-permute-start | bytes 1572872 | tf_op jit(solution)/shard_map/ppermute | solution.py:327
  (48 other events, 262.6 us)

commit v3 on v2

--- a/solution.py
+++ b/solution.py
@@ -12,7 +12,7 @@
 PAIR = 2
 INV_ROOT_TWO = 0.7071067811865476
 INV_ROOT_TAU = 0.3989422804014327
-PEAK = 5.75e9
+PEAK = 3.45e9
 BF16 = jnp.bfloat16
 F32 = jnp.float32
 SMEM = pl.BlockSpec(memory_space=pltpu.SMEM)
@@ -31,7 +31,7 @@
 
 
 def call(
-    kernel, order, operands, specs, out_shape, out_specs, name, mib=24, grid=(1,), scratch=(), cost=1.5
+    kernel, order, operands, specs, out_shape, out_specs, name, mib=24, grid=(1,), scratch=(), cost=0.4
 ):
     result = pl.pallas_call(
         kernel,
@@ -51,8 +51,8 @@
 
 
 class Order:
-    def __init__(self):
-        self.last = None
+    def __init__(self, last=None):
+        self.last = last
 
     def behind(self, operands):
         if self.last is None:
@@ -298,7 +298,7 @@
     refs[-1][0] = total.astype(BF16)
 
 
-def weight_grad(order, lefts, rights, tile, by_left, name):
+def weight_grad(after, lefts, rights, tile, by_left, name):
     m, n = lefts[0].shape[1], rights[0].shape[1]
 
     def spec(array, tiled):
@@ -309,7 +309,7 @@
 
     return call(
         functools.partial(weight_kernel, len(lefts)),
-        order,
+        Order(after),
         [*lefts, *rights],
         [spec(a, by_left) for a in lefts] + [spec(b, not by_left) for b in rights],
         jax.ShapeDtypeStruct((1, m, n), BF16),
@@ -421,20 +421,21 @@
     x.back(0)
     grad.back(0)
     every = range(length)
-    w_out_grad = weight_grad(
-        order, [x.kept[t][1] for t in every], [grad.kept[t][0] for t in every], 512, True, "weights_out"
-    )
     x.cross(top)
     grad.cross(top)
     x.fold(top)
     grad.fold(top)
+    after = order.last
+    w_out_grad = weight_grad(
+        None, [x.kept[t][1] for t in every], [grad.kept[t][0] for t in every], 512, True, "weights_out"
+    )
     w_in_grad = weight_grad(
-        order, [x.kept[t][0] for t in every], [grad.kept[t][1] for t in every], 512, False, "weights_in"
-    )
-    for tensor in both:
-        tensor.cross(0)
-    for tensor in both:
-        tensor.fold(0)
+        after, [x.kept[t][0] for t in every], [grad.kept[t][1] for t in every], 512, False, "weights_in"
+    )
+    x.cross(0)
+    grad.cross(0)
+    x.fold(0)
+    grad.fold(0)
     return x.moving, grad.moving, w_in_grad, w_out_grad
 
 

time: 220 us -> 206 us (0.936)
  waiting for transfers between devices: 87.5 us -> 77.8 us
  starting transfers between devices: 41.7 us -> 37.7 us
    ppermute x44, waiting for transfers between devices: 87.5 us -> 77.8 us  [permute(): return lax.ppermute(value, AXIS, pairs)]
    ppermute x44, starting transfers between devices: 41.7 us -> 37.7 us  [permute(): return lax.ppermute(value, AXIS, pairs)]
  transfers between devices with their start and end apart: 44 -> 44, of which waited for: 12 -> 14; matrix products, arithmetic and copies ran while one was open for 0% -> 0% of each run, Pallas kernels for 36% -> 38%
where the time goes in v3:
time: 206 us; the launch traced here: 205 us
  Pallas kernels  80.3 us (39%)
  waiting for transfers between devices  77.8 us (38%)
  starting transfers between devices  37.7 us (18%)
  local copies, waits for them, and re-layouts  8.27 us (4%)
    pallas_call x35, Pallas kernels, call(): pl.pallas_call(kernel, grid=grid, out_shape=out_shape, in_specs=specs, ou...  80.3 us
    ppermute x44, waiting for transfers between devices, permute(): return lax.ppermute(value, AXIS, pairs)  77.8 us
    ppermute x44, starting transfers between devices, permute(): return lax.ppermute(value, AXIS, pairs)  37.7 us
    unnamed x74, local copies, waits for them, and re-layouts  8.27 us
  transfers between devices with their start and end apart: 44, of which 14 were waited for; matrix products, arithmetic and copies ran while one was open for 0% of the time, Pallas kernels for 38%

profile of v3, /device:TPU:0, one launch (start us, length us, event | category | flops | bytes accessed | tf_op | source)
XLA Modules:
  0.0 205.4 jit_solution(8209274025900755350)
XLA Ops:
  4.8 2.6 %collective-permute-start.4 = (bf16[272,1024]{1,0:T(8,128)(2,1)S(1)}, bf16[272,1024]{1,0:T(8,128)(2,1)S(1)}, u32[]{:S(2)}, u32[]{:S(2)}) collective-permute-start(bf16[272,1024]{1,0:T(8,128)(2,1)S(1)} %stack_block.1.refs_0_), channel_id=1, source_target_pairs={{0,4},{1,5},{2,6},{3,7},{4,12},{5,13},{6,14},{7,15},{12,8},{13,9},... | collective-permute-start | bytes 1671176 | tf_op jit(solution)/shard_map/ppermute | solution.py:327
  8.2 1.6 collective-permute-start.1
  9.8 2.6 %collective-permute-start.3 = (bf16[256,1024]{1,0:T(8,128)(2,1)S(1)}, bf16[256,1024]{1,0:T(8,128)(2,1)S(1)}, u32[]{:S(2)}, u32[]{:S(2)}) collective-permute-start(bf16[256,1024]{1,0:T(8,128)(2,1)S(1)} %copy-done.3), channel_id=1, source_target_pairs={{0,4},{1,5},{2,6},{3,7},{4,12},{5,13},{6,14},{7,15},{12,8},{13,9},... | collective-permute-start | bytes 1572872 | tf_op jit(solution)/shard_map/ppermute | solution.py:327
  12.9 9.0 %collective-permute-done.4.refs_0_ = bf16[272,1024]{1,0:T(8,128)(2,1)S(1)} collective-permute-done((bf16[272,1024]{1,0:T(8,128)(2,1)S(1)}, bf16[272,1024]{1,0:T(8,128)(2,1)S(1)}, u32[]{:S(2)}, u32[]{:S(2)}) %collective-permute-start.4) | collective-permute-done | bytes 557088 | tf_op jit(solution)/shard_map/ppermute | solution.py:327
  22.9 1.5 collective-permute-start.9
  24.5 5.9 %expert_forward.4 = (bf16[192,1024]{1,0:T(8,128)(2,1)S(1)}, bf16[192,1024]{1,0:T(8,128)(2,1)S(1)}, bf16[384,1024]{1,0:T(8,128)(2,1)S(1)}, bf16[384,2048]{1,0:T(8,128)(2,1)S(1)}, f32[384,2048]{1,0:T(8,128)S(1)}) custom-call(bf16[192,1024]{1,0:T(8,128)(2,1)S(1)} %get-tuple-element.280.mine_ref, bf16[192,1024]{1,0:T(8,128)(2,1)S(1)} %collective-permute-done.1.side_ref, ...), custom_call_target="tpu_custom_call" | custom-call | flops 17250000896 | bytes 1000 | tf_op jit(solution)/shard_map/expert_forward/pallas_call | solution.py:36
  33.2 3.4 %collective-permute-start.6 = (bf16[256,1024]{1,0:T(8,128)(2,1)S(1)}, bf16[256,1024]{1,0:T(8,128)(2,1)S(1)}, u32[]{:S(2)}, u32[]{:S(2)}) collective-permute-start(bf16[256,1024]{1,0:T(8,128)(2,1)S(1)} %collective-permute-done.3.refs_0_), channel_id=1, source_target_pairs={{0,4},{1,5},{2,6},{3,7},{4,12},{5,13},{6,14},{7,15},{12,8},{13,9},... | collective-permute-start | bytes 1572872 | tf_op jit(solution)/shard_map/ppermute | solution.py:327
  37.1 5.2 %expert_backward.4 = (bf16[192,1024]{1,0:T(8,128)(2,1)S(1)}, bf16[192,1024]{1,0:T(8,128)(2,1)S(1)}, bf16[384,1024]{1,0:T(8,128)(2,1)S(1)}, bf16[384,2048]{1,0:T(8,128)(2,1)S(1)}) custom-call(bf16[192,1024]{1,0:T(8,128)(2,1)S(1)} %get-tuple-element.297.mine_ref, bf16[192,1024]{1,0:T(8,128)(2,1)S(1)} %collective-permute-done.9.side_ref, ...), custom_call_target="tpu_custom_call" | custom-call | flops 17250000896 | bytes 1000 | tf_op jit(solution)/shard_map/expert_backward/pallas_call | solution.py:36
  42.9 2.2 %collective-permute-done.7.refs_0_ = bf16[272,1024]{1,0:T(8,128)(2,1)S(1)} collective-permute-done((bf16[272,1024]{1,0:T(8,128)(2,1)S(1)}, bf16[272,1024]{1,0:T(8,128)(2,1)S(1)}, u32[]{:S(2)}, u32[]{:S(2)}) %collective-permute-start.7) | collective-permute-done | bytes 557088 | tf_op jit(solution)/shard_map/ppermute | solution.py:327
  46.1 2.1 %collective-permute-done.11.side_ref = bf16[192,1024]{1,0:T(8,128)(2,1)S(1)} collective-permute-done((bf16[192,1024]{1,0:T(8,128)(2,1)S(1)}, bf16[192,1024]{1,0:T(8,128)(2,1)S(1)}, u32[]{:S(2)}, u32[]{:S(2)}) %collective-permute-start.11) | collective-permute-done | bytes 393248 | tf_op jit(solution)/shard_map/ppermute | solution.py:327
  48.7 5.9 %expert_forward.5 = (bf16[192,1024]{1,0:T(8,128)(2,1)S(1)}, bf16[192,1024]{1,0:T(8,128)(2,1)S(1)}, bf16[384,1024]{1,0:T(8,128)(2,1)S(1)}, bf16[384,2048]{1,0:T(8,128)(2,1)S(1)}, f32[384,2048]{1,0:T(8,128)S(1)}) custom-call(bf16[192,1024]{1,0:T(8,128)(2,1)S(1)} %get-tuple-element.312.mine_ref, bf16[192,1024]{1,0:T(8,128)(2,1)S(1)} %collective-permute-done.11.side_ref, ...), custom_call_target="tpu_custom_call" | custom-call | flops 17250000896 | bytes 1000 | tf_op jit(solution)/shard_map/expert_forward/pallas_call | solution.py:36
  55.5 1.5 collective-permute-start.16
  57.9 2.3 %collective-permute-done.13.side_ref = bf16[192,1024]{1,0:T(8,128)(2,1)S(1)} collective-permute-done((bf16[192,1024]{1,0:T(8,128)(2,1)S(1)}, bf16[192,1024]{1,0:T(8,128)(2,1)S(1)}, u32[]{:S(2)}, u32[]{:S(2)}) %collective-permute-start.13) | collective-permute-done | bytes 393248 | tf_op jit(solution)/shard_map/ppermute | solution.py:327
  60.2 5.2 %expert_backward.5 = (bf16[192,1024]{1,0:T(8,128)(2,1)S(1)}, bf16[192,1024]{1,0:T(8,128)(2,1)S(1)}, bf16[384,1024]{1,0:T(8,128)(2,1)S(1)}, bf16[384,2048]{1,0:T(8,128)(2,1)S(1)}) custom-call(bf16[192,1024]{1,0:T(8,128)(2,1)S(1)} %get-tuple-element.327.mine_ref, bf16[192,1024]{1,0:T(8,128)(2,1)S(1)} %collective-permute-done.13.side_ref, ...), custom_call_target="tpu_custom_call" | custom-call | flops 17250000896 | bytes 1000 | tf_op jit(solution)/shard_map/expert_backward/pallas_call | solution.py:36
  65.9 9.9 %collective-permute-done.15.side_ref = bf16[192,1024]{1,0:T(8,128)(2,1)S(1)} collective-permute-done((bf16[192,1024]{1,0:T(8,128)(2,1)S(1)}, bf16[192,1024]{1,0:T(8,128)(2,1)S(1)}, u32[]{:S(2)}, u32[]{:S(2)}) %collective-permute-start.15) | collective-permute-done | bytes 393248 | tf_op jit(solution)/shard_map/ppermute | solution.py:327
  75.8 5.9 %expert_forward.6 = (bf16[192,1024]{1,0:T(8,128)(2,1)S(1)}, bf16[192,1024]{1,0:T(8,128)(2,1)S(1)}, bf16[384,1024]{1,0:T(8,128)(2,1)S(1)}, bf16[384,2048]{1,0:T(8,128)(2,1)S(1)}, f32[384,2048]{1,0:T(8,128)S(1)}) custom-call(bf16[192,1024]{1,0:T(8,128)(2,1)S(1)} %get-tuple-element.343.mine_ref, bf16[192,1024]{1,0:T(8,128)(2,1)S(1)} %collective-permute-done.15.side_ref, ...), custom_call_target="tpu_custom_call" | custom-call | flops 17250000896 | bytes 1000 | tf_op jit(solution)/shard_map/expert_forward/pallas_call | solution.py:36
  82.7 1.8 collective-permute-start.24
  87.8 8.7 %collective-permute-done.14.side_ref = bf16[192,1024]{1,0:T(8,128)(2,1)S(1)} collective-permute-done((bf16[192,1024]{1,0:T(8,128)(2,1)S(1)}, bf16[192,1024]{1,0:T(8,128)(2,1)S(1)}, u32[]{:S(2)}, u32[]{:S(2)}) %collective-permute-start.14) | collective-permute-done | bytes 393248 | tf_op jit(solution)/shard_map/ppermute | solution.py:327
  97.7 5.2 %expert_backward.6 = (bf16[192,1024]{1,0:T(8,128)(2,1)S(1)}, bf16[192,1024]{1,0:T(8,128)(2,1)S(1)}, bf16[384,1024]{1,0:T(8,128)(2,1)S(1)}, bf16[384,2048]{1,0:T(8,128)(2,1)S(1)}) custom-call(bf16[192,1024]{1,0:T(8,128)(2,1)S(1)} %get-tuple-element.368.mine_ref, bf16[192,1024]{1,0:T(8,128)(2,1)S(1)} %collective-permute-done.14.side_ref, ...), custom_call_target="tpu_custom_call" | custom-call | flops 17250000896 | bytes 1000 | tf_op jit(solution)/shard_map/expert_backward/pallas_call | solution.py:36
  104.4 1.6 collective-permute-start.21
  106.5 1.5 collective-permute-start.20
  109.3 7.1 %collective-permute-done.21.refs_1_ = bf16[192,1024]{1,0:T(8,128)(2,1)S(1)} collective-permute-done((bf16[192,1024]{1,0:T(8,128)(2,1)S(1)}, bf16[192,1024]{1,0:T(8,128)(2,1)S(1)}, u32[]{:S(2)}, u32[]{:S(2)}) %collective-permute-start.21) | collective-permute-done | bytes 393248 | tf_op jit(solution)/shard_map/ppermute | solution.py:327
  116.9 7.9 %collective-permute-done.28.side_ref = bf16[192,1024]{1,0:T(8,128)(2,1)S(1)} collective-permute-done((bf16[192,1024]{1,0:T(8,128)(2,1)S(1)}, bf16[192,1024]{1,0:T(8,128)(2,1)S(1)}, u32[]{:S(2)}, u32[]{:S(2)}) %collective-permute-start.28) | collective-permute-done | bytes 393248 | tf_op jit(solution)/shard_map/ppermute | solution.py:327
  126.7 5.9 %expert_forward.7 = (bf16[192,1024]{1,0:T(8,128)(2,1)S(1)}, bf16[192,1024]{1,0:T(8,128)(2,1)S(1)}, bf16[384,1024]{1,0:T(8,128)(2,1)S(1)}, bf16[384,2048]{1,0:T(8,128)(2,1)S(1)}, f32[384,2048]{1,0:T(8,128)S(1)}) custom-call(bf16[192,1024]{1,0:T(8,128)(2,1)S(1)} %get-tuple-element.409.mine_ref, bf16[192,1024]{1,0:T(8,128)(2,1)S(1)} %collective-permute-done.28.side_ref, ...), custom_call_target="tpu_custom_call" | custom-call | flops 17250000896 | bytes 1000 | tf_op jit(solution)/shard_map/expert_forward/pallas_call | solution.py:36
  134.3 7.4 %collective-permute-done.31.side_ref = bf16[192,1024]{1,0:T(8,128)(2,1)S(1)} collective-permute-done((bf16[192,1024]{1,0:T(8,128)(2,1)S(1)}, bf16[192,1024]{1,0:T(8,128)(2,1)S(1)}, u32[]{:S(2)}, u32[]{:S(2)}) %collective-permute-start.31) | collective-permute-done | bytes 393248 | tf_op jit(solution)/shard_map/ppermute | solution.py:327
  142.1 5.2 %expert_backward.7 = (bf16[192,1024]{1,0:T(8,128)(2,1)S(1)}, bf16[192,1024]{1,0:T(8,128)(2,1)S(1)}, bf16[384,1024]{1,0:T(8,128)(2,1)S(1)}, bf16[384,2048]{1,0:T(8,128)(2,1)S(1)}) custom-call(bf16[192,1024]{1,0:T(8,128)(2,1)S(1)} %get-tuple-element.429.mine_ref, bf16[192,1024]{1,0:T(8,128)(2,1)S(1)} %collective-permute-done.31.side_ref, ...), custom_call_target="tpu_custom_call" | custom-call | flops 17250000896 | bytes 1000 | tf_op jit(solution)/shard_map/expert_backward/pallas_call | solution.py:36
  151.2 9.0 %collective-permute-done.33.refs_1_ = bf16[192,1024]{1,0:T(8,128)(2,1)S(1)} collective-permute-done((bf16[192,1024]{1,0:T(8,128)(2,1)S(1)}, bf16[192,1024]{1,0:T(8,128)(2,1)S(1)}, u32[]{:S(2)}, u32[]{:S(2)}) %collective-permute-start.33) | collective-permute-done | bytes 393248 | tf_op jit(solution)/shard_map/ppermute | solution.py:327
  162.2 1.5 collective-permute-start.41
  165.2 10.9 %weights_out.1 = bf16[1,2048,1024]{2,1,0:T(8,128)(2,1)} custom-call(bf16[384,2048]{1,0:T(8,128)(2,1)S(1)} %copy-done.13, bf16[384,2048]{1,0:T(8,128)(2,1)S(1)} %copy-done.15, bf16[384,2048]{1,0:T(8,128)(2,1)S(1)} %copy-done.17, bf16[384,2048]{1,0:T(8,128)(2,1)S(1)} %copy-done.19, bf16[384,1024]{1,0:T(8,128)(2,1)S(1)} %copy-done.21, ...), custom_call_target="tpu_custom_call" | custom-call | flops 34500001792 | bytes 1000 | tf_op jit(solution)/shard_map/weights_out/pallas_call | solution.py:36
  179.0 2.9 %collective-permute-start.43 = (bf16[256,1024]{1,0:T(8,128)(2,1)S(1)}, bf16[256,1024]{1,0:T(8,128)(2,1)S(1)}, u32[]{:S(2)}, u32[]{:S(2)}) collective-permute-start(bf16[256,1024]{1,0:T(8,128)(2,1)S(1)} %combine_rows.27), channel_id=1, source_target_pairs={{0,4},{1,5},{2,6},{3,7},{4,12},{5,13},{6,14},{7,15},{12,8},{13,9},... | collective-permute-start | bytes 1572872 | tf_op jit(solution)/shard_map/ppermute | solution.py:327
  181.9 11.0 %weights_in.1 = bf16[1,1024,2048]{2,1,0:T(8,128)(2,1)} custom-call(bf16[384,1024]{1,0:T(8,128)(2,1)S(1)} %copy-done.29, bf16[384,1024]{1,0:T(8,128)(2,1)S(1)} %copy-done.31, bf16[384,1024]{1,0:T(8,128)(2,1)S(1)} %copy-done.33, bf16[384,1024]{1,0:T(8,128)(2,1)S(1)} %copy-done.35, bf16[384,2048]{1,0:T(8,128)(2,1)S(1)} %copy-done.5, ...), custom_call_target="tpu_custom_call" | custom-call | flops 34500001792 | bytes 1000 | tf_op jit(solution)/shard_map/weights_in/pallas_call | solution.py:36
  194.9 9.2 %collective-permute-done.43.refs_5_ = bf16[256,1024]{1,0:T(8,128)(2,1)S(1)} collective-permute-done((bf16[256,1024]{1,0:T(8,128)(2,1)S(1)}, bf16[256,1024]{1,0:T(8,128)(2,1)S(1)}, u32[]{:S(2)}, u32[]{:S(2)}) %collective-permute-start.43) | collective-permute-done | bytes 524320 | tf_op jit(solution)/shard_map/ppermute | solution.py:327
  (165 shorter events, 40.6 us)
Async XLA Ops:
  4.8 17.1 %collective-permute-start.4 = (bf16[272,1024]{1,0:T(8,128)(2,1)S(1)}, bf16[272,1024]{1,0:T(8,128)(2,1)S(1)}, u32[]{:S(2)}, u32[]{:S(2)}) collective-permute-start(bf16[272,1024]{1,0:T(8,128)(2,1)S(1)} %stack_block.1.refs_0_), channel_id=1, source_target_pairs={{0,4},{1,5},{2,6},{3,7},{4,12},{5,13},{6,14},{7,15},{12,8},{13,9},... | collective-permute-start | bytes 1671176 | tf_op jit(solution)/shard_map/ppermute | solution.py:327
  8.2 16.3 %collective-permute-start.1 = (bf16[192,1024]{1,0:T(8,128)(2,1)S(1)}, bf16[192,1024]{1,0:T(8,128)(2,1)S(1)}, u32[]{:S(2)}, u32[]{:S(2)}) collective-permute-start(bf16[192,1024]{1,0:T(8,128)(2,1)S(1)} %get-tuple-element.270), channel_id=1, source_target_pairs={{0,2},{1,3},{2,0},{3,1},{4,6},{5,7},{6,4},{7,5},{8,10},{9,11},{10,... | collective-permute-start | bytes 1179656 | tf_op jit(solution)/shard_map/ppermute | solution.py:327
  9.8 23.4 %collective-permute-start.3 = (bf16[256,1024]{1,0:T(8,128)(2,1)S(1)}, bf16[256,1024]{1,0:T(8,128)(2,1)S(1)}, u32[]{:S(2)}, u32[]{:S(2)}) collective-permute-start(bf16[256,1024]{1,0:T(8,128)(2,1)S(1)} %copy-done.3), channel_id=1, source_target_pairs={{0,4},{1,5},{2,6},{3,7},{4,12},{5,13},{6,14},{7,15},{12,8},{13,9},... | collective-permute-start | bytes 1572872 | tf_op jit(solution)/shard_map/ppermute | solution.py:327
  21.9 23.2 %collective-permute-start.7 = (bf16[272,1024]{1,0:T(8,128)(2,1)S(1)}, bf16[272,1024]{1,0:T(8,128)(2,1)S(1)}, u32[]{:S(2)}, u32[]{:S(2)}) collective-permute-start(bf16[272,1024]{1,0:T(8,128)(2,1)S(1)} %collective-permute-done.4.refs_0_), channel_id=1, source_target_pairs={{0,4},{1,5},{2,6},{3,7},{4,12},{5,13},{6,14},{7,15},{12,8},{13,9},... | collective-permute-start | bytes 1671176 | tf_op jit(solution)/shard_map/ppermute | solution.py:327
  22.9 13.7 %collective-permute-start.9 = (bf16[192,1024]{1,0:T(8,128)(2,1)S(1)}, bf16[192,1024]{1,0:T(8,128)(2,1)S(1)}, u32[]{:S(2)}, u32[]{:S(2)}) collective-permute-start(bf16[192,1024]{1,0:T(8,128)(2,1)S(1)} %get-tuple-element.295), channel_id=1, source_target_pairs={{0,2},{1,3},{2,0},{3,1},{4,6},{5,7},{6,4},{7,5},{8,10},{9,11},{10,... | collective-permute-start | bytes 1179656 | tf_op jit(solution)/shard_map/ppermute | solution.py:327
  33.2 24.6 %collective-permute-start.6 = (bf16[256,1024]{1,0:T(8,128)(2,1)S(1)}, bf16[256,1024]{1,0:T(8,128)(2,1)S(1)}, u32[]{:S(2)}, u32[]{:S(2)}) collective-permute-start(bf16[256,1024]{1,0:T(8,128)(2,1)S(1)} %collective-permute-done.3.refs_0_), channel_id=1, source_target_pairs={{0,4},{1,5},{2,6},{3,7},{4,12},{5,13},{6,14},{7,15},{12,8},{13,9},... | collective-permute-start | bytes 1572872 | tf_op jit(solution)/shard_map/ppermute | solution.py:327
  45.1 30.7 %collective-permute-start.18 = (bf16[272,1024]{1,0:T(8,128)(2,1)S(1)}, bf16[272,1024]{1,0:T(8,128)(2,1)S(1)}, u32[]{:S(2)}, u32[]{:S(2)}) collective-permute-start(bf16[272,1024]{1,0:T(8,128)(2,1)S(1)} %collective-permute-done.7.refs_0_), channel_id=1, source_target_pairs={{0,4},{1,5},{2,6},{3,7},{4,12},{5,13},{6,14},{7,15},{12,8},{13,9},... | collective-permute-start | bytes 1671176 | tf_op jit(solution)/shard_map/ppermute | solution.py:327
  48.2 12.0 %collective-permute-start.13 = (bf16[192,1024]{1,0:T(8,128)(2,1)S(1)}, bf16[192,1024]{1,0:T(8,128)(2,1)S(1)}, u32[]{:S(2)}, u32[]{:S(2)}) collective-permute-start(bf16[192,1024]{1,0:T(8,128)(2,1)S(1)} %get-tuple-element.325), channel_id=1, source_target_pairs={{0,2},{1,3},{2,0},{3,1},{4,6},{5,7},{6,4},{7,5},{8,10},{9,11},{10,... | collective-permute-start | bytes 1179656 | tf_op jit(solution)/shard_map/ppermute | solution.py:327
  55.5 26.2 %collective-permute-start.16 = (bf16[192,1024]{1,0:T(8,128)(2,1)S(1)}, bf16[192,1024]{1,0:T(8,128)(2,1)S(1)}, u32[]{:S(2)}, u32[]{:S(2)}) collective-permute-start(bf16[192,1024]{1,0:T(8,128)(2,1)S(1)} %get-tuple-element.349), channel_id=1, source_target_pairs={{0,2},{1,3},{2,0},{3,1},{4,6},{5,7},{6,4},{7,5},{8,10},{9,11},{10,... | collective-permute-start | bytes 1179656 | tf_op jit(solution)/shard_map/ppermute | solution.py:327
  60.2 15.6 %collective-permute-start.15 = (bf16[192,1024]{1,0:T(8,128)(2,1)S(1)}, bf16[192,1024]{1,0:T(8,128)(2,1)S(1)}, u32[]{:S(2)}, u32[]{:S(2)}) collective-permute-start(bf16[192,1024]{1,0:T(8,128)(2,1)S(1)} %get-tuple-element.342), channel_id=1, source_target_pairs={{0,2},{1,3},{2,0},{3,1},{4,6},{5,7},{6,4},{7,5},{8,10},{9,11},{10,... | collective-permute-start | bytes 1179656 | tf_op jit(solution)/shard_map/ppermute | solution.py:327
  82.7 15.0 %collective-permute-start.24 = (bf16[256,1024]{1,0:T(8,128)(2,1)S(1)}, bf16[256,1024]{1,0:T(8,128)(2,1)S(1)}, u32[]{:S(2)}, u32[]{:S(2)}) collective-permute-start(bf16[256,1024]{1,0:T(8,128)(2,1)S(1)} %collective-permute-done.6.refs_0_), channel_id=1, source_target_pairs={{0,4},{1,5},{2,6},{3,7},{4,12},{5,13},{6,14},{7,15},{12,8},{13,9},... | collective-permute-start | bytes 1572872 | tf_op jit(solution)/shard_map/ppermute | solution.py:327
  84.5 12.0 %collective-permute-start.14 = (bf16[192,1024]{1,0:T(8,128)(2,1)S(1)}, bf16[192,1024]{1,0:T(8,128)(2,1)S(1)}, u32[]{:S(2)}, u32[]{:S(2)}) collective-permute-start(bf16[192,1024]{1,0:T(8,128)(2,1)S(1)} %get-tuple-element.340), channel_id=1, source_target_pairs={{0,2},{1,3},{2,0},{3,1},{4,6},{5,7},{6,4},{7,5},{8,10},{9,11},{10,... | collective-permute-start | bytes 1179656 | tf_op jit(solution)/shard_map/ppermute | solution.py:327
  86.0 17.9 %collective-permute-start.22 = (bf16[192,1024]{1,0:T(8,128)(2,1)S(1)}, bf16[192,1024]{1,0:T(8,128)(2,1)S(1)}, u32[]{:S(2)}, u32[]{:S(2)}) collective-permute-start(bf16[192,1024]{1,0:T(8,128)(2,1)S(1)} %get-tuple-element.381), channel_id=1, source_target_pairs={{0,2},{1,3},{2,0},{3,1},{4,6},{5,7},{6,4},{7,5},{8,10},{9,11},{10,... | collective-permute-start | bytes 1179656 | tf_op jit(solution)/shard_map/ppermute | solution.py:327
  106.0 18.8 %collective-permute-start.28 = (bf16[192,1024]{1,0:T(8,128)(2,1)S(1)}, bf16[192,1024]{1,0:T(8,128)(2,1)S(1)}, u32[]{:S(2)}, u32[]{:S(2)}) collective-permute-start(bf16[192,1024]{1,0:T(8,128)(2,1)S(1)} %get-tuple-element.408), channel_id=1, source_target_pairs={{0,2},{1,3},{2,0},{3,1},{4,6},{5,7},{6,4},{7,5},{8,10},{9,11},{10,... | collective-permute-start | bytes 1179656 | tf_op jit(solution)/shard_map/ppermute | solution.py:327
  106.5 27.3 %collective-permute-start.20 = (bf16[192,1024]{1,0:T(8,128)(2,1)S(1)}, bf16[192,1024]{1,0:T(8,128)(2,1)S(1)}, u32[]{:S(2)}, u32[]{:S(2)}) collective-permute-start(bf16[192,1024]{1,0:T(8,128)(2,1)S(1)} %get-tuple-element.375), channel_id=1, source_target_pairs={{0,2},{1,3},{2,0},{3,1},{4,6},{5,7},{6,4},{7,5},{8,10},{9,11},{10,... | collective-permute-start | bytes 1179656 | tf_op jit(solution)/shard_map/ppermute | solution.py:327
  108.0 24.6 %collective-permute-start.27 = (bf16[256,1024]{1,0:T(8,128)(2,1)S(1)}, bf16[256,1024]{1,0:T(8,128)(2,1)S(1)}, u32[]{:S(2)}, u32[]{:S(2)}) collective-permute-start(bf16[256,1024]{1,0:T(8,128)(2,1)S(1)} %combine_rows.17), channel_id=1, source_target_pairs={{0,4},{1,5},{2,6},{3,7},{4,12},{5,13},{6,14},{7,15},{12,8},{13,9},... | collective-permute-start | bytes 1572872 | tf_op jit(solution)/shard_map/ppermute | solution.py:327
  116.8 16.4 %collective-permute-start.26 = (bf16[256,1024]{1,0:T(8,128)(2,1)S(1)}, bf16[256,1024]{1,0:T(8,128)(2,1)S(1)}, u32[]{:S(2)}, u32[]{:S(2)}) collective-permute-start(bf16[256,1024]{1,0:T(8,128)(2,1)S(1)} %combine_rows.20), channel_id=1, source_target_pairs={{0,1},{1,0},{2,3},{3,2},{4,5},{5,4},{6,7},{7,6},{8,9},{9,8},{10,11... | collective-permute-start | bytes 1572872 | tf_op jit(solution)/shard_map/ppermute | solution.py:327
  124.8 24.8 %collective-permute-start.30 = (bf16[256,1024]{1,0:T(8,128)(2,1)S(1)}, bf16[256,1024]{1,0:T(8,128)(2,1)S(1)}, u32[]{:S(2)}, u32[]{:S(2)}) collective-permute-start(bf16[256,1024]{1,0:T(8,128)(2,1)S(1)} %combine_rows.19), channel_id=1, source_target_pairs={{0,4},{1,5},{2,6},{3,7},{4,12},{5,13},{6,14},{7,15},{12,8},{13,9},... | collective-permute-start | bytes 1572872 | tf_op jit(solution)/shard_map/ppermute | solution.py:327
  125.2 16.5 %collective-permute-start.31 = (bf16[192,1024]{1,0:T(8,128)(2,1)S(1)}, bf16[192,1024]{1,0:T(8,128)(2,1)S(1)}, u32[]{:S(2)}, u32[]{:S(2)}) collective-permute-start(bf16[192,1024]{1,0:T(8,128)(2,1)S(1)} %get-tuple-element.427), channel_id=1, source_target_pairs={{0,2},{1,3},{2,0},{3,1},{4,6},{5,7},{6,4},{7,5},{8,10},{9,11},{10,... | collective-permute-start | bytes 1179656 | tf_op jit(solution)/shard_map/ppermute | solution.py:327
  132.6 18.1 %collective-permute-start.34 = (bf16[192,1024]{1,0:T(8,128)(2,1)S(1)}, bf16[192,1024]{1,0:T(8,128)(2,1)S(1)}, u32[]{:S(2)}, u32[]{:S(2)}) collective-permute-start(bf16[192,1024]{1,0:T(8,128)(2,1)S(1)} %get-tuple-element.449), channel_id=1, source_target_pairs={{0,2},{1,3},{2,0},{3,1},{4,6},{5,7},{6,4},{7,5},{8,10},{9,11},{10,... | collective-permute-start | bytes 1179656 | tf_op jit(solution)/shard_map/ppermute | solution.py:327
  134.2 15.5 %collective-permute-start.29 = (bf16[256,1024]{1,0:T(8,128)(2,1)S(1)}, bf16[256,1024]{1,0:T(8,128)(2,1)S(1)}, u32[]{:S(2)}, u32[]{:S(2)}) collective-permute-start(bf16[256,1024]{1,0:T(8,128)(2,1)S(1)} %combine_rows.22), channel_id=1, source_target_pairs={{0,1},{1,0},{2,3},{3,2},{4,5},{5,4},{6,7},{7,6},{8,9},{9,8},{10,11... | collective-permute-start | bytes 1572872 | tf_op jit(solution)/shard_map/ppermute | solution.py:327
  141.7 20.5 %collective-permute-start.38 = (bf16[256,1024]{1,0:T(8,128)(2,1)S(1)}, bf16[256,1024]{1,0:T(8,128)(2,1)S(1)}, u32[]{:S(2)}, u32[]{:S(2)}) collective-permute-start(bf16[256,1024]{1,0:T(8,128)(2,1)S(1)} %combine_rows.21), channel_id=1, source_target_pairs={{0,4},{1,5},{2,6},{3,7},{4,12},{5,13},{6,14},{7,15},{12,8},{13,9},... | collective-permute-start | bytes 1572872 | tf_op jit(solution)/shard_map/ppermute | solution.py:327
  148.2 12.1 %collective-permute-start.33 = (bf16[192,1024]{1,0:T(8,128)(2,1)S(1)}, bf16[192,1024]{1,0:T(8,128)(2,1)S(1)}, u32[]{:S(2)}, u32[]{:S(2)}) collective-permute-start(bf16[192,1024]{1,0:T(8,128)(2,1)S(1)} %get-tuple-element.445), channel_id=1, source_target_pairs={{0,2},{1,3},{2,0},{3,1},{4,6},{5,7},{6,4},{7,5},{8,10},{9,11},{10,... | collective-permute-start | bytes 1179656 | tf_op jit(solution)/shard_map/ppermute | solution.py:327
  150.1 27.0 %collective-permute-start.32 = (bf16[192,1024]{1,0:T(8,128)(2,1)S(1)}, bf16[192,1024]{1,0:T(8,128)(2,1)S(1)}, u32[]{:S(2)}, u32[]{:S(2)}) collective-permute-start(bf16[192,1024]{1,0:T(8,128)(2,1)S(1)} %get-tuple-element.441), channel_id=1, source_target_pairs={{0,2},{1,3},{2,0},{3,1},{4,6},{5,7},{6,4},{7,5},{8,10},{9,11},{10,... | collective-permute-start | bytes 1179656 | tf_op jit(solution)/shard_map/ppermute | solution.py:327
  160.6 16.0 %collective-permute-start.35 = (bf16[256,1024]{1,0:T(8,128)(2,1)S(1)}, bf16[256,1024]{1,0:T(8,128)(2,1)S(1)}, u32[]{:S(2)}, u32[]{:S(2)}) collective-permute-start(bf16[256,1024]{1,0:T(8,128)(2,1)S(1)} %combine_rows.25), channel_id=1, source_target_pairs={{0,1},{1,0},{2,3},{3,2},{4,5},{5,4},{6,7},{7,6},{8,9},{9,8},{10,11... | collective-permute-start | bytes 1572872 | tf_op jit(solution)/shard_map/ppermute | solution.py:327
  160.7 15.9 %collective-permute-start.36 = (bf16[256,1024]{1,0:T(8,128)(2,1)S(1)}, bf16[256,1024]{1,0:T(8,128)(2,1)S(1)}, u32[]{:S(2)}, u32[]{:S(2)}) collective-permute-start(bf16[256,1024]{1,0:T(8,128)(2,1)S(1)} %combine_rows.23), channel_id=1, source_target_pairs={{0,4},{1,5},{2,6},{3,7},{4,12},{5,13},{6,14},{7,15},{12,8},{13,9},... | collective-permute-start | bytes 1572872 | tf_op jit(solution)/shard_map/ppermute | solution.py:327
  162.2 13.9 %collective-permute-start.37 = (bf16[256,1024]{1,0:T(8,128)(2,1)S(1)}, bf16[256,1024]{1,0:T(8,128)(2,1)S(1)}, u32[]{:S(2)}, u32[]{:S(2)}) collective-permute-start(bf16[256,1024]{1,0:T(8,128)(2,1)S(1)} %combine_rows.24), channel_id=1, source_target_pairs={{0,1},{1,0},{2,3},{3,2},{4,5},{5,4},{6,7},{7,6},{8,9},{9,8},{10,11... | collective-permute-start | bytes 1572872 | tf_op jit(solution)/shard_map/ppermute | solution.py:327
  162.2 16.3 %collective-permute-start.41 = (bf16[192,1024]{1,0:T(8,128)(2,1)S(1)}, bf16[192,1024]{1,0:T(8,128)(2,1)S(1)}, u32[]{:S(2)}, u32[]{:S(2)}) collective-permute-start(bf16[192,1024]{1,0:T(8,128)(2,1)S(1)} %get-tuple-element.481), channel_id=1, source_target_pairs={{0,2},{1,3},{2,0},{3,1},{4,6},{5,7},{6,4},{7,5},{8,10},{9,11},{10,... | collective-permute-start | bytes 1179656 | tf_op jit(solution)/shard_map/ppermute | solution.py:327
  177.6 15.3 %collective-permute-start.39 = (bf16[256,1024]{1,0:T(8,128)(2,1)S(1)}, bf16[256,1024]{1,0:T(8,128)(2,1)S(1)}, u32[]{:S(2)}, u32[]{:S(2)}) collective-permute-start(bf16[256,1024]{1,0:T(8,128)(2,1)S(1)} %combine_rows.28), channel_id=1, source_target_pairs={{0,1},{1,0},{2,3},{3,2},{4,5},{5,4},{6,7},{7,6},{8,9},{9,8},{10,11... | collective-permute-start | bytes 1572872 | tf_op jit(solution)/shard_map/ppermute | solution.py:327
  177.9 15.7 %collective-permute-start.40 = (bf16[256,1024]{1,0:T(8,128)(2,1)S(1)}, bf16[256,1024]{1,0:T(8,128)(2,1)S(1)}, u32[]{:S(2)}, u32[]{:S(2)}) collective-permute-start(bf16[256,1024]{1,0:T(8,128)(2,1)S(1)} %combine_rows.26), channel_id=1, source_target_pairs={{0,4},{1,5},{2,6},{3,7},{4,12},{5,13},{6,14},{7,15},{12,8},{13,9},... | collective-permute-start | bytes 1572872 | tf_op jit(solution)/shard_map/ppermute | solution.py:327
  178.9 16.0 %collective-permute-start.42 = (bf16[256,1024]{1,0:T(8,128)(2,1)S(1)}, bf16[256,1024]{1,0:T(8,128)(2,1)S(1)}, u32[]{:S(2)}, u32[]{:S(2)}) collective-permute-start(bf16[256,1024]{1,0:T(8,128)(2,1)S(1)} %combine_rows.29), channel_id=1, source_target_pairs={{0,1},{1,0},{2,3},{3,2},{4,5},{5,4},{6,7},{7,6},{8,9},{9,8},{10,11... | collective-permute-start | bytes 1572872 | tf_op jit(solution)/shard_map/ppermute | solution.py:327
  179.0 25.2 %collective-permute-start.43 = (bf16[256,1024]{1,0:T(8,128)(2,1)S(1)}, bf16[256,1024]{1,0:T(8,128)(2,1)S(1)}, u32[]{:S(2)}, u32[]{:S(2)}) collective-permute-start(bf16[256,1024]{1,0:T(8,128)(2,1)S(1)} %combine_rows.27), channel_id=1, source_target_pairs={{0,4},{1,5},{2,6},{3,7},{4,12},{5,13},{6,14},{7,15},{12,8},{13,9},... | collective-permute-start | bytes 1572872 | tf_op jit(solution)/shard_map/ppermute | solution.py:327
  (48 other events, 364.5 us)

commit v4 on v3

--- a/solution.py
+++ b/solution.py
@@ -12,7 +12,7 @@
 PAIR = 2
 INV_ROOT_TWO = 0.7071067811865476
 INV_ROOT_TAU = 0.3989422804014327
-PEAK = 3.45e9
+PEAK = 5.2e9
 BF16 = jnp.bfloat16
 F32 = jnp.float32
 SMEM = pl.BlockSpec(memory_space=pltpu.SMEM)
@@ -402,11 +402,11 @@
             tensor.step(t + 1)
             tensor.swap(t)
             tensor.serve(t - 1)
-            if t > 1:
-                tensor.back(t - 1)
             if t > 2:
                 tensor.cross(t - 2)
             tensor.pick(t)
+            if t > 1:
+                tensor.back(t - 1)
             if t > 2:
                 tensor.fold(t - 2)
     top = length - 1

time: 206 us -> 200 us (0.971)
  waiting for transfers between devices: 77.8 us -> 68.4 us
  starting transfers between devices: 37.7 us -> 41.1 us
    ppermute x44, waiting for transfers between devices: 77.8 us -> 68.4 us  [permute(): return lax.ppermute(value, AXIS, pairs)]
    ppermute x44, starting transfers between devices: 37.7 us -> 41.1 us  [permute(): return lax.ppermute(value, AXIS, pairs)]
    unnamed x74 -> x70, local copies, waits for them, and re-layouts: 8.27 us -> 8.26 us
  transfers between devices with their start and end apart: 44 -> 44, of which waited for: 14 -> 17; matrix products, arithmetic and copies ran while one was open for 0% -> 0% of each run, Pallas kernels for 38% -> 40%
where the time goes in v4:
time: 200 us; the launch traced here: 199 us
  Pallas kernels  80.3 us (40%)
  waiting for transfers between devices  68.4 us (34%)
  starting transfers between devices  41.1 us (21%)
  local copies, waits for them, and re-layouts  8.26 us (4%)
    pallas_call x35, Pallas kernels, call(): pl.pallas_call(kernel, grid=grid, out_shape=out_shape, in_specs=specs, ou...  80.3 us
    ppermute x44, waiting for transfers between devices, permute(): return lax.ppermute(value, AXIS, pairs)  68.4 us
    ppermute x44, starting transfers between devices, permute(): return lax.ppermute(value, AXIS, pairs)  41.1 us
    unnamed x70, local copies, waits for them, and re-layouts  8.26 us
  transfers between devices with their start and end apart: 44, of which 17 were waited for; matrix products, arithmetic and copies ran while one was open for 0% of the time, Pallas kernels for 40%

profile of v4, /device:TPU:0, one launch (start us, length us, event | category | flops | bytes accessed | tf_op | source)
XLA Modules:
  0.0 199.4 jit_solution(13583727758320613762)
XLA Ops:
  4.8 2.6 %collective-permute-start.4 = (bf16[272,1024]{1,0:T(8,128)(2,1)S(1)}, bf16[272,1024]{1,0:T(8,128)(2,1)S(1)}, u32[]{:S(2)}, u32[]{:S(2)}) collective-permute-start(bf16[272,1024]{1,0:T(8,128)(2,1)S(1)} %stack_block.1.refs_0_), channel_id=1, source_target_pairs={{0,4},{1,5},{2,6},{3,7},{4,12},{5,13},{6,14},{7,15},{12,8},{13,9},... | collective-permute-start | bytes 1671176 | tf_op jit(solution)/shard_map/ppermute | solution.py:327
  8.2 1.6 collective-permute-start.1
  9.8 2.6 %collective-permute-start.3 = (bf16[256,1024]{1,0:T(8,128)(2,1)S(1)}, bf16[256,1024]{1,0:T(8,128)(2,1)S(1)}, u32[]{:S(2)}, u32[]{:S(2)}) collective-permute-start(bf16[256,1024]{1,0:T(8,128)(2,1)S(1)} %copy-done.3), channel_id=1, source_target_pairs={{0,4},{1,5},{2,6},{3,7},{4,12},{5,13},{6,14},{7,15},{12,8},{13,9},... | collective-permute-start | bytes 1572872 | tf_op jit(solution)/shard_map/ppermute | solution.py:327
  12.8 9.0 %collective-permute-done.4.refs_0_ = bf16[272,1024]{1,0:T(8,128)(2,1)S(1)} collective-permute-done((bf16[272,1024]{1,0:T(8,128)(2,1)S(1)}, bf16[272,1024]{1,0:T(8,128)(2,1)S(1)}, u32[]{:S(2)}, u32[]{:S(2)}) %collective-permute-start.4) | collective-permute-done | bytes 557088 | tf_op jit(solution)/shard_map/ppermute | solution.py:327
  24.5 5.9 %expert_forward.4 = (bf16[192,1024]{1,0:T(8,128)(2,1)S(1)}, bf16[192,1024]{1,0:T(8,128)(2,1)S(1)}, bf16[384,1024]{1,0:T(8,128)(2,1)S(1)}, bf16[384,2048]{1,0:T(8,128)(2,1)S(1)}, f32[384,2048]{1,0:T(8,128)S(1)}) custom-call(bf16[192,1024]{1,0:T(8,128)(2,1)S(1)} %get-tuple-element.280.mine_ref, bf16[192,1024]{1,0:T(8,128)(2,1)S(1)} %collective-permute-done.1.side_ref, ...), custom_call_target="tpu_custom_call" | custom-call | flops 25999998976 | bytes 1000 | tf_op jit(solution)/shard_map/expert_forward/pallas_call | solution.py:36
  33.1 2.7 %collective-permute-start.6 = (bf16[256,1024]{1,0:T(8,128)(2,1)S(1)}, bf16[256,1024]{1,0:T(8,128)(2,1)S(1)}, u32[]{:S(2)}, u32[]{:S(2)}) collective-permute-start(bf16[256,1024]{1,0:T(8,128)(2,1)S(1)} %collective-permute-done.3.refs_0_), channel_id=1, source_target_pairs={{0,4},{1,5},{2,6},{3,7},{4,12},{5,13},{6,14},{7,15},{12,8},{13,9},... | collective-permute-start | bytes 1572872 | tf_op jit(solution)/shard_map/ppermute | solution.py:327
  36.3 5.2 %expert_backward.4 = (bf16[192,1024]{1,0:T(8,128)(2,1)S(1)}, bf16[192,1024]{1,0:T(8,128)(2,1)S(1)}, bf16[384,1024]{1,0:T(8,128)(2,1)S(1)}, bf16[384,2048]{1,0:T(8,128)(2,1)S(1)}) custom-call(bf16[192,1024]{1,0:T(8,128)(2,1)S(1)} %get-tuple-element.297.mine_ref, bf16[192,1024]{1,0:T(8,128)(2,1)S(1)} %collective-permute-done.9.side_ref, ...), custom_call_target="tpu_custom_call" | custom-call | flops 25999998976 | bytes 1000 | tf_op jit(solution)/shard_map/expert_backward/pallas_call | solution.py:36
  42.9 2.1 %collective-permute-done.7.refs_0_ = bf16[272,1024]{1,0:T(8,128)(2,1)S(1)} collective-permute-done((bf16[272,1024]{1,0:T(8,128)(2,1)S(1)}, bf16[272,1024]{1,0:T(8,128)(2,1)S(1)}, u32[]{:S(2)}, u32[]{:S(2)}) %collective-permute-start.7) | collective-permute-done | bytes 557088 | tf_op jit(solution)/shard_map/ppermute | solution.py:327
  47.8 5.9 %expert_forward.5 = (bf16[192,1024]{1,0:T(8,128)(2,1)S(1)}, bf16[192,1024]{1,0:T(8,128)(2,1)S(1)}, bf16[384,1024]{1,0:T(8,128)(2,1)S(1)}, bf16[384,2048]{1,0:T(8,128)(2,1)S(1)}, f32[384,2048]{1,0:T(8,128)S(1)}) custom-call(bf16[192,1024]{1,0:T(8,128)(2,1)S(1)} %get-tuple-element.312.mine_ref, bf16[192,1024]{1,0:T(8,128)(2,1)S(1)} %collective-permute-done.11.side_ref, ...), custom_call_target="tpu_custom_call" | custom-call | flops 25999998976 | bytes 1000 | tf_op jit(solution)/shard_map/expert_forward/pallas_call | solution.py:36
  56.3 1.8 collective-permute-done.13.side_ref
  60.1 5.2 %expert_backward.5 = (bf16[192,1024]{1,0:T(8,128)(2,1)S(1)}, bf16[192,1024]{1,0:T(8,128)(2,1)S(1)}, bf16[384,1024]{1,0:T(8,128)(2,1)S(1)}, bf16[384,2048]{1,0:T(8,128)(2,1)S(1)}) custom-call(bf16[192,1024]{1,0:T(8,128)(2,1)S(1)} %get-tuple-element.327.mine_ref, bf16[192,1024]{1,0:T(8,128)(2,1)S(1)} %collective-permute-done.13.side_ref, ...), custom_call_target="tpu_custom_call" | custom-call | flops 25999998976 | bytes 1000 | tf_op jit(solution)/shard_map/expert_backward/pallas_call | solution.py:36
  66.7 3.4 %collective-permute-done.15.side_ref = bf16[192,1024]{1,0:T(8,128)(2,1)S(1)} collective-permute-done((bf16[192,1024]{1,0:T(8,128)(2,1)S(1)}, bf16[192,1024]{1,0:T(8,128)(2,1)S(1)}, u32[]{:S(2)}, u32[]{:S(2)}) %collective-permute-start.15) | collective-permute-done | bytes 393248 | tf_op jit(solution)/shard_map/ppermute | solution.py:327
  70.1 5.9 %expert_forward.6 = (bf16[192,1024]{1,0:T(8,128)(2,1)S(1)}, bf16[192,1024]{1,0:T(8,128)(2,1)S(1)}, bf16[384,1024]{1,0:T(8,128)(2,1)S(1)}, bf16[384,2048]{1,0:T(8,128)(2,1)S(1)}, f32[384,2048]{1,0:T(8,128)S(1)}) custom-call(bf16[192,1024]{1,0:T(8,128)(2,1)S(1)} %get-tuple-element.343.mine_ref, bf16[192,1024]{1,0:T(8,128)(2,1)S(1)} %collective-permute-done.15.side_ref, ...), custom_call_target="tpu_custom_call" | custom-call | flops 25999998976 | bytes 1000 | tf_op jit(solution)/shard_map/expert_forward/pallas_call | solution.py:36
  78.0 2.7 %collective-permute-start.20 = (bf16[256,1024]{1,0:T(8,128)(2,1)S(1)}, bf16[256,1024]{1,0:T(8,128)(2,1)S(1)}, u32[]{:S(2)}, u32[]{:S(2)}) collective-permute-start(bf16[256,1024]{1,0:T(8,128)(2,1)S(1)} %collective-permute-done.6.refs_0_), channel_id=1, source_target_pairs={{0,4},{1,5},{2,6},{3,7},{4,12},{5,13},{6,14},{7,15},{12,8},{13,9},... | collective-permute-start | bytes 1572872 | tf_op jit(solution)/shard_map/ppermute | solution.py:327
  84.0 8.7 %collective-permute-done.14.side_ref = bf16[192,1024]{1,0:T(8,128)(2,1)S(1)} collective-permute-done((bf16[192,1024]{1,0:T(8,128)(2,1)S(1)}, bf16[192,1024]{1,0:T(8,128)(2,1)S(1)}, u32[]{:S(2)}, u32[]{:S(2)}) %collective-permute-start.14) | collective-permute-done | bytes 393248 | tf_op jit(solution)/shard_map/ppermute | solution.py:327
  92.7 5.2 %expert_backward.6 = (bf16[192,1024]{1,0:T(8,128)(2,1)S(1)}, bf16[192,1024]{1,0:T(8,128)(2,1)S(1)}, bf16[384,1024]{1,0:T(8,128)(2,1)S(1)}, bf16[384,2048]{1,0:T(8,128)(2,1)S(1)}) custom-call(bf16[192,1024]{1,0:T(8,128)(2,1)S(1)} %get-tuple-element.368.mine_ref, bf16[192,1024]{1,0:T(8,128)(2,1)S(1)} %collective-permute-done.14.side_ref, ...), custom_call_target="tpu_custom_call" | custom-call | flops 25999998976 | bytes 1000 | tf_op jit(solution)/shard_map/expert_backward/pallas_call | solution.py:36
  97.9 1.9 collective-permute-done.22.refs_1_
  100.3 1.6 collective-permute-start.24
  104.2 1.6 collective-permute-start.23
  106.2 6.1 %collective-permute-done.24.refs_1_ = bf16[192,1024]{1,0:T(8,128)(2,1)S(1)} collective-permute-done((bf16[192,1024]{1,0:T(8,128)(2,1)S(1)}, bf16[192,1024]{1,0:T(8,128)(2,1)S(1)}, u32[]{:S(2)}, u32[]{:S(2)}) %collective-permute-start.24) | collective-permute-done | bytes 393248 | tf_op jit(solution)/shard_map/ppermute | solution.py:327
  112.8 7.9 %collective-permute-done.28.side_ref = bf16[192,1024]{1,0:T(8,128)(2,1)S(1)} collective-permute-done((bf16[192,1024]{1,0:T(8,128)(2,1)S(1)}, bf16[192,1024]{1,0:T(8,128)(2,1)S(1)}, u32[]{:S(2)}, u32[]{:S(2)}) %collective-permute-start.28) | collective-permute-done | bytes 393248 | tf_op jit(solution)/shard_map/ppermute | solution.py:327
  123.6 5.9 %expert_forward.7 = (bf16[192,1024]{1,0:T(8,128)(2,1)S(1)}, bf16[192,1024]{1,0:T(8,128)(2,1)S(1)}, bf16[384,1024]{1,0:T(8,128)(2,1)S(1)}, bf16[384,2048]{1,0:T(8,128)(2,1)S(1)}, f32[384,2048]{1,0:T(8,128)S(1)}) custom-call(bf16[192,1024]{1,0:T(8,128)(2,1)S(1)} %get-tuple-element.409.mine_ref, bf16[192,1024]{1,0:T(8,128)(2,1)S(1)} %collective-permute-done.28.side_ref, ...), custom_call_target="tpu_custom_call" | custom-call | flops 25999998976 | bytes 1000 | tf_op jit(solution)/shard_map/expert_forward/pallas_call | solution.py:36
  131.3 6.3 %collective-permute-done.31.side_ref = bf16[192,1024]{1,0:T(8,128)(2,1)S(1)} collective-permute-done((bf16[192,1024]{1,0:T(8,128)(2,1)S(1)}, bf16[192,1024]{1,0:T(8,128)(2,1)S(1)}, u32[]{:S(2)}, u32[]{:S(2)}) %collective-permute-start.31) | collective-permute-done | bytes 393248 | tf_op jit(solution)/shard_map/ppermute | solution.py:327
  137.6 5.2 %expert_backward.7 = (bf16[192,1024]{1,0:T(8,128)(2,1)S(1)}, bf16[192,1024]{1,0:T(8,128)(2,1)S(1)}, bf16[384,1024]{1,0:T(8,128)(2,1)S(1)}, bf16[384,2048]{1,0:T(8,128)(2,1)S(1)}) custom-call(bf16[192,1024]{1,0:T(8,128)(2,1)S(1)} %get-tuple-element.429.mine_ref, bf16[192,1024]{1,0:T(8,128)(2,1)S(1)} %collective-permute-done.31.side_ref, ...), custom_call_target="tpu_custom_call" | custom-call | flops 25999998976 | bytes 1000 | tf_op jit(solution)/shard_map/expert_backward/pallas_call | solution.py:36
  142.8 1.6 collective-permute-start.33
  147.2 7.7 %collective-permute-done.33.refs_1_ = bf16[192,1024]{1,0:T(8,128)(2,1)S(1)} collective-permute-done((bf16[192,1024]{1,0:T(8,128)(2,1)S(1)}, bf16[192,1024]{1,0:T(8,128)(2,1)S(1)}, u32[]{:S(2)}, u32[]{:S(2)}) %collective-permute-start.33) | collective-permute-done | bytes 393248 | tf_op jit(solution)/shard_map/ppermute | solution.py:327
  157.0 11.0 %weights_out.1 = bf16[1,2048,1024]{2,1,0:T(8,128)(2,1)} custom-call(bf16[384,2048]{1,0:T(8,128)(2,1)S(1)} %copy-done.13, bf16[384,2048]{1,0:T(8,128)(2,1)S(1)} %copy-done.15, bf16[384,2048]{1,0:T(8,128)(2,1)S(1)} %copy-done.17, bf16[384,2048]{1,0:T(8,128)(2,1)S(1)} %copy-done.19, bf16[384,1024]{1,0:T(8,128)(2,1)S(1)} %copy-done.21, ...), custom_call_target="tpu_custom_call" | custom-call | flops 51999997952 | bytes 1000 | tf_op jit(solution)/shard_map/weights_out/pallas_call | solution.py:36
  171.7 1.6 collective-permute-start.40
  173.3 6.2 %collective-permute-done.41.refs_1_ = bf16[192,1024]{1,0:T(8,128)(2,1)S(1)} collective-permute-done((bf16[192,1024]{1,0:T(8,128)(2,1)S(1)}, bf16[192,1024]{1,0:T(8,128)(2,1)S(1)}, u32[]{:S(2)}, u32[]{:S(2)}) %collective-permute-start.41) | collective-permute-done | bytes 393248 | tf_op jit(solution)/shard_map/ppermute | solution.py:327
  180.0 2.0 %collective-permute-start.43 = (bf16[256,1024]{1,0:T(8,128)(2,1)S(1)}, bf16[256,1024]{1,0:T(8,128)(2,1)S(1)}, u32[]{:S(2)}, u32[]{:S(2)}) collective-permute-start(bf16[256,1024]{1,0:T(8,128)(2,1)S(1)} %combine_rows.27), channel_id=1, source_target_pairs={{0,4},{1,5},{2,6},{3,7},{4,12},{5,13},{6,14},{7,15},{12,8},{13,9},... | collective-permute-start | bytes 1572872 | tf_op jit(solution)/shard_map/ppermute | solution.py:327
  182.1 11.0 %weights_in.1 = bf16[1,1024,2048]{2,1,0:T(8,128)(2,1)} custom-call(bf16[384,1024]{1,0:T(8,128)(2,1)S(1)} %copy-done.27, bf16[384,1024]{1,0:T(8,128)(2,1)S(1)} %copy-done.29, bf16[384,1024]{1,0:T(8,128)(2,1)S(1)} %copy-done.31, bf16[384,1024]{1,0:T(8,128)(2,1)S(1)} %copy-done.33, bf16[384,2048]{1,0:T(8,128)(2,1)S(1)} %copy-done.5, ...), custom_call_target="tpu_custom_call" | custom-call | flops 51999997952 | bytes 1000 | tf_op jit(solution)/shard_map/weights_in/pallas_call | solution.py:36
  194.4 3.8 %collective-permute-done.43.refs_5_ = bf16[256,1024]{1,0:T(8,128)(2,1)S(1)} collective-permute-done((bf16[256,1024]{1,0:T(8,128)(2,1)S(1)}, bf16[256,1024]{1,0:T(8,128)(2,1)S(1)}, u32[]{:S(2)}, u32[]{:S(2)}) %collective-permute-start.43) | collective-permute-done | bytes 524320 | tf_op jit(solution)/shard_map/ppermute | solution.py:327
  (161 shorter events, 46.5 us)
Async XLA Ops:
  4.8 17.1 %collective-permute-start.4 = (bf16[272,1024]{1,0:T(8,128)(2,1)S(1)}, bf16[272,1024]{1,0:T(8,128)(2,1)S(1)}, u32[]{:S(2)}, u32[]{:S(2)}) collective-permute-start(bf16[272,1024]{1,0:T(8,128)(2,1)S(1)} %stack_block.1.refs_0_), channel_id=1, source_target_pairs={{0,4},{1,5},{2,6},{3,7},{4,12},{5,13},{6,14},{7,15},{12,8},{13,9},... | collective-permute-start | bytes 1671176 | tf_op jit(solution)/shard_map/ppermute | solution.py:327
  8.2 16.3 %collective-permute-start.1 = (bf16[192,1024]{1,0:T(8,128)(2,1)S(1)}, bf16[192,1024]{1,0:T(8,128)(2,1)S(1)}, u32[]{:S(2)}, u32[]{:S(2)}) collective-permute-start(bf16[192,1024]{1,0:T(8,128)(2,1)S(1)} %get-tuple-element.270), channel_id=1, source_target_pairs={{0,2},{1,3},{2,0},{3,1},{4,6},{5,7},{6,4},{7,5},{8,10},{9,11},{10,... | collective-permute-start | bytes 1179656 | tf_op jit(solution)/shard_map/ppermute | solution.py:327
  9.8 23.3 %collective-permute-start.3 = (bf16[256,1024]{1,0:T(8,128)(2,1)S(1)}, bf16[256,1024]{1,0:T(8,128)(2,1)S(1)}, u32[]{:S(2)}, u32[]{:S(2)}) collective-permute-start(bf16[256,1024]{1,0:T(8,128)(2,1)S(1)} %copy-done.3), channel_id=1, source_target_pairs={{0,4},{1,5},{2,6},{3,7},{4,12},{5,13},{6,14},{7,15},{12,8},{13,9},... | collective-permute-start | bytes 1572872 | tf_op jit(solution)/shard_map/ppermute | solution.py:327
  21.9 23.2 %collective-permute-start.7 = (bf16[272,1024]{1,0:T(8,128)(2,1)S(1)}, bf16[272,1024]{1,0:T(8,128)(2,1)S(1)}, u32[]{:S(2)}, u32[]{:S(2)}) collective-permute-start(bf16[272,1024]{1,0:T(8,128)(2,1)S(1)} %collective-permute-done.4.refs_0_), channel_id=1, source_target_pairs={{0,4},{1,5},{2,6},{3,7},{4,12},{5,13},{6,14},{7,15},{12,8},{13,9},... | collective-permute-start | bytes 1671176 | tf_op jit(solution)/shard_map/ppermute | solution.py:327
  22.9 12.9 %collective-permute-start.9 = (bf16[192,1024]{1,0:T(8,128)(2,1)S(1)}, bf16[192,1024]{1,0:T(8,128)(2,1)S(1)}, u32[]{:S(2)}, u32[]{:S(2)}) collective-permute-start(bf16[192,1024]{1,0:T(8,128)(2,1)S(1)} %get-tuple-element.295), channel_id=1, source_target_pairs={{0,2},{1,3},{2,0},{3,1},{4,6},{5,7},{6,4},{7,5},{8,10},{9,11},{10,... | collective-permute-start | bytes 1179656 | tf_op jit(solution)/shard_map/ppermute | solution.py:327
  33.1 23.2 %collective-permute-start.6 = (bf16[256,1024]{1,0:T(8,128)(2,1)S(1)}, bf16[256,1024]{1,0:T(8,128)(2,1)S(1)}, u32[]{:S(2)}, u32[]{:S(2)}) collective-permute-start(bf16[256,1024]{1,0:T(8,128)(2,1)S(1)} %collective-permute-done.3.refs_0_), channel_id=1, source_target_pairs={{0,4},{1,5},{2,6},{3,7},{4,12},{5,13},{6,14},{7,15},{12,8},{13,9},... | collective-permute-start | bytes 1572872 | tf_op jit(solution)/shard_map/ppermute | solution.py:327
  45.1 25.1 %collective-permute-start.18 = (bf16[272,1024]{1,0:T(8,128)(2,1)S(1)}, bf16[272,1024]{1,0:T(8,128)(2,1)S(1)}, u32[]{:S(2)}, u32[]{:S(2)}) collective-permute-start(bf16[272,1024]{1,0:T(8,128)(2,1)S(1)} %collective-permute-done.7.refs_0_), channel_id=1, source_target_pairs={{0,4},{1,5},{2,6},{3,7},{4,12},{5,13},{6,14},{7,15},{12,8},{13,9},... | collective-permute-start | bytes 1671176 | tf_op jit(solution)/shard_map/ppermute | solution.py:327
  58.1 12.1 %collective-permute-start.15 = (bf16[192,1024]{1,0:T(8,128)(2,1)S(1)}, bf16[192,1024]{1,0:T(8,128)(2,1)S(1)}, u32[]{:S(2)}, u32[]{:S(2)}) collective-permute-start(bf16[192,1024]{1,0:T(8,128)(2,1)S(1)} %get-tuple-element.342), channel_id=1, source_target_pairs={{0,2},{1,3},{2,0},{3,1},{4,6},{5,7},{6,4},{7,5},{8,10},{9,11},{10,... | collective-permute-start | bytes 1179656 | tf_op jit(solution)/shard_map/ppermute | solution.py:327
  58.9 17.5 %collective-permute-start.16 = (bf16[192,1024]{1,0:T(8,128)(2,1)S(1)}, bf16[192,1024]{1,0:T(8,128)(2,1)S(1)}, u32[]{:S(2)}, u32[]{:S(2)}) collective-permute-start(bf16[192,1024]{1,0:T(8,128)(2,1)S(1)} %get-tuple-element.349), channel_id=1, source_target_pairs={{0,2},{1,3},{2,0},{3,1},{4,6},{5,7},{6,4},{7,5},{8,10},{9,11},{10,... | collective-permute-start | bytes 1179656 | tf_op jit(solution)/shard_map/ppermute | solution.py:327
  70.1 12.6 %collective-permute-start.19 = (bf16[272,1024]{1,0:T(8,128)(2,1)S(1)}, bf16[272,1024]{1,0:T(8,128)(2,1)S(1)}, u32[]{:S(2)}, u32[]{:S(2)}) collective-permute-start(bf16[272,1024]{1,0:T(8,128)(2,1)S(1)} %collective-permute-done.18.refs_0_), channel_id=1, source_target_pairs={{0,1},{1,0},{2,3},{3,2},{4,5},{5,4},{6,7},{7,6},{8,9},{9,8},{10,11... | collective-permute-start | bytes 1671176 | tf_op jit(solution)/shard_map/ppermute | solution.py:327
  78.0 14.7 %collective-permute-start.20 = (bf16[256,1024]{1,0:T(8,128)(2,1)S(1)}, bf16[256,1024]{1,0:T(8,128)(2,1)S(1)}, u32[]{:S(2)}, u32[]{:S(2)}) collective-permute-start(bf16[256,1024]{1,0:T(8,128)(2,1)S(1)} %collective-permute-done.6.refs_0_), channel_id=1, source_target_pairs={{0,4},{1,5},{2,6},{3,7},{4,12},{5,13},{6,14},{7,15},{12,8},{13,9},... | collective-permute-start | bytes 1572872 | tf_op jit(solution)/shard_map/ppermute | solution.py:327
  80.6 12.0 %collective-permute-start.14 = (bf16[192,1024]{1,0:T(8,128)(2,1)S(1)}, bf16[192,1024]{1,0:T(8,128)(2,1)S(1)}, u32[]{:S(2)}, u32[]{:S(2)}) collective-permute-start(bf16[192,1024]{1,0:T(8,128)(2,1)S(1)} %get-tuple-element.340), channel_id=1, source_target_pairs={{0,2},{1,3},{2,0},{3,1},{4,6},{5,7},{6,4},{7,5},{8,10},{9,11},{10,... | collective-permute-start | bytes 1179656 | tf_op jit(solution)/shard_map/ppermute | solution.py:327
  82.2 17.6 %collective-permute-start.22 = (bf16[192,1024]{1,0:T(8,128)(2,1)S(1)}, bf16[192,1024]{1,0:T(8,128)(2,1)S(1)}, u32[]{:S(2)}, u32[]{:S(2)}) collective-permute-start(bf16[192,1024]{1,0:T(8,128)(2,1)S(1)} %get-tuple-element.379), channel_id=1, source_target_pairs={{0,2},{1,3},{2,0},{3,1},{4,6},{5,7},{6,4},{7,5},{8,10},{9,11},{10,... | collective-permute-start | bytes 1179656 | tf_op jit(solution)/shard_map/ppermute | solution.py:327
  100.3 12.0 %collective-permute-start.24 = (bf16[192,1024]{1,0:T(8,128)(2,1)S(1)}, bf16[192,1024]{1,0:T(8,128)(2,1)S(1)}, u32[]{:S(2)}, u32[]{:S(2)}) collective-permute-start(bf16[192,1024]{1,0:T(8,128)(2,1)S(1)} %get-tuple-element.394), channel_id=1, source_target_pairs={{0,2},{1,3},{2,0},{3,1},{4,6},{5,7},{6,4},{7,5},{8,10},{9,11},{10,... | collective-permute-start | bytes 1179656 | tf_op jit(solution)/shard_map/ppermute | solution.py:327
  101.9 27.5 %collective-permute-start.27 = (bf16[256,1024]{1,0:T(8,128)(2,1)S(1)}, bf16[256,1024]{1,0:T(8,128)(2,1)S(1)}, u32[]{:S(2)}, u32[]{:S(2)}) collective-permute-start(bf16[256,1024]{1,0:T(8,128)(2,1)S(1)} %combine_rows.17), channel_id=1, source_target_pairs={{0,4},{1,5},{2,6},{3,7},{4,12},{5,13},{6,14},{7,15},{12,8},{13,9},... | collective-permute-start | bytes 1572872 | tf_op jit(solution)/shard_map/ppermute | solution.py:327
  103.2 17.6 %collective-permute-start.28 = (bf16[192,1024]{1,0:T(8,128)(2,1)S(1)}, bf16[192,1024]{1,0:T(8,128)(2,1)S(1)}, u32[]{:S(2)}, u32[]{:S(2)}) collective-permute-start(bf16[192,1024]{1,0:T(8,128)(2,1)S(1)} %get-tuple-element.408), channel_id=1, source_target_pairs={{0,2},{1,3},{2,0},{3,1},{4,6},{5,7},{6,4},{7,5},{8,10},{9,11},{10,... | collective-permute-start | bytes 1179656 | tf_op jit(solution)/shard_map/ppermute | solution.py:327
  104.2 26.7 %collective-permute-start.23 = (bf16[192,1024]{1,0:T(8,128)(2,1)S(1)}, bf16[192,1024]{1,0:T(8,128)(2,1)S(1)}, u32[]{:S(2)}, u32[]{:S(2)}) collective-permute-start(bf16[192,1024]{1,0:T(8,128)(2,1)S(1)} %get-tuple-element.390), channel_id=1, source_target_pairs={{0,2},{1,3},{2,0},{3,1},{4,6},{5,7},{6,4},{7,5},{8,10},{9,11},{10,... | collective-permute-start | bytes 1179656 | tf_op jit(solution)/shard_map/ppermute | solution.py:327
  112.7 17.3 %collective-permute-start.26 = (bf16[256,1024]{1,0:T(8,128)(2,1)S(1)}, bf16[256,1024]{1,0:T(8,128)(2,1)S(1)}, u32[]{:S(2)}, u32[]{:S(2)}) collective-permute-start(bf16[256,1024]{1,0:T(8,128)(2,1)S(1)} %combine_rows.20), channel_id=1, source_target_pairs={{0,1},{1,0},{2,3},{3,2},{4,5},{5,4},{6,7},{7,6},{8,9},{9,8},{10,11... | collective-permute-start | bytes 1572872 | tf_op jit(solution)/shard_map/ppermute | solution.py:327
  120.7 24.9 %collective-permute-start.30 = (bf16[256,1024]{1,0:T(8,128)(2,1)S(1)}, bf16[256,1024]{1,0:T(8,128)(2,1)S(1)}, u32[]{:S(2)}, u32[]{:S(2)}) collective-permute-start(bf16[256,1024]{1,0:T(8,128)(2,1)S(1)} %combine_rows.19), channel_id=1, source_target_pairs={{0,4},{1,5},{2,6},{3,7},{4,12},{5,13},{6,14},{7,15},{12,8},{13,9},... | collective-permute-start | bytes 1572872 | tf_op jit(solution)/shard_map/ppermute | solution.py:327
  122.0 15.6 %collective-permute-start.31 = (bf16[192,1024]{1,0:T(8,128)(2,1)S(1)}, bf16[192,1024]{1,0:T(8,128)(2,1)S(1)}, u32[]{:S(2)}, u32[]{:S(2)}) collective-permute-start(bf16[192,1024]{1,0:T(8,128)(2,1)S(1)} %get-tuple-element.427), channel_id=1, source_target_pairs={{0,2},{1,3},{2,0},{3,1},{4,6},{5,7},{6,4},{7,5},{8,10},{9,11},{10,... | collective-permute-start | bytes 1179656 | tf_op jit(solution)/shard_map/ppermute | solution.py:327
  129.5 17.3 %collective-permute-start.34 = (bf16[192,1024]{1,0:T(8,128)(2,1)S(1)}, bf16[192,1024]{1,0:T(8,128)(2,1)S(1)}, u32[]{:S(2)}, u32[]{:S(2)}) collective-permute-start(bf16[192,1024]{1,0:T(8,128)(2,1)S(1)} %get-tuple-element.449), channel_id=1, source_target_pairs={{0,2},{1,3},{2,0},{3,1},{4,6},{5,7},{6,4},{7,5},{8,10},{9,11},{10,... | collective-permute-start | bytes 1179656 | tf_op jit(solution)/shard_map/ppermute | solution.py:327
  131.2 14.4 %collective-permute-start.29 = (bf16[256,1024]{1,0:T(8,128)(2,1)S(1)}, bf16[256,1024]{1,0:T(8,128)(2,1)S(1)}, u32[]{:S(2)}, u32[]{:S(2)}) collective-permute-start(bf16[256,1024]{1,0:T(8,128)(2,1)S(1)} %combine_rows.22), channel_id=1, source_target_pairs={{0,1},{1,0},{2,3},{3,2},{4,5},{5,4},{6,7},{7,6},{8,9},{9,8},{10,11... | collective-permute-start | bytes 1572872 | tf_op jit(solution)/shard_map/ppermute | solution.py:327
  142.8 12.1 %collective-permute-start.33 = (bf16[192,1024]{1,0:T(8,128)(2,1)S(1)}, bf16[192,1024]{1,0:T(8,128)(2,1)S(1)}, u32[]{:S(2)}, u32[]{:S(2)}) collective-permute-start(bf16[192,1024]{1,0:T(8,128)(2,1)S(1)} %get-tuple-element.445), channel_id=1, source_target_pairs={{0,2},{1,3},{2,0},{3,1},{4,6},{5,7},{6,4},{7,5},{8,10},{9,11},{10,... | collective-permute-start | bytes 1179656 | tf_op jit(solution)/shard_map/ppermute | solution.py:327
  144.4 23.6 %collective-permute-start.38 = (bf16[256,1024]{1,0:T(8,128)(2,1)S(1)}, bf16[256,1024]{1,0:T(8,128)(2,1)S(1)}, u32[]{:S(2)}, u32[]{:S(2)}) collective-permute-start(bf16[256,1024]{1,0:T(8,128)(2,1)S(1)} %combine_rows.21), channel_id=1, source_target_pairs={{0,4},{1,5},{2,6},{3,7},{4,12},{5,13},{6,14},{7,15},{12,8},{13,9},... | collective-permute-start | bytes 1572872 | tf_op jit(solution)/shard_map/ppermute | solution.py:327
  146.1 25.0 %collective-permute-start.32 = (bf16[192,1024]{1,0:T(8,128)(2,1)S(1)}, bf16[192,1024]{1,0:T(8,128)(2,1)S(1)}, u32[]{:S(2)}, u32[]{:S(2)}) collective-permute-start(bf16[192,1024]{1,0:T(8,128)(2,1)S(1)} %get-tuple-element.441), channel_id=1, source_target_pairs={{0,2},{1,3},{2,0},{3,1},{4,6},{5,7},{6,4},{7,5},{8,10},{9,11},{10,... | collective-permute-start | bytes 1179656 | tf_op jit(solution)/shard_map/ppermute | solution.py:327
  155.3 14.7 %collective-permute-start.35 = (bf16[256,1024]{1,0:T(8,128)(2,1)S(1)}, bf16[256,1024]{1,0:T(8,128)(2,1)S(1)}, u32[]{:S(2)}, u32[]{:S(2)}) collective-permute-start(bf16[256,1024]{1,0:T(8,128)(2,1)S(1)} %combine_rows.25), channel_id=1, source_target_pairs={{0,1},{1,0},{2,3},{3,2},{4,5},{5,4},{6,7},{7,6},{8,9},{9,8},{10,11... | collective-permute-start | bytes 1572872 | tf_op jit(solution)/shard_map/ppermute | solution.py:327
  155.4 15.2 %collective-permute-start.36 = (bf16[256,1024]{1,0:T(8,128)(2,1)S(1)}, bf16[256,1024]{1,0:T(8,128)(2,1)S(1)}, u32[]{:S(2)}, u32[]{:S(2)}) collective-permute-start(bf16[256,1024]{1,0:T(8,128)(2,1)S(1)} %combine_rows.23), channel_id=1, source_target_pairs={{0,4},{1,5},{2,6},{3,7},{4,12},{5,13},{6,14},{7,15},{12,8},{13,9},... | collective-permute-start | bytes 1572872 | tf_op jit(solution)/shard_map/ppermute | solution.py:327
  157.0 12.5 %collective-permute-start.37 = (bf16[256,1024]{1,0:T(8,128)(2,1)S(1)}, bf16[256,1024]{1,0:T(8,128)(2,1)S(1)}, u32[]{:S(2)}, u32[]{:S(2)}) collective-permute-start(bf16[256,1024]{1,0:T(8,128)(2,1)S(1)} %combine_rows.24), channel_id=1, source_target_pairs={{0,1},{1,0},{2,3},{3,2},{4,5},{5,4},{6,7},{7,6},{8,9},{9,8},{10,11... | collective-permute-start | bytes 1572872 | tf_op jit(solution)/shard_map/ppermute | solution.py:327
  171.6 21.4 %collective-permute-start.39 = (bf16[256,1024]{1,0:T(8,128)(2,1)S(1)}, bf16[256,1024]{1,0:T(8,128)(2,1)S(1)}, u32[]{:S(2)}, u32[]{:S(2)}) collective-permute-start(bf16[256,1024]{1,0:T(8,128)(2,1)S(1)} %combine_rows.28), channel_id=1, source_target_pairs={{0,1},{1,0},{2,3},{3,2},{4,5},{5,4},{6,7},{7,6},{8,9},{9,8},{10,11... | collective-permute-start | bytes 1572872 | tf_op jit(solution)/shard_map/ppermute | solution.py:327
  171.7 21.4 %collective-permute-start.40 = (bf16[256,1024]{1,0:T(8,128)(2,1)S(1)}, bf16[256,1024]{1,0:T(8,128)(2,1)S(1)}, u32[]{:S(2)}, u32[]{:S(2)}) collective-permute-start(bf16[256,1024]{1,0:T(8,128)(2,1)S(1)} %combine_rows.26), channel_id=1, source_target_pairs={{0,4},{1,5},{2,6},{3,7},{4,12},{5,13},{6,14},{7,15},{12,8},{13,9},... | collective-permute-start | bytes 1572872 | tf_op jit(solution)/shard_map/ppermute | solution.py:327
  179.9 14.5 %collective-permute-start.42 = (bf16[256,1024]{1,0:T(8,128)(2,1)S(1)}, bf16[256,1024]{1,0:T(8,128)(2,1)S(1)}, u32[]{:S(2)}, u32[]{:S(2)}) collective-permute-start(bf16[256,1024]{1,0:T(8,128)(2,1)S(1)} %combine_rows.29), channel_id=1, source_target_pairs={{0,1},{1,0},{2,3},{3,2},{4,5},{5,4},{6,7},{7,6},{8,9},{9,8},{10,11... | collective-permute-start | bytes 1572872 | tf_op jit(solution)/shard_map/ppermute | solution.py:327
  180.0 18.1 %collective-permute-start.43 = (bf16[256,1024]{1,0:T(8,128)(2,1)S(1)}, bf16[256,1024]{1,0:T(8,128)(2,1)S(1)}, u32[]{:S(2)}, u32[]{:S(2)}) collective-permute-start(bf16[256,1024]{1,0:T(8,128)(2,1)S(1)} %combine_rows.27), channel_id=1, source_target_pairs={{0,4},{1,5},{2,6},{3,7},{4,12},{5,13},{6,14},{7,15},{12,8},{13,9},... | collective-permute-start | bytes 1572872 | tf_op jit(solution)/shard_map/ppermute | solution.py:327
  (46 other events, 310.4 us)
